TPU v7x, 32 devices: a whole 2x2x4 slice. The times are simulated.
32 devices in a mesh: band: 4 (over z), row: 2 (over x), col: 4 (over y, core).
Axes of the slice: x: 2, y: 2, z: 4, core: 2. Of those that a mesh axis runs over, the one named last changes fastest.
Arguments:
- spectral_cube: bfloat16 [88, 8, 4096], P('band', ('row', 'col')), may hold values from -6 to 6
- aperture: int32 [8, 4096], P(('row', 'col')), may hold values 0 or 1
- measurement: float32 [8, 4444], P(('row', 'col')), may hold values from -48 to 48
- shears: int32 [88], P('band'), may hold values from 0 to 348, as said below
- step_sizes: float32 [88], P('band'), may hold values from 0.5 to 2
- spatial_weight: bfloat16 [16, 9], replicated, may hold values from -2 to 2
- spatial_bias: float32 [16], replicated, may hold values from -3 to 3
- spectral_weight: bfloat16 [7, 16, 16], replicated, may hold values from -0.5 to 0.5
- spectral_bias: float32 [16], replicated, may hold values from -3 to 3
- out_weight: float32 [16], replicated, may hold values from -1.5 to 1.5
Outputs:
- denoised: bfloat16 [88, 8, 4096], P('band', ('row', 'col'))
Inputs may be any that keep to these rules, and one draw needn't show every extreme that they name: `shears`: strictly increasing over the bands, the first 0 and the last 348.
All inputs are finite; a program needn't handle non-finite values. No bound on the sum of `aperture` on one device may be relied on, other than what follows from the above.
Results may differ from a plain program's by a relative error of at most 0.0047.
Values may be sent and summed in bfloat16 or wider, within the bound.
No kernel may reach another device: no remote copies, remote signals or barrier semaphores. Data moves between devices by JAX's collectives and lax.ppermute only.
A program may use at most 64 MiB of HBM per device.

v0:
```python
import jax
import jax.numpy as jnp
from jax import lax
from jax.sharding import PartitionSpec as P


def with_halo(cells, sides, width):
    for axis, dim in sides:
        count = lax.axis_size(axis)
        ends = count - 1
        head = lax.slice_in_dim(cells, 0, width, axis=dim)
        tail = lax.slice_in_dim(cells, cells.shape[dim] - width, cells.shape[dim], axis=dim)
        cells = jnp.concatenate(
            [
                lax.ppermute(tail, axis, [(i, (i + 1) % count) for i in range(ends)]),
                cells,
                lax.ppermute(head, axis, [((i + 1) % count, i) for i in range(ends)]),
            ],
            axis=dim,
        )
    return cells


def denoise(
    padded,
    band_start,
    total_bands,
    block_width,
    spatial_weight,
    spatial_bias,
    spectral_weight,
    spectral_bias,
    out_weight,
):
    bands_in, rows_pad, cols_pad = padded.shape
    row_count = rows_pad - 2
    col_count = cols_pad - 2
    bands_out = bands_in - 6
    across = col_count // block_width
    band_ids = band_start + jnp.arange(bands_in, dtype=jnp.int32)
    band_valid = (band_ids >= 0) & (band_ids < total_bands)

    def one_block(block_index):
        row_index = block_index // across
        col_start = block_index % across * block_width
        window = lax.dynamic_slice(
            padded, (jnp.int32(0), row_index, col_start), (bands_in, 3, block_width + 2)
        )
        patches = jnp.stack([window[:, i, j : j + block_width] for i in range(3) for j in range(3)])
        spatial_out = (
            jnp.einsum("kq,qbc->kbc", spatial_weight, patches, preferred_element_type=jnp.float32)
            + spatial_bias[:, None, None]
        )
        active = jnp.where(band_valid[None, :, None], jax.nn.silu(spatial_out), 0.0).astype(
            jnp.bfloat16
        )
        second = (
            jnp.zeros((spatial_out.shape[0], bands_out, block_width), jnp.float32)
            + spectral_bias[:, None, None]
        )
        for d in range(spectral_weight.shape[0]):
            second = second + jnp.einsum(
                "kj,jbc->kbc",
                spectral_weight[d],
                active[:, d : d + bands_out],
                preferred_element_type=jnp.float32,
            )
        update_term = jnp.einsum(
            "k,kbc->bc", out_weight, jax.nn.silu(second), precision=lax.Precision.HIGHEST
        )
        center = window[3 : 3 + bands_out, 1, 1 : 1 + block_width].astype(jnp.float32)
        return (center + update_term).astype(jnp.bfloat16)

    blocks = lax.map(one_block, jnp.arange(row_count * across, dtype=jnp.int32))
    return (
        blocks.reshape(row_count, across, bands_out, block_width)
        .transpose(2, 0, 1, 3)
        .reshape(bands_out, row_count, col_count)
    )


def on_device(
    spectral_cube,
    aperture,
    measurement,
    shears,
    step_sizes,
    spatial_weight,
    spatial_bias,
    spectral_weight,
    spectral_bias,
    out_weight,
):
    local_bands, row_count, col_count = spectral_cube.shape
    detector_width = measurement.shape[1]
    aperture_f = aperture.astype(jnp.float32)
    masked = spectral_cube.astype(jnp.float32) * aperture_f[None]

    def place(carry, inputs):
        band_layer, offset = inputs
        empty_plane = jnp.zeros((row_count, detector_width), jnp.float32)
        placed_band = lax.dynamic_update_slice(empty_plane, band_layer, (jnp.int32(0), offset))
        opened = lax.dynamic_update_slice(empty_plane, aperture_f, (jnp.int32(0), offset))
        return ((carry[0] + placed_band, carry[1] + opened), None)

    start_sums = (
        jnp.zeros((row_count, detector_width), jnp.float32),
        jnp.zeros((row_count, detector_width), jnp.float32),
    )
    (predicted_part, count_part), _ = lax.scan(place, start_sums, (masked, shears))
    predicted, counts = lax.psum((predicted_part, count_part), "band")
    residual = (measurement - predicted) / jnp.maximum(counts, 1.0)

    def adjoint(inputs):
        offset, step_one = inputs
        pulled = lax.dynamic_slice(residual, (jnp.int32(0), offset), (row_count, col_count))
        return pulled * aperture_f * step_one

    updates = lax.map(adjoint, (shears, step_sizes))
    updated = (spectral_cube.astype(jnp.float32) + updates).astype(jnp.bfloat16)
    band_groups = lax.axis_size("band")
    total_bands = local_bands * band_groups
    banded = with_halo(updated, (("band", 0),), 3)
    rimmed = with_halo(banded, ((("row", "col"), 1),), 1)
    padded = jnp.pad(rimmed, ((0, 0), (0, 0), (1, 1)))
    band_first = lax.axis_index("band") * local_bands - 3
    return denoise(
        padded,
        band_first,
        total_bands,
        min(col_count, 512),
        spatial_weight,
        spatial_bias,
        spectral_weight,
        spectral_bias,
        out_weight,
    )


def solution(mesh):
    in_specs = (
        P("band", ("row", "col"), None),
        P(("row", "col"), None),
        P(("row", "col"), None),
        P("band"),
        P("band"),
        P(),
        P(),
        P(),
        P(),
        P(),
    )
    out_specs = P("band", ("row", "col"), None)
    return jax.shard_map(
        on_device, mesh=mesh, in_specs=in_specs, out_specs=out_specs, check_vma=False
    )
```

profile of v0, /device:TPU:13, one launch (start us, length us, event | category | flops | bytes accessed | tf_op | source)
XLA Modules:
  0.0 304.0 jit_solution(3440564261374438505)
XLA Ops:
  1.8 99.3 %while.35 = (s32[]{:T(128)}, f32[1,4444]{1,0:T(1,128)S(1)}, f32[1,4444]{1,0:T(1,128)S(1)}, s32[22]{0:T(128)}, f32[22,1,4096]{2,0,1:T(8,128)S(1)}, /*index=5*/f32...) while((s32[]{:T(128)}, f32[1,4444]{1,0:T(1,128)S(1)}, f32[1,4444]{1,0:T(1,128)S(1)}, s32[22]{0:T(128)}, ...), condition=%wide.region_1.2_spmd, body=%wide.region_0.1_spmd.sunk | while | flops 8197 | bytes 163995 | solution.py:110
  1.8 1.3 dynamic_slice.43
  6.3 1.3 dynamic_slice.43
  10.9 1.3 dynamic_slice.43
  15.4 1.3 dynamic_slice.43
  19.9 1.3 dynamic_slice.43
  24.4 1.3 dynamic_slice.43
  42.4 1.3 dynamic_slice.43
  74.0 1.3 dynamic_slice.43
  92.1 1.3 dynamic_slice.43
  101.1 12.8 %all-reduce.1 = (f32[1,4444]{1,0:T(1,128)S(1)}, f32[1,4444]{1,0:T(1,128)S(1)}) all-reduce(f32[1,4444]{1,0:T(1,128)S(1)} %get-tuple-element.197, f32[1,4444]{1,0:T(1,128)S(1)} %get-tuple-element.196), channel_id=1, replica_groups=mesh['band'=4,'row'=2,'col'=4] {'band'}, use_global_device_ids=true, to_apply=%region_3.4 | all-reduce | flops 8888 | bytes 71104 | tf_op jit(solution)/shard_map/psum | solution.py:111
  114.0 108.9 %while.36 = (s32[]{:T(128)}, f32[22,1,4096]{2,0,1:T(8,128)S(1)}, s32[22]{0:T(128)}, f32[1,4444]{1,0:T(1,128)S(1)}, f32[1,4096]{1,0:T(1,128)S(1)}, /*index=5*/f32[22]{0:T(128)S(1)}, s32[]{:T(128)}, s32[]{:T(128)}, s32[]{:T(128)}) while((s32[]{:T(128)}, f32[22,1,4096]{2,0,1:T(8,128)S(1)}, s32[22]{0:T(128)}, f32[1,4444]{1,0:T(1,128)S(1)}, ...), condition=%wide.region_5.6_spmd, body=%wide.region_4.5_spmd.sunk | while | flops 8197 | bytes 82083 | solution.py:119
  128.8 1.3 dynamic_slice.45
  143.7 1.3 dynamic_slice.45
  183.2 1.3 dynamic_slice.45
  198.1 1.3 dynamic_slice.45
  222.9 4.3 %collective-permute-start = (bf16[3,1,4096]{2,0,1:T(4,128)(2,1)S(1)}, bf16[3,1,4096]{2,0,1:T(4,128)(2,1)S(1)}, u32[]{:S(2)}, u32[]{:S(2)}) collective-permute-start(bf16[3,1,4096]{2,0,1:T(4,128)(2,1)S(1)} %get-tuple-element.340), channel_id=1, source_target_pairs={{0,8},{8,16},{16,24},{1,9},{9,17},{17,25},{2,10},{10,18},{18,26},{... | collective-permute-start | bytes 73736 | tf_op jit(solution)/shard_map/ppermute | solution.py:15
  227.2 2.2 collective-permute-start.1
  229.4 2.5 collective-permute-done.1
  232.1 9.0 %collective-permute-start.2 = (bf16[28,1,4096]{2,0,1:T(8,128)(2,1)S(1)}, bf16[28,1,4096]{2,0,1:T(8,128)(2,1)S(1)}, u32[]{:S(2)}, u32[]{:S(2)}) collective-permute-start(bf16[28,1,4096]{2,0,1:T(8,128)(2,1)S(1)} %pad_maximum_fusion), channel_id=1, source_target_pairs={{0,1},{1,2},{2,3},{3,4},{4,5},{5,6},{6,7},{8,9},{9,10},{10,11},{11... | collective-permute-start | bytes 688136 | tf_op jit(solution)/shard_map/ppermute | solution.py:15
  241.1 1.9 collective-permute-start.3
  243.0 1.4 collective-permute-done.2
  244.4 5.3 %collective-permute-done.3 = bf16[28,1,4096]{2,0,1:T(8,128)(2,1)S(1)} collective-permute-done((bf16[28,1,4096]{2,0,1:T(8,128)(2,1)S(1)}, bf16[28,1,4096]{2,0,1:T(8,128)(2,1)S(1)}, u32[]{:S(2)}, u32[]{:S(2)}) %collective-permute-start.3) | collective-permute-done | bytes 229408 | tf_op jit(solution)/shard_map/ppermute | solution.py:17
  250.1 53.0 %while.37 = (s32[]{:T(128)}, bf16[8,22,512]{2,1,0:T(8,128)(2,1)S(1)}, s32[8]{0:T(128)S(1)}, bf16[28,3,4098]{2,0,1:T(8,128)(2,1)S(1)}, f32[16]{0:T(128)S(1)}, /*i...) while((s32[]{:T(128)}, ...), condition=%wide.region_7.8_spmd.clone, body=%wide.region_6.7_spmd.clone.sunk | while | flops 50283652 | bytes 15050128 | solution.py:74
  (378 shorter events, 147.8 us)
Async XLA Ops:
  0.7 113.2 %copy-start.2 = (f32[1,4444]{1,0:T(1,128)S(1)}, f32[1,4444]{1,0:T(1,128)}, u32[]{:S(2)}) copy-start(f32[1,4444]{1,0:T(1,128)} %param.18) | copy-start | bytes 53332
  0.7 113.2 %copy-start.5 = (f32[22]{0:T(128)S(1)}, f32[22]{0:T(128)}, u32[]{:S(2)}) copy-start(f32[22]{0:T(128)} %param.20) | copy-start | bytes 268
  1.8 221.1 %copy-start = (bf16[22,1,4096]{2,0,1:T(8,128)(2,1)S(1)}, bf16[22,1,4096]{2,0,1:T(8,128)(2,1)}, u32[]{:S(2)}) copy-start(bf16[22,1,4096]{2,0,1:T(8,128)(2,1)} %param.16) | copy-start | bytes 540676
  222.9 6.5 %collective-permute-start = (bf16[3,1,4096]{2,0,1:T(4,128)(2,1)S(1)}, bf16[3,1,4096]{2,0,1:T(4,128)(2,1)S(1)}, u32[]{:S(2)}, u32[]{:S(2)}) collective-permute-start(bf16[3,1,4096]{2,0,1:T(4,128)(2,1)S(1)} %get-tuple-element.340), channel_id=1, source_target_pairs={{0,8},{8,16},{16,24},{1,9},{9,17},{17,25},{2,10},{10,18},{18,26},{... | collective-permute-start | bytes 73736 | tf_op jit(solution)/shard_map/ppermute | solution.py:15
  227.2 4.7 %collective-permute-start.1 = (bf16[3,1,4096]{2,0,1:T(4,128)(2,1)S(1)}, bf16[3,1,4096]{2,0,1:T(4,128)(2,1)S(1)}, u32[]{:S(2)}, u32[]{:S(2)}) collective-permute-start(bf16[3,1,4096]{2,0,1:T(4,128)(2,1)S(1)} %get-tuple-element.341), channel_id=1, source_target_pairs={{8,0},{16,8},{24,16},{9,1},{17,9},{25,17},{10,2},{18,10},{26,18},{... | collective-permute-start | bytes 73736 | tf_op jit(solution)/shard_map/ppermute | solution.py:17
  232.0 18.1 %copy-start.1 = (bf16[7,16,16]{2,1,0:T(8,128)(2,1)S(1)}, bf16[7,16,16]{2,1,0:T(8,128)(2,1)}, u32[]{:S(2)}) copy-start(bf16[7,16,16]{2,1,0:T(8,128)(2,1)} %param.23) | copy-start | bytes 10756
  232.0 18.1 %copy-start.3 = (f32[16]{0:T(128)S(1)}, f32[16]{0:T(128)}, u32[]{:S(2)}) copy-start(f32[16]{0:T(128)} %param.24) | copy-start | bytes 196
  232.0 18.1 %copy-start.4 = (bf16[16,9]{1,0:T(8,128)(2,1)S(1)}, bf16[16,9]{1,0:T(8,128)(2,1)}, u32[]{:S(2)}) copy-start(bf16[16,9]{1,0:T(8,128)(2,1)} %param.21) | copy-start | bytes 868
  232.0 18.1 %copy-start.6 = (f32[16]{0:T(128)S(1)}, f32[16]{0:T(128)}, u32[]{:S(2)}) copy-start(f32[16]{0:T(128)} %param.22) | copy-start | bytes 196
  232.1 18.1 %copy-start.7 = (f32[16]{0:T(128)S(1)}, f32[16]{0:T(128)}, u32[]{:S(2)}) copy-start(f32[16]{0:T(128)} %param.25) | copy-start | bytes 196
  232.1 12.3 %collective-permute-start.2 = (bf16[28,1,4096]{2,0,1:T(8,128)(2,1)S(1)}, bf16[28,1,4096]{2,0,1:T(8,128)(2,1)S(1)}, u32[]{:S(2)}, u32[]{:S(2)}) collective-permute-start(bf16[28,1,4096]{2,0,1:T(8,128)(2,1)S(1)} %pad_maximum_fusion), channel_id=1, source_target_pairs={{0,1},{1,2},{2,3},{3,4},{4,5},{5,6},{6,7},{8,9},{9,10},{10,11},{11... | collective-permute-start | bytes 688136 | tf_op jit(solution)/shard_map/ppermute | solution.py:15
  241.1 8.6 %collective-permute-start.3 = (bf16[28,1,4096]{2,0,1:T(8,128)(2,1)S(1)}, bf16[28,1,4096]{2,0,1:T(8,128)(2,1)S(1)}, u32[]{:S(2)}, u32[]{:S(2)}) collective-permute-start(bf16[28,1,4096]{2,0,1:T(8,128)(2,1)S(1)} %pad_maximum_fusion), channel_id=1, source_target_pairs={{1,0},{2,1},{3,2},{4,3},{5,4},{6,5},{7,6},{9,8},{10,9},{11,10},{12... | collective-permute-start | bytes 688136 | tf_op jit(solution)/shard_map/ppermute | solution.py:17
where the time goes:
time: 307 us; the launch traced here: 304 us
  local copies, waits for them, and re-layouts  121 us (39%)
  loops' own time  100 us (33%)
  other arithmetic  22.5 us (7%)
  matrix products  21.1 us (7%)
  starting transfers between devices  17.4 us (6%)
  blocking collectives  12.8 us (4%)
  waiting for transfers between devices  9.13 us (3%)
    dynamic_slice x44, local copies, waits for them, and re-layouts, on_device(): lax.scan(place, start_sums, (masked, shears))  55.6 us
    another operation x1, loops' own time, on_device(): lax.scan(place, start_sums, (masked, shears))  42.9 us
    another operation x1, loops' own time, on_device(): updates = lax.map(adjoint, (shears, step_sizes))  42.8 us
    add x44, local copies, waits for them, and re-layouts, place(): return ((carry[0] + placed_band, carry[1] + opened), None)  25.5 us
    dynamic_update_slice x22, other arithmetic, on_device(): updates = lax.map(adjoint, (shears, step_sizes))  16.2 us
    another operation x1, loops' own time, denoise(): blocks = lax.map(one_block, jnp.arange(row_count * across, dtype=jnp.int32))  14.6 us
    dynamic_slice x22, local copies, waits for them, and re-layouts, on_device(): updates = lax.map(adjoint, (shears, step_sizes))  13.4 us
    ppermute x2, starting transfers between devices, with_halo(): lax.ppermute(tail, axis, [(i, (i + 1) % count) for i in range(ends)])  13.3 us
  transfers between devices with their start and end apart: 4, of which 3 were waited for; matrix products, arithmetic and copies ran while one was open for 0% of the time, Pallas kernels for 0%

commit v1 on v0

v1 whole, which is shorter than its diff:
```python
import functools

import jax
import jax.numpy as jnp
from jax import lax
from jax.experimental import pallas as pl
from jax.experimental.pallas import tpu as pltpu
from jax.sharding import PartitionSpec as P

LANES = 128
SUB = 8
F32 = jnp.float32
BF16 = jnp.bfloat16
I32 = jnp.int32


def lanes_of(shape=(SUB, LANES)):
    return lax.broadcasted_iota(I32, shape, 1)


def rows_of(shape=(SUB, LANES)):
    return lax.broadcasted_iota(I32, shape, 0)


def column(row, rows):
    n = row.shape[1]
    eye = rows_of((rows, n)) == lanes_of((rows, n))
    return jnp.sum(jnp.where(eye, jnp.broadcast_to(row, (rows, n)), 0.0), axis=1, keepdims=True)


def turn(chunk, index):
    return jnp.take_along_axis(chunk, index, axis=1, mode="promise_in_bounds")


def choose(delay, options):
    result = options[-1]
    for d in range(len(options) - 2, -1, -1):
        result = jnp.where(delay == d, options[d], result)
    return result


def split3(x):
    hi = x.astype(BF16).astype(F32)
    mid = (x - hi).astype(BF16).astype(F32)
    return hi, mid, x - hi - mid


def project_kernel(reach, cube_ref, ap_ref, shear_ref, step_ref, up_ref, dn_ref, raw):
    bands, cols = cube_ref.shape
    groups = -(-bands // SUB)
    inner = cols // LANES
    outer = up_ref.shape[1] // LANES
    raw[bands // SUB * SUB :, :] = jnp.zeros((raw.shape[0] - bands // SUB * SUB, cols), F32)
    raw[0:bands, :] = cube_ref[...].astype(F32)
    shear_f = column(shear_ref[...].astype(F32), groups * SUB)
    step_f = column(step_ref[...], groups * SUB)
    shear_i = shear_f.astype(I32)
    lane, sub = lanes_of(), rows_of()
    index, delay = [], []
    for g in range(groups):
        s = jnp.broadcast_to(shear_i[g * SUB : (g + 1) * SUB], (SUB, LANES))
        rest = s & (LANES - 1)
        index.append((lane - rest) & (LANES - 1))
        delay.append((s >> 7) + jnp.where(lane < rest, 1, 0))
    zero = jnp.zeros((SUB, LANES), F32)
    turned = [[zero] * (reach - 1) for _ in range(groups)]
    opened = [[zero] * (reach - 1) for _ in range(groups)]
    low_first = (bands - 3) % SUB
    for p in range(outer):
        total = zero
        count = zero
        if p < inner:
            open_p = jnp.broadcast_to(
                ap_ref[:, p * LANES : (p + 1) * LANES].astype(F32), (SUB, LANES)
            )
            layers = [
                raw[g * SUB : (g + 1) * SUB, p * LANES : (p + 1) * LANES] for g in range(groups)
            ]
        for g in range(groups):
            if p < inner:
                here = turn(layers[g] * open_p, index[g])
                here_open = turn(open_p, index[g])
            else:
                here = here_open = zero
            options = [here] + turned[g]
            options_open = [here_open] + opened[g]
            turned[g] = options[:-1]
            opened[g] = options_open[:-1]
            total = total + choose(delay[g], options)
            part = choose(delay[g], options_open)
            if (g + 1) * SUB > bands:
                part = jnp.where(sub < bands - g * SUB, part, 0.0)
            count = count + part
        predicted = jnp.sum(total, axis=0, keepdims=True)
        hi = predicted.astype(BF16).astype(F32)
        lo = predicted - hi
        counts = jnp.sum(count, axis=0, keepdims=True)
        if p < inner:
            first, last = layers[0], layers[-1]
        elif p == inner:
            sides = []
            for g in (0, groups - 1):
                s = shear_i[g * SUB : (g + 1) * SUB]
                parts = [(s >> 1).astype(F32), (s & 1).astype(F32)]
                parts += list(split3(step_f[g * SUB : (g + 1) * SUB]))
                side = zero
                for i, part in enumerate(parts):
                    side = jnp.where(lane == i, part, side)
                sides.append(side)
            first, last = sides
        else:
            first = last = zero
        up = jnp.where((sub >= low_first) & (sub < low_first + 3), last, 0.0)
        dn = jnp.where(sub < 3, first, 0.0)
        for i, value in enumerate((hi, lo, counts)):
            up = jnp.where(sub == i, value, up)
            dn = jnp.where(sub == 3 + i, value, dn)
        up_ref[:, p * LANES : (p + 1) * LANES] = up.astype(BF16)
        dn_ref[:, p * LANES : (p + 1) * LANES] = dn.astype(BF16)


def update_kernel(
    reach,
    fars,
    cube_ref,
    ap_ref,
    meas_ref,
    shear_ref,
    step_ref,
    own_ref,
    below_ref,
    above_ref,
    *rest_refs,
):
    far_refs = rest_refs[:fars]
    out_ref, raw, meas = rest_refs[fars:]
    bands, cols = cube_ref.shape
    groups = -(-bands // SUB)
    inner = cols // LANES
    outer = own_ref.shape[1] // LANES
    raw[bands // SUB * SUB :, :] = jnp.zeros((raw.shape[0] - bands // SUB * SUB, cols), F32)
    raw[0:bands, :] = cube_ref[...].astype(F32)
    meas[:, (outer - 1) * LANES :] = jnp.zeros((1, LANES), F32)
    meas[:, 0 : meas_ref.shape[1]] = meas_ref[...]
    shear_f = column(shear_ref[...].astype(F32), groups * SUB)
    step_f = column(step_ref[...], groups * SUB)
    lane, sub = lanes_of(), rows_of()

    def halo(p):
        where = slice(p * LANES, (p + 1) * LANES)
        return jnp.where(sub < 3, above_ref[:, where].astype(F32), below_ref[:, where].astype(F32))

    side = halo(inner)
    shear_cols = [shear_f[g * SUB : (g + 1) * SUB] for g in range(groups)]
    step_cols = [step_f[g * SUB : (g + 1) * SUB] for g in range(groups)]
    inside = rows_of((SUB, 1)) < 6
    shear_cols.append(jnp.where(inside, 2.0 * side[:, 0:1] + side[:, 1:2], 0.0))
    step_cols.append(jnp.where(inside, side[:, 2:3] + side[:, 3:4] + side[:, 4:5], 0.0))
    index, delay, steps = [], [], []
    for g in range(groups + 1):
        s = jnp.broadcast_to(shear_cols[g].astype(I32), (SUB, LANES))
        rest = s & (LANES - 1)
        index.append((lane + rest) & (LANES - 1))
        delay.append((s >> 7) + jnp.where(lane + rest >= LANES, 1, 0))
        steps.append(jnp.broadcast_to(step_cols[g], (SUB, LANES)))
    turned = [[] for _ in range(groups + 1)]
    for p in range(outer + 1):
        if p < outer:
            where = slice(p * LANES, (p + 1) * LANES)
            up_sum = own_ref[:, where].astype(F32) + below_ref[:, where].astype(F32)
            for far in far_refs:
                up_sum = up_sum + far[:, where].astype(F32)
            dn_sum = above_ref[:, where].astype(F32)
            predicted = up_sum[0:1] + up_sum[1:2] + dn_sum[3:4] + dn_sum[4:5]
            counts = up_sum[2:3] + dn_sum[5:6]
            residual = (meas[:, where] - predicted) / jnp.maximum(counts, 1.0)
            residual = jnp.broadcast_to(residual, (SUB, LANES))
        else:
            residual = jnp.zeros((SUB, LANES), F32)
        for g in range(groups + 1):
            turned[g].append(turn(residual, index[g]) if p < outer else residual)
        q = p - (reach - 1)
        if q < 0 or q >= inner:
            continue
        here = slice(q * LANES, (q + 1) * LANES)
        open_q = jnp.broadcast_to(ap_ref[:, here].astype(F32), (SUB, LANES))
        pieces = []
        for g in range(groups + 1):
            pulled = choose(delay[g], turned[g][q : q + reach])
            base = raw[g * SUB : (g + 1) * SUB, here] if g < groups else halo(q)
            if g == groups:
                base = jnp.where(sub < 6, base, 0.0)
            pieces.append(base + pulled * open_q * steps[g])
        out_ref[:, here] = jnp.concatenate(pieces, axis=0).astype(BF16)


def weights_kernel(edge_ref, sw_ref, sb_ref, cw_ref, cb_ref, main_ref, halo_ref, band_ref):
    ch, taps2 = sw_ref.shape
    taps = cw_ref.shape[0]

    def spread(rows, which):
        return (which(rows_of((rows, ch))) == lanes_of((rows, ch))).astype(F32).astype(BF16)

    def bias_column(row_ref, rows, which):
        pick = which(rows_of((rows, ch))) == lanes_of((rows, ch))
        row = jnp.broadcast_to(row_ref[...], (rows, ch))
        return 0.5 * jnp.sum(jnp.where(pick, row, 0.0), axis=1, keepdims=True)

    def with_bias(matrix, bias, start):
        lane = lanes_of(matrix.shape)
        for i, part in enumerate(split3(bias)):
            matrix = jnp.where(lane == start + i, part, matrix)
        return matrix

    width = main_ref.shape[1]
    slots = 16
    fan = (lanes_of((taps2, width)) // slots == rows_of((taps2, width))).astype(F32).astype(BF16)
    flat = jnp.dot(sw_ref[...], fan, preferred_element_type=F32).astype(BF16)
    for ref, slot_of in (
        (main_ref, lambda b: b),
        (halo_ref, lambda b: jnp.where(b < 3, 11 + b, jnp.where(b < 9, b - 3, b - 1))),
    ):
        rows = ref.shape[0]
        which = lambda r: r % ch
        full = jnp.dot(spread(rows, which), flat, preferred_element_type=F32)
        lane = lanes_of((rows, width))
        band = rows_of((rows, width)) // ch
        keep = (lane % slots == slot_of(band)) & (lane < taps2 * slots)
        matrix = with_bias(
            jnp.where(keep, 0.5 * full, 0.0), bias_column(sb_ref, rows, which), taps2 * slots
        )
        if ref is halo_ref:
            valid = jnp.where(band < 3, edge_ref[0], jnp.where(band >= 9, edge_ref[1], 1))
            matrix = jnp.where(valid > 0, matrix, 0.0)
        ref[...] = matrix.astype(BF16)

    rows, width = band_ref.shape
    per = rows // ch
    used = (per + taps - 1) * ch
    which = lambda r: r // per
    fan = (lanes_of((ch, width)) % ch == rows_of((ch, width))).astype(F32).astype(BF16)
    picks = spread(rows, which)
    lane = lanes_of((rows, width))
    ahead = lane // ch - rows_of((rows, width)) % per
    matrix = jnp.zeros((rows, width), F32)
    for d in range(taps):
        flat = jnp.dot(cw_ref[d], fan, preferred_element_type=F32).astype(BF16)
        full = jnp.dot(picks, flat, preferred_element_type=F32)
        matrix = jnp.where(ahead == d, 0.5 * full, matrix)
    matrix = jnp.where(lane < used, matrix, 0.0)
    matrix = with_bias(matrix, bias_column(cb_ref, rows, which), used)
    band_ref[...] = matrix.astype(BF16)


def denoise_kernel(
    tile, ow_ref, up_ref, mid_ref, dn_ref, main_ref, halo_ref, band_ref, out_ref, act
):
    bands, cols = out_ref.shape
    slots = 16
    ch = ow_ref.shape[0]
    tiles = cols // tile
    wide = tile + 2 * LANES
    rows = act.shape[0]
    act[rows - 2 * slots :, :] = jnp.zeros((2 * slots, tile), BF16)
    ones = jnp.where(rows_of((slots, tile)) < 3, 1.0, 0.0).astype(BF16)

    def silu_twice(half):
        return half + half * jnp.tanh(half)

    def body(t, carry):
        start = pl.multiple_of(t * tile, LANES)
        before = pl.multiple_of(jnp.maximum(start - LANES, 0), LANES)
        after = pl.multiple_of(jnp.minimum(start + tile, cols - LANES), LANES)
        patches = []
        center = None
        for ref in (up_ref, mid_ref, dn_ref):
            left = ref[:, pl.ds(before, LANES)].astype(F32)
            here = ref[:, pl.ds(start, tile)]
            right = ref[:, pl.ds(after, LANES)].astype(F32)
            left = jnp.where(t > 0, left, 0.0)
            right = jnp.where(t < tiles - 1, right, 0.0)
            here_f = here.astype(F32)
            row = jnp.concatenate([left, here_f, right], axis=1)
            back = pltpu.roll(row, 1, 1)[:, LANES : LANES + tile].astype(BF16)
            ahead = pltpu.roll(row, wide - 1, 1)[:, LANES : LANES + tile].astype(BF16)
            patches += [back, here, ahead]
            if ref is mid_ref:
                center = here_f
        for part, w_ref in enumerate((main_ref, halo_ref)):
            x = jnp.concatenate(
                [p[part * slots : (part + 1) * slots] for p in patches] + [ones], axis=0
            )
            half = jnp.dot(w_ref[...], x, preferred_element_type=F32)
            value = silu_twice(half).astype(BF16)
            if part == 0:
                act[3 * ch : 19 * ch, :] = value
            else:
                act[0 : 3 * ch, :] = value[0 : 3 * ch]
                act[19 * ch : 28 * ch, :] = value[3 * ch :]
        weights = band_ref[...]
        per = weights.shape[0] // ch
        used = (per + 6) * ch
        pieces = []
        for i in range(-(-bands // per)):
            x = jnp.concatenate([act[i * per * ch : i * per * ch + used, :], ones], axis=0)
            half = jnp.dot(weights, x, preferred_element_type=F32)
            total = center[i * per : (i + 1) * per]
            for k in range(ch):
                total = total + ow_ref[k] * silu_twice(half[k * per : (k + 1) * per])
            pieces.append(total)
        result = jnp.concatenate(pieces, axis=0)[0:bands]
        out_ref[:, pl.ds(start, tile)] = result.astype(BF16)
        return carry

    lax.fori_loop(0, tiles, body, 0)


def vmem(n):
    return [pl.BlockSpec(memory_space=pltpu.VMEM)] * n


SMEM = pl.BlockSpec(memory_space=pltpu.SMEM)


def on_device(
    spectral_cube,
    aperture,
    measurement,
    shears,
    step_sizes,
    spatial_weight,
    spatial_bias,
    spectral_weight,
    spectral_bias,
    out_weight,
):
    bands, row_count, cols = spectral_cube.shape
    width = measurement.shape[1]
    reach = (width - cols) // LANES + 2
    outer = -(-width // LANES)
    groups = -(-bands // SUB)
    slots = (groups + 1) * SUB
    taps, ch = spectral_weight.shape[:2]
    taps2 = spatial_weight.shape[1]
    count = lax.axis_size("band")
    place = lax.axis_index("band")
    cube = spectral_cube.reshape(bands, cols)
    shear_row = shears.reshape(1, bands)
    step_row = step_sizes.reshape(1, bands)
    params = pltpu.CompilerParams(vmem_limit_bytes=48 * 2**20)

    payload = jax.ShapeDtypeStruct((SUB, outer * LANES), BF16)
    up, dn = pl.pallas_call(
        functools.partial(project_kernel, reach),
        out_shape=(payload, payload),
        in_specs=vmem(4),
        out_specs=tuple(vmem(2)),
        scratch_shapes=[pltpu.VMEM((groups * SUB, cols), F32)],
        compiler_params=params,
        name="project",
    )(cube, aperture, shear_row, step_row)

    def around(x, shift):
        return lax.ppermute(x, "band", [(i, (i + shift) % count) for i in range(count)])

    below = around(up, 1)
    above = around(dn, -1)
    far = [around(up, s) for s in range(2, count - 1)]

    edges = jnp.stack([place > 0, place < count - 1]).astype(I32)
    used = taps2 * 16
    main_w, halo_w, band_w = pl.pallas_call(
        weights_kernel,
        out_shape=(
            jax.ShapeDtypeStruct((16 * ch, used + 16), BF16),
            jax.ShapeDtypeStruct((12 * ch, used + 16), BF16),
            jax.ShapeDtypeStruct((SUB * ch, (SUB + taps - 1) * ch + 16), BF16),
        ),
        in_specs=[SMEM] + vmem(4),
        out_specs=tuple(vmem(3)),
        compiler_params=params,
        name="weights",
    )(
        edges,
        spatial_weight,
        spatial_bias.reshape(1, ch),
        spectral_weight,
        spectral_bias.reshape(1, ch),
    )

    updated = pl.pallas_call(
        functools.partial(update_kernel, reach, len(far)),
        out_shape=jax.ShapeDtypeStruct((slots, cols), BF16),
        in_specs=vmem(8 + len(far)),
        out_specs=vmem(1)[0],
        scratch_shapes=[
            pltpu.VMEM((groups * SUB, cols), F32),
            pltpu.VMEM((1, outer * LANES), F32),
        ],
        compiler_params=params,
        name="update",
    )(cube, aperture, measurement, shear_row, step_row, up, below, above, *far)

    lines = lax.axis_size(("row", "col"))
    over = lax.ppermute(updated, ("row", "col"), [(i, i + 1) for i in range(lines - 1)])
    under = lax.ppermute(updated, ("row", "col"), [(i + 1, i) for i in range(lines - 1)])

    tile = 512
    result = pl.pallas_call(
        functools.partial(denoise_kernel, tile),
        out_shape=jax.ShapeDtypeStruct((bands, cols), BF16),
        in_specs=[SMEM] + vmem(6),
        out_specs=vmem(1)[0],
        scratch_shapes=[pltpu.VMEM((30 * ch, tile), BF16)],
        compiler_params=params,
        name="denoise",
    )(out_weight, over, updated, under, main_w, halo_w, band_w)
    return result.reshape(bands, 1, cols)


def solution(mesh):
    in_specs = (
        P("band", ("row", "col"), None),
        P(("row", "col"), None),
        P(("row", "col"), None),
        P("band"),
        P("band"),
        P(),
        P(),
        P(),
        P(),
        P(),
    )
    out_specs = P("band", ("row", "col"), None)
    return jax.shard_map(
        on_device, mesh=mesh, in_specs=in_specs, out_specs=out_specs, check_vma=False
    )
```

time: 307 us -> 33.3 us (0.11)
  the two profiles are of different devices: /device:TPU:13 before, /device:TPU:1 now
where the time goes in v1:
time: 33.3 us; the launch traced here: 33 us
  starting transfers between devices  10.2 us (31%)
  waiting for transfers between devices  9.75 us (29%)
  Pallas kernels  9.23 us (28%)
  local copies, waits for them, and re-layouts  3.65 us (11%)
    ppermute x3, waiting for transfers between devices, around(): lax.ppermute(x, 'band', [(i, (i + shift) % count) for i in range(count)])  6.86 us
    pallas_call x1, Pallas kernels, on_device(): pl.pallas_call(functools.partial(denoise_kernel, tile), out_shape=jax.Sha...  6.61 us
    ppermute x3, starting transfers between devices, around(): lax.ppermute(x, 'band', [(i, (i + shift) % count) for i in range(count)])  4.66 us
    unnamed x20, local copies, waits for them, and re-layouts  3.65 us
    ppermute x1, starting transfers between devices, on_device(): lax.ppermute(updated, ('row', 'col'), [(i, i + 1) for i in range(lines -...  3.12 us
    ppermute x1, waiting for transfers between devices, on_device(): lax.ppermute(updated, ('row', 'col'), [(i, i + 1) for i in range(lines -...  2.89 us
    ppermute x1, starting transfers between devices, on_device(): lax.ppermute(updated, ('row', 'col'), [(i + 1, i) for i in range(lines -...  2.44 us
    pallas_call x1, Pallas kernels, on_device(): pl.pallas_call(weights_kernel, out_shape=(jax.ShapeDtypeStruct((16 * ch,...  1.48 us
  transfers between devices with their start and end apart: 5, of which 3 were waited for; matrix products, arithmetic and copies ran while one was open for 0% of the time, Pallas kernels for 4%

profile of v1, /device:TPU:1, one launch (start us, length us, event | category | flops | bytes accessed | tf_op | source)
XLA Modules:
  0.0 33.0 jit_solution(5872498162749403967)
XLA Ops:
  0.0 0.7 %copy-done.5 = s32[22]{0:T(128)S(1)} copy-done((s32[22]{0:T(128)S(1)}, s32[22]{0:T(128)}, u32[]{:S(2)}) %copy-start.5) | copy-done | bytes 112
  0.7 0.0 copy-done.6
  0.7 0.9 %copy-done = bf16[22,1,4096]{2,0,1:T(8,128)(2,1)S(1)} copy-done((bf16[22,1,4096]{2,0,1:T(8,128)(2,1)S(1)}, bf16[22,1,4096]{2,0,1:T(8,128)(2,1)}, u32[]{:S(2)}) %copy-start) | copy-done | bytes 180248
  1.6 0.7 %copy-done.1 = s32[1,4096]{1,0:T(1,128)S(1)} copy-done((s32[1,4096]{1,0:T(1,128)S(1)}, s32[1,4096]{1,0:T(1,128)}, u32[]{:S(2)}) %copy-start.1) | copy-done | bytes 16408
  2.3 0.6 %project.1 = (bf16[8,4480]{1,0:T(8,128)(2,1)S(1)}, bf16[8,4480]{1,0:T(8,128)(2,1)S(1)}) custom-call(bf16[22,4096]{1,0:T(8,128)(2,1)S(1)} %bitcast.8, s32[1,4096]{1,0:T(1,128)S(1)} %copy-done.1, s32[1,22]{1,0:T(1,128)S(1)} %bitcast.10, f32[1,22]{1,0:T(1,128)S(1)} %bitcast.12), custom_call_target="tpu_custom_call" | custom-call | tf_op jit(solution)/shard_map/project/pallas_call | solution.py:353
  2.9 4.2 %collective-permute-start.1 = (bf16[8,4480]{1,0:T(8,128)(2,1)S(1)}, bf16[8,4480]{1,0:T(8,128)(2,1)S(1)}, u32[]{:S(2)}, u32[]{:S(2)}) collective-permute-start(bf16[8,4480]{1,0:T(8,128)(2,1)S(1)} %get-tuple-element.11), channel_id=1, source_target_pairs={{0,24},{8,0},{16,8},{24,16},{1,25},{9,1},{17,9},{25,17},{2,26},{10... | collective-permute-start | bytes 215048 | tf_op jit(solution)/shard_map/ppermute | solution.py:364
  7.1 0.0 collective-permute-start.2
  7.1 0.5 %collective-permute-start = (bf16[8,4480]{1,0:T(8,128)(2,1)S(1)}, bf16[8,4480]{1,0:T(8,128)(2,1)S(1)}, u32[]{:S(2)}, u32[]{:S(2)}) collective-permute-start(bf16[8,4480]{1,0:T(8,128)(2,1)S(1)} %get-tuple-element.10.own_ref), channel_id=1, source_target_pairs={{0,8},{8,16},{16,24},{24,0},{1,9},{9,17},{17,25},{25,1},{2,10},{10... | collective-permute-start | bytes 215048 | tf_op jit(solution)/shard_map/ppermute | solution.py:364
  7.6 0.9 %collective-permute-done.1.above_ref = bf16[8,4480]{1,0:T(8,128)(2,1)S(1)} collective-permute-done((bf16[8,4480]{1,0:T(8,128)(2,1)S(1)}, bf16[8,4480]{1,0:T(8,128)(2,1)S(1)}, u32[]{:S(2)}, u32[]{:S(2)}) %collective-permute-start.1) | collective-permute-done | bytes 71712 | tf_op jit(solution)/shard_map/ppermute | solution.py:364
  8.5 5.9 %collective-permute-done.2.rest_refs_0_ = bf16[8,4480]{1,0:T(8,128)(2,1)S(1)} collective-permute-done((bf16[8,4480]{1,0:T(8,128)(2,1)S(1)}, bf16[8,4480]{1,0:T(8,128)(2,1)S(1)}, u32[]{:S(2)}, u32[]{:S(2)}) %collective-permute-start.2) | collective-permute-done | bytes 71712 | tf_op jit(solution)/shard_map/ppermute | solution.py:364
  14.5 0.0 collective-permute-done.below_ref
  14.5 0.5 %update.1.mid_ref = bf16[32,4096]{1,0:T(8,128)(2,1)S(1)} custom-call(bf16[22,4096]{1,0:T(8,128)(2,1)S(1)} %bitcast.9, s32[1,4096]{1,0:T(1,128)S(1)} %copy-done.1, f32[1,4444]{1,0:T(1,128)S(1)} %copy-done.3, s32[1,22]{1,0:T(1,128)S(1)} %bitcast.11, f32[1,22]{1,0:T(1,128)S(1)} %bitcast.13, bf16[8,4480]{1,0:T(8,128)(2,1)S(1)} %get-tuple-element.10.own_ref, ...), custom_call_target="tpu_custom_call" | custom-call | tf_op jit(solution)/shard_map/update/pallas_call | solution.py:391
  15.0 2.4 %collective-permute-start.4 = (bf16[32,4096]{1,0:T(8,128)(2,1)S(1)}, bf16[32,4096]{1,0:T(8,128)(2,1)S(1)}, u32[]{:S(2)}, u32[]{:S(2)}) collective-permute-start(bf16[32,4096]{1,0:T(8,128)(2,1)S(1)} %update.1.mid_ref), channel_id=1, source_target_pairs={{1,0},{2,1},{3,2},{4,3},{5,4},{6,5},{7,6},{9,8},{10,9},{11,10},{12... | collective-permute-start | bytes 786440 | tf_op jit(solution)/shard_map/ppermute | solution.py:406
  17.4 3.1 %collective-permute-start.3 = (bf16[32,4096]{1,0:T(8,128)(2,1)S(1)}, bf16[32,4096]{1,0:T(8,128)(2,1)S(1)}, u32[]{:S(2)}, u32[]{:S(2)}) collective-permute-start(bf16[32,4096]{1,0:T(8,128)(2,1)S(1)} %update.1.mid_ref), channel_id=1, source_target_pairs={{0,1},{1,2},{2,3},{3,4},{4,5},{5,6},{6,7},{8,9},{9,10},{10,11},{11... | collective-permute-start | bytes 786440 | tf_op jit(solution)/shard_map/ppermute | solution.py:405
  20.6 0.0 copy-start.4
  20.6 0.1 add_convert_fusion.edge_ref
  20.7 0.6 %copy-done.4 = bf16[16,9]{1,0:T(8,128)(2,1)S(1)} copy-done((bf16[16,9]{1,0:T(8,128)(2,1)S(1)}, bf16[16,9]{1,0:T(8,128)(2,1)}, u32[]{:S(2)}) %copy-start.4) | copy-done | bytes 312
  21.3 0.1 copy-done.7
  21.3 0.0 copy-done.8
  21.3 1.5 %weights.1 = (bf16[256,160]{1,0:T(8,128)(2,1)S(1)}, bf16[192,160]{1,0:T(8,128)(2,1)S(1)}, bf16[128,240]{1,0:T(8,128)(2,1)S(1)}) custom-call(s32[2]{0:T(128)S(1)} %add_convert_fusion.edge_ref, bf16[16,9]{1,0:T(8,128)(2,1)S(1)} %copy-done.4, f32[1,16]{1,0:T(1,128)S(1)} %bitcast.14, bf16[7,16,16]{2,1,0:T(8,128)(2,1)S(1)} %copy-done.2, f32[1,16]{1,0:T(1,128)S(1)} %bitcast.15), custom_call_target="tpu_custom_call" | custom-call | tf_op jit(solution)/shard_map/weights/pallas_call | solution.py:372
  22.8 0.0 collective-permute-done.4.dn_ref
  22.8 2.9 %collective-permute-done.3.up_ref = bf16[32,4096]{1,0:T(8,128)(2,1)S(1)} collective-permute-done((bf16[32,4096]{1,0:T(8,128)(2,1)S(1)}, bf16[32,4096]{1,0:T(8,128)(2,1)S(1)}, u32[]{:S(2)}, u32[]{:S(2)}) %collective-permute-start.3) | collective-permute-done | bytes 262176 | tf_op jit(solution)/shard_map/ppermute | solution.py:405
  25.7 0.7 %copy-done.9 = f32[16]{0:T(128)S(1)} copy-done((f32[16]{0:T(128)S(1)}, f32[16]{0:T(128)}, u32[]{:S(2)}) %copy-start.9) | copy-done | bytes 88
  26.4 6.6 %denoise.1 = bf16[22,4096]{1,0:T(8,128)(2,1)} custom-call(f32[16]{0:T(128)S(1)} %copy-done.9, bf16[32,4096]{1,0:T(8,128)(2,1)S(1)} %collective-permute-done.3.up_ref, bf16[32,4096]{1,0:T(8,128)(2,1)S(1)} %update.1.mid_ref, bf16[32,4096]{1,0:T(8,128)(2,1)S(1)} %collective-permute-done.4.dn_ref, bf16[256,160]{1,0:T(8,128)(2,1)S(1)} %get-tuple-element.12.main_ref, ...), custom_call_target="tpu_custom_call" | custom-call | tf_op jit(solution)/shard_map/denoise/pallas_call | solution.py:409
  (11 shorter events, 0.0 us)
Async XLA Ops:
  0.0 0.7 %copy-start.5 = (s32[22]{0:T(128)S(1)}, s32[22]{0:T(128)}, u32[]{:S(2)}) copy-start(s32[22]{0:T(128)} %param.13) | copy-start | bytes 268
  0.0 0.7 %copy-start.6 = (f32[22]{0:T(128)S(1)}, f32[22]{0:T(128)}, u32[]{:S(2)}) copy-start(f32[22]{0:T(128)} %param.14) | copy-start | bytes 268
  0.7 0.9 %copy-start = (bf16[22,1,4096]{2,0,1:T(8,128)(2,1)S(1)}, bf16[22,1,4096]{2,0,1:T(8,128)(2,1)}, u32[]{:S(2)}) copy-start(bf16[22,1,4096]{2,0,1:T(8,128)(2,1)} %param.10) | copy-start | bytes 540676
  1.6 0.7 %copy-start.1 = (s32[1,4096]{1,0:T(1,128)S(1)}, s32[1,4096]{1,0:T(1,128)}, u32[]{:S(2)}) copy-start(s32[1,4096]{1,0:T(1,128)} %ap_ref.3) | copy-start | bytes 49156
  2.3 12.1 %copy-start.3 = (f32[1,4444]{1,0:T(1,128)S(1)}, f32[1,4444]{1,0:T(1,128)}, u32[]{:S(2)}) copy-start(f32[1,4444]{1,0:T(1,128)} %meas_ref.1) | copy-start | bytes 53332
  2.9 5.6 %collective-permute-start.1 = (bf16[8,4480]{1,0:T(8,128)(2,1)S(1)}, bf16[8,4480]{1,0:T(8,128)(2,1)S(1)}, u32[]{:S(2)}, u32[]{:S(2)}) collective-permute-start(bf16[8,4480]{1,0:T(8,128)(2,1)S(1)} %get-tuple-element.11), channel_id=1, source_target_pairs={{0,24},{8,0},{16,8},{24,16},{1,25},{9,1},{17,9},{25,17},{2,26},{10... | collective-permute-start | bytes 215048 | tf_op jit(solution)/shard_map/ppermute | solution.py:364
  7.1 7.3 %collective-permute-start.2 = (bf16[8,4480]{1,0:T(8,128)(2,1)S(1)}, bf16[8,4480]{1,0:T(8,128)(2,1)S(1)}, u32[]{:S(2)}, u32[]{:S(2)}) collective-permute-start(bf16[8,4480]{1,0:T(8,128)(2,1)S(1)} %get-tuple-element.10.own_ref), channel_id=1, source_target_pairs={{0,16},{8,24},{16,0},{24,8},{1,17},{9,25},{17,1},{25,9},{2,18},{10... | collective-permute-start | bytes 215048 | tf_op jit(solution)/shard_map/ppermute | solution.py:364
  7.1 7.3 %collective-permute-start = (bf16[8,4480]{1,0:T(8,128)(2,1)S(1)}, bf16[8,4480]{1,0:T(8,128)(2,1)S(1)}, u32[]{:S(2)}, u32[]{:S(2)}) collective-permute-start(bf16[8,4480]{1,0:T(8,128)(2,1)S(1)} %get-tuple-element.10.own_ref), channel_id=1, source_target_pairs={{0,8},{8,16},{16,24},{24,0},{1,9},{9,17},{17,25},{25,1},{2,10},{10... | collective-permute-start | bytes 215048 | tf_op jit(solution)/shard_map/ppermute | solution.py:364
  14.5 6.2 %copy-start.2 = (bf16[7,16,16]{2,1,0:T(8,128)(2,1)S(1)}, bf16[7,16,16]{2,1,0:T(8,128)(2,1)}, u32[]{:S(2)}) copy-start(bf16[7,16,16]{2,1,0:T(8,128)(2,1)} %cw_ref.1) | copy-start | bytes 10756
  15.0 7.8 %collective-permute-start.4 = (bf16[32,4096]{1,0:T(8,128)(2,1)S(1)}, bf16[32,4096]{1,0:T(8,128)(2,1)S(1)}, u32[]{:S(2)}, u32[]{:S(2)}) collective-permute-start(bf16[32,4096]{1,0:T(8,128)(2,1)S(1)} %update.1.mid_ref), channel_id=1, source_target_pairs={{1,0},{2,1},{3,2},{4,3},{5,4},{6,5},{7,6},{9,8},{10,9},{11,10},{12... | collective-permute-start | bytes 786440 | tf_op jit(solution)/shard_map/ppermute | solution.py:406
  17.4 8.3 %collective-permute-start.3 = (bf16[32,4096]{1,0:T(8,128)(2,1)S(1)}, bf16[32,4096]{1,0:T(8,128)(2,1)S(1)}, u32[]{:S(2)}, u32[]{:S(2)}) collective-permute-start(bf16[32,4096]{1,0:T(8,128)(2,1)S(1)} %update.1.mid_ref), channel_id=1, source_target_pairs={{0,1},{1,2},{2,3},{3,4},{4,5},{5,6},{6,7},{8,9},{9,10},{10,11},{11... | collective-permute-start | bytes 786440 | tf_op jit(solution)/shard_map/ppermute | solution.py:405
  20.6 0.7 %copy-start.4 = (bf16[16,9]{1,0:T(8,128)(2,1)S(1)}, bf16[16,9]{1,0:T(8,128)(2,1)}, u32[]{:S(2)}) copy-start(bf16[16,9]{1,0:T(8,128)(2,1)} %sw_ref.1) | copy-start | bytes 868
  20.7 0.7 %copy-start.7 = (f32[16]{0:T(128)S(1)}, f32[16]{0:T(128)}, u32[]{:S(2)}) copy-start(f32[16]{0:T(128)} %param.16) | copy-start | bytes 196
  20.7 0.7 %copy-start.8 = (f32[16]{0:T(128)S(1)}, f32[16]{0:T(128)}, u32[]{:S(2)}) copy-start(f32[16]{0:T(128)} %param.18) | copy-start | bytes 196
  25.7 0.7 %copy-start.9 = (f32[16]{0:T(128)S(1)}, f32[16]{0:T(128)}, u32[]{:S(2)}) copy-start(f32[16]{0:T(128)} %ow_ref.1) | copy-start | bytes 196

commit v2 on v1

--- a/solution.py
+++ b/solution.py
@@ -45,7 +45,23 @@
     return hi, mid, x - hi - mid
 
 
-def project_kernel(reach, cube_ref, ap_ref, shear_ref, step_ref, up_ref, dn_ref, raw):
+def fetch(sources, targets, sems):
+    copies = [
+        pltpu.make_async_copy(src, dst, sems.at[i]) for i, (src, dst) in enumerate(zip(sources, targets))
+    ]
+    for copy in copies:
+        copy.start()
+    return copies
+
+
+def project_kernel(
+    reach, cube_in, ap_in, meas_in, shear_in, step_in, up_ref, dn_ref, *rest_refs
+):
+    kept, (raw, sems) = rest_refs[:5], rest_refs[5:]
+    cube_ref, ap_ref, meas_ref, shear_ref, step_ref = kept
+    copies = fetch((cube_in, ap_in, meas_in, shear_in, step_in), kept, sems)
+    for copy in copies:
+        copy.wait()
     bands, cols = cube_ref.shape
     groups = -(-bands // SUB)
     inner = cols // LANES
@@ -130,6 +146,7 @@
     own_ref,
     below_ref,
     above_ref,
+    _,
     *rest_refs,
 ):
     far_refs = rest_refs[:fars]
@@ -194,9 +211,18 @@
         out_ref[:, here] = jnp.concatenate(pieces, axis=0).astype(BF16)
 
 
-def weights_kernel(edge_ref, sw_ref, sb_ref, cw_ref, cb_ref, main_ref, halo_ref, band_ref):
+def weights_kernel(
+    _, sw_in, sb_in, cw_in, cb_in, ow_in, main_ref, halo_ref, first_ref, second_ref, out_w_ref, *rest
+):
+    local, sems = rest[:5], rest[5]
+    for copy in fetch((sw_in, sb_in, cw_in, cb_in, ow_in), local, sems):
+        copy.wait()
+    sw_ref, sb_ref, cw_ref, cb_ref, ow_ref = local
     ch, taps2 = sw_ref.shape
     taps = cw_ref.shape[0]
+    place = lax.axis_index("band")
+    has_low = jnp.where(place > 0, 1, 0)
+    has_high = jnp.where(place < lax.axis_size("band") - 1, 1, 0)
 
     def spread(rows, which):
         return (which(rows_of((rows, ch))) == lanes_of((rows, ch))).astype(F32).astype(BF16)
@@ -230,62 +256,63 @@
             jnp.where(keep, 0.5 * full, 0.0), bias_column(sb_ref, rows, which), taps2 * slots
         )
         if ref is halo_ref:
-            valid = jnp.where(band < 3, edge_ref[0], jnp.where(band >= 9, edge_ref[1], 1))
+            valid = jnp.where(band < 3, has_low, jnp.where(band >= 9, has_high, 1))
             matrix = jnp.where(valid > 0, matrix, 0.0)
         ref[...] = matrix.astype(BF16)
 
-    rows, width = band_ref.shape
-    per = rows // ch
+    per = SUB
+    rows = per * ch
+    width = first_ref.shape[1]
     used = (per + taps - 1) * ch
     which = lambda r: r // per
     fan = (lanes_of((ch, width)) % ch == rows_of((ch, width))).astype(F32).astype(BF16)
     picks = spread(rows, which)
     lane = lanes_of((rows, width))
-    ahead = lane // ch - rows_of((rows, width)) % per
-    matrix = jnp.zeros((rows, width), F32)
+    ahead = jnp.where(lane < used, lane // ch - rows_of((rows, width)) % per, -LANES)
+    shifts = (0, per, per - (per + taps - 1), 2 * per - (per + taps - 1))
+    blocks = [jnp.zeros((rows, width), F32) for _ in shifts]
     for d in range(taps):
         flat = jnp.dot(cw_ref[d], fan, preferred_element_type=F32).astype(BF16)
-        full = jnp.dot(picks, flat, preferred_element_type=F32)
-        matrix = jnp.where(ahead == d, 0.5 * full, matrix)
-    matrix = jnp.where(lane < used, matrix, 0.0)
-    matrix = with_bias(matrix, bias_column(cb_ref, rows, which), used)
-    band_ref[...] = matrix.astype(BF16)
+        full = 0.5 * jnp.dot(picks, flat, preferred_element_type=F32)
+        blocks = [jnp.where(ahead == d + s, full, b) for s, b in zip(shifts, blocks)]
+    bias = bias_column(cb_ref, rows, which)
+    for i, block in enumerate(blocks):
+        block = block if i == 2 else with_bias(block, bias, used)
+        ref = first_ref if i < 2 else second_ref
+        ref[i % 2 * rows : (i % 2 + 1) * rows, :] = block.astype(BF16)
+    pick = which(rows_of((rows, ch))) == lanes_of((rows, ch))
+    scale = jnp.sum(jnp.where(pick, ow_ref[...], 0.0), axis=1, keepdims=True)
+    out_w_ref[...] = jnp.broadcast_to(scale, out_w_ref.shape)
 
 
 def denoise_kernel(
-    tile, ow_ref, up_ref, mid_ref, dn_ref, main_ref, halo_ref, band_ref, out_ref, act
+    tile, ow_ref, up_ref, mid_ref, dn_ref, main_ref, halo_ref, first_ref, second_ref, out_ref, act
 ):
     bands, cols = out_ref.shape
     slots = 16
-    ch = ow_ref.shape[0]
+    ch = main_ref.shape[0] // slots
     tiles = cols // tile
     wide = tile + 2 * LANES
-    rows = act.shape[0]
-    act[rows - 2 * slots :, :] = jnp.zeros((2 * slots, tile), BF16)
+    split = act.shape[1] // 2
     ones = jnp.where(rows_of((slots, tile)) < 3, 1.0, 0.0).astype(BF16)
+    blank = jnp.zeros((32, LANES), F32)
 
     def silu_twice(half):
         return half + half * jnp.tanh(half)
 
-    def body(t, carry):
-        start = pl.multiple_of(t * tile, LANES)
-        before = pl.multiple_of(jnp.maximum(start - LANES, 0), LANES)
-        after = pl.multiple_of(jnp.minimum(start + tile, cols - LANES), LANES)
+    def spatial(t):
+        start = t * tile
         patches = []
-        center = None
         for ref in (up_ref, mid_ref, dn_ref):
-            left = ref[:, pl.ds(before, LANES)].astype(F32)
-            here = ref[:, pl.ds(start, tile)]
-            right = ref[:, pl.ds(after, LANES)].astype(F32)
-            left = jnp.where(t > 0, left, 0.0)
-            right = jnp.where(t < tiles - 1, right, 0.0)
-            here_f = here.astype(F32)
-            row = jnp.concatenate([left, here_f, right], axis=1)
+            left = ref[:, start - LANES : start].astype(F32) if t else blank
+            here = ref[:, start : start + tile]
+            end = start + tile
+            right = ref[:, end : end + LANES].astype(F32) if t < tiles - 1 else blank
+            row = jnp.concatenate([left, here.astype(F32), right], axis=1)
             back = pltpu.roll(row, 1, 1)[:, LANES : LANES + tile].astype(BF16)
             ahead = pltpu.roll(row, wide - 1, 1)[:, LANES : LANES + tile].astype(BF16)
             patches += [back, here, ahead]
-            if ref is mid_ref:
-                center = here_f
+        buf = act.at[t % act.shape[0]]
         for part, w_ref in enumerate((main_ref, halo_ref)):
             x = jnp.concatenate(
                 [p[part * slots : (part + 1) * slots] for p in patches] + [ones], axis=0
@@ -293,33 +320,53 @@
             half = jnp.dot(w_ref[...], x, preferred_element_type=F32)
             value = silu_twice(half).astype(BF16)
             if part == 0:
-                act[3 * ch : 19 * ch, :] = value
+                buf[3 * ch : 19 * ch, :] = value
             else:
-                act[0 : 3 * ch, :] = value[0 : 3 * ch]
-                act[19 * ch : 28 * ch, :] = value[3 * ch :]
-        weights = band_ref[...]
-        per = weights.shape[0] // ch
-        used = (per + 6) * ch
+                buf[0 : 3 * ch, :] = value[0 : 3 * ch]
+                buf[19 * ch : 28 * ch, :] = value[3 * ch :]
+
+    def spectral(t):
+        start = t * tile
+        buf = act.at[t % act.shape[0]]
+        halves = []
+        for part, w_ref in enumerate((first_ref, second_ref)):
+            x = jnp.concatenate([buf[part * split : (part + 1) * split, :], ones], axis=0)
+            halves.append(jnp.dot(w_ref[...], x, preferred_element_type=F32))
+        rows = SUB * ch
+        blocks = [halves[0][0:rows], halves[0][rows:] + halves[1][0:rows], halves[1][rows:]]
         pieces = []
-        for i in range(-(-bands // per)):
-            x = jnp.concatenate([act[i * per * ch : i * per * ch + used, :], ones], axis=0)
-            half = jnp.dot(weights, x, preferred_element_type=F32)
-            total = center[i * per : (i + 1) * per]
+        for half in blocks:
+            total = None
             for k in range(ch):
-                total = total + ow_ref[k] * silu_twice(half[k * per : (k + 1) * per])
+                weight = ow_ref[k * SUB : (k + 1) * SUB, :]
+                weight = jnp.concatenate([weight] * (tile // LANES), axis=1)
+                term = weight * silu_twice(half[k * SUB : (k + 1) * SUB])
+                total = term if total is None else total + term
             pieces.append(total)
-        result = jnp.concatenate(pieces, axis=0)[0:bands]
-        out_ref[:, pl.ds(start, tile)] = result.astype(BF16)
-        return carry
-
-    lax.fori_loop(0, tiles, body, 0)
+        update = jnp.concatenate(pieces, axis=0)[0:bands]
+        center = mid_ref[:, start : start + tile].astype(F32)[0:bands]
+        out_ref[:, start : start + tile] = (center + update).astype(BF16)
+
+    spatial(0)
+    for t in range(tiles):
+        if t + 1 < tiles:
+            spatial(t + 1)
+        spectral(t)
 
 
 def vmem(n):
     return [pl.BlockSpec(memory_space=pltpu.VMEM)] * n
 
 
-SMEM = pl.BlockSpec(memory_space=pltpu.SMEM)
+def hbm(n):
+    return [pl.BlockSpec(memory_space=pltpu.HBM)] * n
+
+
+def in_hbm(arrays):
+    return [pltpu.with_memory_space_constraint(x, pltpu.HBM) for x in arrays]
+
+
+ANY = pl.BlockSpec(memory_space=pl.ANY)
 
 
 def on_device(
@@ -350,15 +397,20 @@
     params = pltpu.CompilerParams(vmem_limit_bytes=48 * 2**20)
 
     payload = jax.ShapeDtypeStruct((SUB, outer * LANES), BF16)
-    up, dn = pl.pallas_call(
+    inputs = (cube, aperture, measurement, shear_row, step_row)
+    up, dn, *kept = pl.pallas_call(
         functools.partial(project_kernel, reach),
-        out_shape=(payload, payload),
-        in_specs=vmem(4),
-        out_specs=tuple(vmem(2)),
-        scratch_shapes=[pltpu.VMEM((groups * SUB, cols), F32)],
+        out_shape=(payload, payload)
+        + tuple(jax.ShapeDtypeStruct(x.shape, x.dtype) for x in inputs),
+        in_specs=hbm(5),
+        out_specs=tuple(vmem(7)),
+        scratch_shapes=[
+            pltpu.VMEM((groups * SUB, cols), F32),
+            pltpu.SemaphoreType.DMA((5,)),
+        ],
         compiler_params=params,
         name="project",
-    )(cube, aperture, shear_row, step_row)
+    )(*in_hbm(inputs))
 
     def around(x, shift):
         return lax.ppermute(x, "band", [(i, (i + shift) % count) for i in range(count)])
@@ -367,31 +419,35 @@
     above = around(dn, -1)
     far = [around(up, s) for s in range(2, count - 1)]
 
-    edges = jnp.stack([place > 0, place < count - 1]).astype(I32)
-    used = taps2 * 16
-    main_w, halo_w, band_w = pl.pallas_call(
-        weights_kernel,
-        out_shape=(
-            jax.ShapeDtypeStruct((16 * ch, used + 16), BF16),
-            jax.ShapeDtypeStruct((12 * ch, used + 16), BF16),
-            jax.ShapeDtypeStruct((SUB * ch, (SUB + taps - 1) * ch + 16), BF16),
-        ),
-        in_specs=[SMEM] + vmem(4),
-        out_specs=tuple(vmem(3)),
-        compiler_params=params,
-        name="weights",
-    )(
-        edges,
+    small = (
         spatial_weight,
         spatial_bias.reshape(1, ch),
         spectral_weight,
         spectral_bias.reshape(1, ch),
+        out_weight.reshape(1, ch),
     )
+    reached = (SUB + taps - 1) * ch
+    main_w, halo_w, first_w, second_w, out_w = pl.pallas_call(
+        weights_kernel,
+        out_shape=(
+            jax.ShapeDtypeStruct((16 * ch, taps2 * 16 + 16), BF16),
+            jax.ShapeDtypeStruct((12 * ch, taps2 * 16 + 16), BF16),
+            jax.ShapeDtypeStruct((2 * SUB * ch, reached + 16), BF16),
+            jax.ShapeDtypeStruct((2 * SUB * ch, reached + 16), BF16),
+            jax.ShapeDtypeStruct((SUB * ch, LANES), F32),
+        ),
+        in_specs=[ANY] + hbm(5),
+        out_specs=tuple(vmem(5)),
+        scratch_shapes=[pltpu.VMEM(x.shape, x.dtype) for x in small]
+        + [pltpu.SemaphoreType.DMA((5,))],
+        compiler_params=params,
+        name="weights",
+    )(up, *in_hbm(small))
 
     updated = pl.pallas_call(
         functools.partial(update_kernel, reach, len(far)),
         out_shape=jax.ShapeDtypeStruct((slots, cols), BF16),
-        in_specs=vmem(8 + len(far)),
+        in_specs=vmem(8) + [ANY] + vmem(len(far)),
         out_specs=vmem(1)[0],
         scratch_shapes=[
             pltpu.VMEM((groups * SUB, cols), F32),
@@ -399,7 +455,7 @@
         ],
         compiler_params=params,
         name="update",
-    )(cube, aperture, measurement, shear_row, step_row, up, below, above, *far)
+    )(*kept, up, below, above, out_w, *far)
 
     lines = lax.axis_size(("row", "col"))
     over = lax.ppermute(updated, ("row", "col"), [(i, i + 1) for i in range(lines - 1)])
@@ -409,12 +465,12 @@
     result = pl.pallas_call(
         functools.partial(denoise_kernel, tile),
         out_shape=jax.ShapeDtypeStruct((bands, cols), BF16),
-        in_specs=[SMEM] + vmem(6),
+        in_specs=vmem(8),
         out_specs=vmem(1)[0],
-        scratch_shapes=[pltpu.VMEM((30 * ch, tile), BF16)],
+        scratch_shapes=[pltpu.VMEM((4, 28 * ch, tile), BF16)],
         compiler_params=params,
         name="denoise",
-    )(out_weight, over, updated, under, main_w, halo_w, band_w)
+    )(out_w, over, updated, under, main_w, halo_w, first_w, second_w)
     return result.reshape(bands, 1, cols)
 
 

time: 33.3 us -> 28.4 us (0.85)
  local copies, waits for them, and re-layouts: 3.65 us -> 0 us
  Pallas kernels: 9.23 us -> 7.71 us
  waiting for transfers between devices: 9.75 us -> 10.2 us
    unnamed x20 -> x0, local copies, waits for them, and re-layouts: 3.65 us -> none
    pallas_call x1, Pallas kernels: 6.61 us -> 3.73 us  [on_device(): pl.pallas_call(functools.partial(denoise_kernel, tile), out_shape=jax.Sha...]
    ppermute x1, waiting for transfers between devices: 0.01 us -> 2.11 us  [on_device(): lax.ppermute(updated, ('row', 'col'), [(i + 1, i) for i in range(lines -...]
    ppermute x3, waiting for transfers between devices: 6.86 us -> 5 us  [around(): lax.ppermute(x, 'band', [(i, (i + shift) % count) for i in range(count)])]
    pallas_call x1, Pallas kernels: 0.61 us -> 1.62 us  [on_device(): pl.pallas_call(functools.partial(project_kernel, reach), out_shape=(paylo...]
    pallas_call x1, Pallas kernels: 1.48 us -> 1.84 us  [on_device(): pl.pallas_call(weights_kernel, out_shape=(jax.ShapeDtypeStruct((16 * ch,...]
  transfers between devices with their start and end apart: 5 -> 5, of which waited for: 3 -> 3; matrix products, arithmetic and copies ran while one was open for 0% -> 0% of each run, Pallas kernels for 4% -> 7%
where the time goes in v2:
time: 28.4 us; the launch traced here: 28.1 us
  starting transfers between devices  10.2 us (36%)
  waiting for transfers between devices  10.2 us (36%)
  Pallas kernels  7.71 us (27%)
    ppermute x3, waiting for transfers between devices, around(): lax.ppermute(x, 'band', [(i, (i + shift) % count) for i in range(count)])  5 us
    ppermute x3, starting transfers between devices, around(): lax.ppermute(x, 'band', [(i, (i + shift) % count) for i in range(count)])  4.66 us
    pallas_call x1, Pallas kernels, on_device(): pl.pallas_call(functools.partial(denoise_kernel, tile), out_shape=jax.Sha...  3.73 us
    ppermute x1, starting transfers between devices, on_device(): lax.ppermute(updated, ('row', 'col'), [(i, i + 1) for i in range(lines -...  3.12 us
    ppermute x1, waiting for transfers between devices, on_device(): lax.ppermute(updated, ('row', 'col'), [(i, i + 1) for i in range(lines -...  3.04 us
    ppermute x1, starting transfers between devices, on_device(): lax.ppermute(updated, ('row', 'col'), [(i + 1, i) for i in range(lines -...  2.44 us
    ppermute x1, waiting for transfers between devices, on_device(): lax.ppermute(updated, ('row', 'col'), [(i + 1, i) for i in range(lines -...  2.11 us
    pallas_call x1, Pallas kernels, on_device(): pl.pallas_call(weights_kernel, out_shape=(jax.ShapeDtypeStruct((16 * ch,...  1.84 us
  transfers between devices with their start and end apart: 5, of which 3 were waited for; matrix products, arithmetic and copies ran while one was open for 0% of the time, Pallas kernels for 7%

profile of v2, /device:TPU:1, one launch (start us, length us, event | category | flops | bytes accessed | tf_op | source)
XLA Modules:
  0.0 28.1 jit_solution(1421190625385050538)
XLA Ops:
  0.0 1.6 %project.1 = (bf16[8,4480]{1,0:T(8,128)(2,1)S(1)}, bf16[8,4480]{1,0:T(8,128)(2,1)S(1)}, bf16[22,4096]{1,0:T(8,128)(2,1)S(1)}, s32[1,4096]{1,0:T(1,128)S(1)}, f32...) custom-call(bf16[22,4096]{1,0:T(8,128)(2,1)} %bitcast.7, s32[1,4096]{1,0:T(1,128)} %ap_in.1, ...), custom_call_target="tpu_custom_call" | custom-call | tf_op jit(solution)/shard_map/project/pallas_call | solution.py:401
  1.6 4.2 %collective-permute-start.1 = (bf16[8,4480]{1,0:T(8,128)(2,1)S(1)}, bf16[8,4480]{1,0:T(8,128)(2,1)S(1)}, u32[]{:S(2)}, u32[]{:S(2)}) collective-permute-start(bf16[8,4480]{1,0:T(8,128)(2,1)S(1)} %get-tuple-element.24), channel_id=1, source_target_pairs={{0,24},{8,0},{16,8},{24,16},{1,25},{9,1},{17,9},{25,17},{2,26},{10... | collective-permute-start | bytes 215048 | tf_op jit(solution)/shard_map/ppermute | solution.py:416
  5.8 0.0 collective-permute-start.2
  5.8 0.5 %collective-permute-start = (bf16[8,4480]{1,0:T(8,128)(2,1)S(1)}, bf16[8,4480]{1,0:T(8,128)(2,1)S(1)}, u32[]{:S(2)}, u32[]{:S(2)}) collective-permute-start(bf16[8,4480]{1,0:T(8,128)(2,1)S(1)} %get-tuple-element.17._.own_ref), channel_id=1, source_target_pairs={{0,8},{8,16},{16,24},{24,0},{1,9},{9,17},{17,25},{25,1},{2,10},{10... | collective-permute-start | bytes 215048 | tf_op jit(solution)/shard_map/ppermute | solution.py:416
  6.3 1.8 %weights.1 = (bf16[256,160]{1,0:T(8,128)(2,1)S(1)}, bf16[192,160]{1,0:T(8,128)(2,1)S(1)}, bf16[256,240]{1,0:T(8,128)(2,1)S(1)}, bf16[256,240]{1,0:T(8,128)(2,1)S(1)}, f32[128,128]{1,0:T(8,128)S(1)}) custom-call(bf16[8,4480]{1,0:T(8,128)(2,1)S(1)} %get-tuple-element.17._.own_ref, bf16[16,9]{1,0:T(8,128)(2,1)} %sw_in.1, f32[1,16]{1,0:T(1,128)} %bitcast.10, ...), custom_call_target="tpu_custom_call" | custom-call | tf_op jit(solution)/shard_map/weights/pallas_call | solution.py:430
  8.1 0.0 collective-permute-done.1.above_ref
  8.1 5.0 %collective-permute-done.2.rest_refs_0_ = bf16[8,4480]{1,0:T(8,128)(2,1)S(1)} collective-permute-done((bf16[8,4480]{1,0:T(8,128)(2,1)S(1)}, bf16[8,4480]{1,0:T(8,128)(2,1)S(1)}, u32[]{:S(2)}, u32[]{:S(2)}) %collective-permute-start.2) | collective-permute-done | bytes 71712 | tf_op jit(solution)/shard_map/ppermute | solution.py:416
  13.1 0.0 collective-permute-done.below_ref
  13.1 0.5 %update.1.mid_ref = bf16[32,4096]{1,0:T(8,128)(2,1)S(1)} custom-call(bf16[22,4096]{1,0:T(8,128)(2,1)S(1)} %get-tuple-element.19.cube_ref, s32[1,4096]{1,0:T(1,128)S(1)} %get-tuple-element.20.ap_ref, f32[1,4444]{1,0:T(1,128)S(1)} %get-tuple-element.21.meas_ref, s32[1,22]{1,0:T(1,128)S(1)} %get-tuple-element.22.shear_ref, ...), custom_call_target="tpu_custom_call" | custom-call | tf_op jit(solution)/shard_map/update/pallas_call | solution.py:447
  13.7 2.4 %collective-permute-start.4 = (bf16[32,4096]{1,0:T(8,128)(2,1)S(1)}, bf16[32,4096]{1,0:T(8,128)(2,1)S(1)}, u32[]{:S(2)}, u32[]{:S(2)}) collective-permute-start(bf16[32,4096]{1,0:T(8,128)(2,1)S(1)} %update.1.mid_ref), channel_id=1, source_target_pairs={{1,0},{2,1},{3,2},{4,3},{5,4},{6,5},{7,6},{9,8},{10,9},{11,10},{12... | collective-permute-start | bytes 786440 | tf_op jit(solution)/shard_map/ppermute | solution.py:462
  16.1 3.1 %collective-permute-start.3 = (bf16[32,4096]{1,0:T(8,128)(2,1)S(1)}, bf16[32,4096]{1,0:T(8,128)(2,1)S(1)}, u32[]{:S(2)}, u32[]{:S(2)}) collective-permute-start(bf16[32,4096]{1,0:T(8,128)(2,1)S(1)} %update.1.mid_ref), channel_id=1, source_target_pairs={{0,1},{1,2},{2,3},{3,4},{4,5},{5,6},{6,7},{8,9},{9,10},{10,11},{11... | collective-permute-start | bytes 786440 | tf_op jit(solution)/shard_map/ppermute | solution.py:461
  19.3 2.1 %collective-permute-done.4.dn_ref = bf16[32,4096]{1,0:T(8,128)(2,1)S(1)} collective-permute-done((bf16[32,4096]{1,0:T(8,128)(2,1)S(1)}, bf16[32,4096]{1,0:T(8,128)(2,1)S(1)}, u32[]{:S(2)}, u32[]{:S(2)}) %collective-permute-start.4) | collective-permute-done | bytes 262176 | tf_op jit(solution)/shard_map/ppermute | solution.py:462
  21.4 3.0 %collective-permute-done.3.up_ref = bf16[32,4096]{1,0:T(8,128)(2,1)S(1)} collective-permute-done((bf16[32,4096]{1,0:T(8,128)(2,1)S(1)}, bf16[32,4096]{1,0:T(8,128)(2,1)S(1)}, u32[]{:S(2)}, u32[]{:S(2)}) %collective-permute-start.3) | collective-permute-done | bytes 262176 | tf_op jit(solution)/shard_map/ppermute | solution.py:461
  24.4 3.7 %denoise.1 = bf16[22,4096]{1,0:T(8,128)(2,1)} custom-call(f32[128,128]{1,0:T(8,128)S(1)} %get-tuple-element.18._.ow_ref, bf16[32,4096]{1,0:T(8,128)(2,1)S(1)} %collective-permute-done.3.up_ref, bf16[32,4096]{1,0:T(8,128)(2,1)S(1)} %update.1.mid_ref, bf16[32,4096]{1,0:T(8,128)(2,1)S(1)} %collective-permute-done.4.dn_ref, ...), custom_call_target="tpu_custom_call" | custom-call | tf_op jit(solution)/shard_map/denoise/pallas_call | solution.py:465
Async XLA Ops:
  1.6 6.5 %collective-permute-start.1 = (bf16[8,4480]{1,0:T(8,128)(2,1)S(1)}, bf16[8,4480]{1,0:T(8,128)(2,1)S(1)}, u32[]{:S(2)}, u32[]{:S(2)}) collective-permute-start(bf16[8,4480]{1,0:T(8,128)(2,1)S(1)} %get-tuple-element.24), channel_id=1, source_target_pairs={{0,24},{8,0},{16,8},{24,16},{1,25},{9,1},{17,9},{25,17},{2,26},{10... | collective-permute-start | bytes 215048 | tf_op jit(solution)/shard_map/ppermute | solution.py:416
  5.8 7.3 %collective-permute-start.2 = (bf16[8,4480]{1,0:T(8,128)(2,1)S(1)}, bf16[8,4480]{1,0:T(8,128)(2,1)S(1)}, u32[]{:S(2)}, u32[]{:S(2)}) collective-permute-start(bf16[8,4480]{1,0:T(8,128)(2,1)S(1)} %get-tuple-element.17._.own_ref), channel_id=1, source_target_pairs={{0,16},{8,24},{16,0},{24,8},{1,17},{9,25},{17,1},{25,9},{2,18},{10... | collective-permute-start | bytes 215048 | tf_op jit(solution)/shard_map/ppermute | solution.py:416
  5.8 7.3 %collective-permute-start = (bf16[8,4480]{1,0:T(8,128)(2,1)S(1)}, bf16[8,4480]{1,0:T(8,128)(2,1)S(1)}, u32[]{:S(2)}, u32[]{:S(2)}) collective-permute-start(bf16[8,4480]{1,0:T(8,128)(2,1)S(1)} %get-tuple-element.17._.own_ref), channel_id=1, source_target_pairs={{0,8},{8,16},{16,24},{24,0},{1,9},{9,17},{17,25},{25,1},{2,10},{10... | collective-permute-start | bytes 215048 | tf_op jit(solution)/shard_map/ppermute | solution.py:416
  13.7 7.7 %collective-permute-start.4 = (bf16[32,4096]{1,0:T(8,128)(2,1)S(1)}, bf16[32,4096]{1,0:T(8,128)(2,1)S(1)}, u32[]{:S(2)}, u32[]{:S(2)}) collective-permute-start(bf16[32,4096]{1,0:T(8,128)(2,1)S(1)} %update.1.mid_ref), channel_id=1, source_target_pairs={{1,0},{2,1},{3,2},{4,3},{5,4},{6,5},{7,6},{9,8},{10,9},{11,10},{12... | collective-permute-start | bytes 786440 | tf_op jit(solution)/shard_map/ppermute | solution.py:462
  16.1 8.3 %collective-permute-start.3 = (bf16[32,4096]{1,0:T(8,128)(2,1)S(1)}, bf16[32,4096]{1,0:T(8,128)(2,1)S(1)}, u32[]{:S(2)}, u32[]{:S(2)}) collective-permute-start(bf16[32,4096]{1,0:T(8,128)(2,1)S(1)} %update.1.mid_ref), channel_id=1, source_target_pairs={{0,1},{1,2},{2,3},{3,4},{4,5},{5,6},{6,7},{8,9},{9,10},{10,11},{11... | collective-permute-start | bytes 786440 | tf_op jit(solution)/shard_map/ppermute | solution.py:461

commit v3 on v2

--- a/solution.py
+++ b/solution.py
@@ -55,7 +55,7 @@
 
 
 def project_kernel(
-    reach, cube_in, ap_in, meas_in, shear_in, step_in, up_ref, dn_ref, *rest_refs
+    reach, cube_in, ap_in, meas_in, shear_in, step_in, part_ref, up_ref, dn_ref, *rest_refs
 ):
     kept, (raw, sems) = rest_refs[:5], rest_refs[5:]
     cube_ref, ap_ref, meas_ref, shear_ref, step_ref = kept
@@ -65,7 +65,8 @@
     bands, cols = cube_ref.shape
     groups = -(-bands // SUB)
     inner = cols // LANES
-    outer = up_ref.shape[1] // LANES
+    tall = part_ref.shape[0] // 2
+    outer = -(-meas_ref.shape[1] // LANES)
     raw[bands // SUB * SUB :, :] = jnp.zeros((raw.shape[0] - bands // SUB * SUB, cols), F32)
     raw[0:bands, :] = cube_ref[...].astype(F32)
     shear_f = column(shear_ref[...].astype(F32), groups * SUB)
@@ -81,7 +82,9 @@
     zero = jnp.zeros((SUB, LANES), F32)
     turned = [[zero] * (reach - 1) for _ in range(groups)]
     opened = [[zero] * (reach - 1) for _ in range(groups)]
-    low_first = (bands - 3) % SUB
+    sums = [zero] * (tall // SUB)
+    counts = [zero] * (tall // SUB)
+    firsts, lasts = [], []
     for p in range(outer):
         total = zero
         count = zero
@@ -92,6 +95,8 @@
             layers = [
                 raw[g * SUB : (g + 1) * SUB, p * LANES : (p + 1) * LANES] for g in range(groups)
             ]
+            firsts.append(layers[0])
+            lasts.append(layers[-1])
         for g in range(groups):
             if p < inner:
                 here = turn(layers[g] * open_p, index[g])
@@ -107,32 +112,28 @@
             if (g + 1) * SUB > bands:
                 part = jnp.where(sub < bands - g * SUB, part, 0.0)
             count = count + part
-        predicted = jnp.sum(total, axis=0, keepdims=True)
-        hi = predicted.astype(BF16).astype(F32)
-        lo = predicted - hi
-        counts = jnp.sum(count, axis=0, keepdims=True)
-        if p < inner:
-            first, last = layers[0], layers[-1]
-        elif p == inner:
-            sides = []
-            for g in (0, groups - 1):
-                s = shear_i[g * SUB : (g + 1) * SUB]
-                parts = [(s >> 1).astype(F32), (s & 1).astype(F32)]
-                parts += list(split3(step_f[g * SUB : (g + 1) * SUB]))
-                side = zero
-                for i, part in enumerate(parts):
-                    side = jnp.where(lane == i, part, side)
-                sides.append(side)
-            first, last = sides
-        else:
-            first = last = zero
-        up = jnp.where((sub >= low_first) & (sub < low_first + 3), last, 0.0)
-        dn = jnp.where(sub < 3, first, 0.0)
-        for i, value in enumerate((hi, lo, counts)):
-            up = jnp.where(sub == i, value, up)
-            dn = jnp.where(sub == 3 + i, value, dn)
-        up_ref[:, p * LANES : (p + 1) * LANES] = up.astype(BF16)
-        dn_ref[:, p * LANES : (p + 1) * LANES] = dn.astype(BF16)
+        v, at = divmod(p, SUB)
+        sums[v] = jnp.where(sub == at, jnp.sum(total, axis=0, keepdims=True), sums[v])
+        counts[v] = jnp.where(sub == at, jnp.sum(count, axis=0, keepdims=True), counts[v])
+    sides = []
+    for g in (0, groups - 1):
+        s = shear_i[g * SUB : (g + 1) * SUB]
+        parts = [(s >> 1).astype(F32), (s & 1).astype(F32)]
+        parts += list(split3(step_f[g * SUB : (g + 1) * SUB]))
+        side = zero
+        for i, part in enumerate(parts):
+            side = jnp.where(lane == i, part, side)
+        sides.append(side)
+    half = inner // 2
+    dn = [
+        jnp.where(sub < 3, firsts[q], pltpu.roll(firsts[q + half], 3, 0)) for q in range(half)
+    ] + [sides[0], zero]
+    up = [
+        jnp.where(sub < 3, pltpu.roll(lasts[q + half], SUB - 3, 0), lasts[q]) for q in range(half)
+    ] + [sides[1], zero]
+    part_ref[...] = jnp.concatenate(sums + counts, axis=0).astype(BF16)
+    up_ref[...] = jnp.concatenate(sums + counts + up, axis=0).astype(BF16)
+    dn_ref[...] = jnp.concatenate(sums + counts + dn, axis=0).astype(BF16)
 
 
 def update_kernel(
@@ -150,11 +151,13 @@
     *rest_refs,
 ):
     far_refs = rest_refs[:fars]
-    out_ref, raw, meas = rest_refs[fars:]
+    out_ref, raw, meas, rest_row = rest_refs[fars:]
     bands, cols = cube_ref.shape
     groups = -(-bands // SUB)
     inner = cols // LANES
-    outer = own_ref.shape[1] // LANES
+    half = inner // 2
+    tall = own_ref.shape[0] // 2
+    outer = -(-meas_ref.shape[1] // LANES)
     raw[bands // SUB * SUB :, :] = jnp.zeros((raw.shape[0] - bands // SUB * SUB, cols), F32)
     raw[0:bands, :] = cube_ref[...].astype(F32)
     meas[:, (outer - 1) * LANES :] = jnp.zeros((1, LANES), F32)
@@ -162,12 +165,30 @@
     shear_f = column(shear_ref[...].astype(F32), groups * SUB)
     step_f = column(step_ref[...], groups * SUB)
     lane, sub = lanes_of(), rows_of()
-
-    def halo(p):
-        where = slice(p * LANES, (p + 1) * LANES)
-        return jnp.where(sub < 3, above_ref[:, where].astype(F32), below_ref[:, where].astype(F32))
-
-    side = halo(inner)
+    below = below_ref[...].astype(F32)
+    above = above_ref[...].astype(F32)
+    sums = own_ref[...].astype(F32) + below[0 : 2 * tall] + above[0 : 2 * tall]
+    for far in far_refs:
+        sums = sums + far[...].astype(F32)
+    measured = []
+    for v in range(tall // SUB):
+        tile = jnp.zeros((SUB, LANES), F32)
+        for at in range(min(SUB, outer - v * SUB)):
+            p = v * SUB + at
+            tile = jnp.where(sub == at, meas[:, p * LANES : (p + 1) * LANES], tile)
+        measured.append(tile)
+    measured = jnp.concatenate(measured, axis=0)
+    rest_row[...] = (measured - sums[0:tall]) / jnp.maximum(sums[tall:], 1.0)
+
+    def halo(q):
+        at = 2 * tall + q % half * SUB
+        high, low = above[at : at + SUB], below[at : at + SUB]
+        if q // half == 1:
+            high, low = pltpu.roll(high, SUB - 3, 0), pltpu.roll(low, 3, 0)
+        return jnp.where(sub < 3, high, jnp.where(sub < 6, low, 0.0))
+
+    side = 2 * tall + half * SUB
+    side = jnp.where(sub < 3, above[side : side + SUB], below[side : side + SUB])
     shear_cols = [shear_f[g * SUB : (g + 1) * SUB] for g in range(groups)]
     step_cols = [step_f[g * SUB : (g + 1) * SUB] for g in range(groups)]
     inside = rows_of((SUB, 1)) < 6
@@ -183,15 +204,7 @@
     turned = [[] for _ in range(groups + 1)]
     for p in range(outer + 1):
         if p < outer:
-            where = slice(p * LANES, (p + 1) * LANES)
-            up_sum = own_ref[:, where].astype(F32) + below_ref[:, where].astype(F32)
-            for far in far_refs:
-                up_sum = up_sum + far[:, where].astype(F32)
-            dn_sum = above_ref[:, where].astype(F32)
-            predicted = up_sum[0:1] + up_sum[1:2] + dn_sum[3:4] + dn_sum[4:5]
-            counts = up_sum[2:3] + dn_sum[5:6]
-            residual = (meas[:, where] - predicted) / jnp.maximum(counts, 1.0)
-            residual = jnp.broadcast_to(residual, (SUB, LANES))
+            residual = jnp.broadcast_to(rest_row[p : p + 1, :], (SUB, LANES))
         else:
             residual = jnp.zeros((SUB, LANES), F32)
         for g in range(groups + 1):
@@ -205,8 +218,6 @@
         for g in range(groups + 1):
             pulled = choose(delay[g], turned[g][q : q + reach])
             base = raw[g * SUB : (g + 1) * SUB, here] if g < groups else halo(q)
-            if g == groups:
-                base = jnp.where(sub < 6, base, 0.0)
             pieces.append(base + pulled * open_q * steps[g])
         out_ref[:, here] = jnp.concatenate(pieces, axis=0).astype(BF16)
 
@@ -240,7 +251,13 @@
 
     width = main_ref.shape[1]
     slots = 16
-    fan = (lanes_of((taps2, width)) // slots == rows_of((taps2, width))).astype(F32).astype(BF16)
+    line = lax.axis_index("row") * lax.axis_size("col") + lax.axis_index("col")
+    lines = lax.axis_size("row") * lax.axis_size("col")
+    group = lanes_of((taps2, width)) // slots
+    offset = jnp.where(line % 2 == 1, group // 3, 2 - group // 3)
+    present = (line + offset >= 1) & (line + offset <= lines)
+    fan = (rows_of((taps2, width)) == 3 * offset + group % 3) & present
+    fan = fan.astype(F32).astype(BF16)
     flat = jnp.dot(sw_ref[...], fan, preferred_element_type=F32).astype(BF16)
     for ref, slot_of in (
         (main_ref, lambda b: b),
@@ -390,20 +407,24 @@
     taps, ch = spectral_weight.shape[:2]
     taps2 = spatial_weight.shape[1]
     count = lax.axis_size("band")
-    place = lax.axis_index("band")
     cube = spectral_cube.reshape(bands, cols)
     shear_row = shears.reshape(1, bands)
     step_row = step_sizes.reshape(1, bands)
     params = pltpu.CompilerParams(vmem_limit_bytes=48 * 2**20)
 
-    payload = jax.ShapeDtypeStruct((SUB, outer * LANES), BF16)
+    tall = -(-outer // SUB) * SUB
+    side = (cols // LANES // 2 + 2) * SUB
     inputs = (cube, aperture, measurement, shear_row, step_row)
-    up, dn, *kept = pl.pallas_call(
+    part, up, dn, *kept = pl.pallas_call(
         functools.partial(project_kernel, reach),
-        out_shape=(payload, payload)
+        out_shape=(
+            jax.ShapeDtypeStruct((2 * tall, LANES), BF16),
+            jax.ShapeDtypeStruct((2 * tall + side, LANES), BF16),
+            jax.ShapeDtypeStruct((2 * tall + side, LANES), BF16),
+        )
         + tuple(jax.ShapeDtypeStruct(x.shape, x.dtype) for x in inputs),
         in_specs=hbm(5),
-        out_specs=tuple(vmem(7)),
+        out_specs=tuple(vmem(8)),
         scratch_shapes=[
             pltpu.VMEM((groups * SUB, cols), F32),
             pltpu.SemaphoreType.DMA((5,)),
@@ -417,7 +438,7 @@
 
     below = around(up, 1)
     above = around(dn, -1)
-    far = [around(up, s) for s in range(2, count - 1)]
+    far = [around(part, s) for s in range(2, count - 1)]
 
     small = (
         spatial_weight,
@@ -442,7 +463,7 @@
         + [pltpu.SemaphoreType.DMA((5,))],
         compiler_params=params,
         name="weights",
-    )(up, *in_hbm(small))
+    )(part, *in_hbm(small))
 
     updated = pl.pallas_call(
         functools.partial(update_kernel, reach, len(far)),
@@ -452,14 +473,17 @@
         scratch_shapes=[
             pltpu.VMEM((groups * SUB, cols), F32),
             pltpu.VMEM((1, outer * LANES), F32),
+            pltpu.VMEM((tall, LANES), F32),
         ],
         compiler_params=params,
         name="update",
-    )(*kept, up, below, above, out_w, *far)
+    )(*kept, part, below, above, out_w, *far)
 
     lines = lax.axis_size(("row", "col"))
-    over = lax.ppermute(updated, ("row", "col"), [(i, i + 1) for i in range(lines - 1)])
-    under = lax.ppermute(updated, ("row", "col"), [(i + 1, i) for i in range(lines - 1)])
+    partner = lax.ppermute(updated, ("row", "col"), [(i, i ^ 1) for i in range(lines)])
+    other = lax.ppermute(
+        updated, ("row", "col"), [(i, (i - 1 + i % 2 * 2) % lines) for i in range(lines)]
+    )
 
     tile = 512
     result = pl.pallas_call(
@@ -470,7 +494,7 @@
         scratch_shapes=[pltpu.VMEM((4, 28 * ch, tile), BF16)],
         compiler_params=params,
         name="denoise",
-    )(out_w, over, updated, under, main_w, halo_w, first_w, second_w)
+    )(out_w, partner, updated, other, main_w, halo_w, first_w, second_w)
     return result.reshape(bands, 1, cols)
 
 

time: 28.4 us -> 24.2 us (0.85)
  starting transfers between devices: 10.2 us -> 7.89 us
  waiting for transfers between devices: 10.2 us -> 8.37 us
    ppermute x3, waiting for transfers between devices: 5 us -> 1.5 us  [around(): lax.ppermute(x, 'band', [(i, (i + shift) % count) for i in range(count)])]
    ppermute x2, starting transfers between devices: 5.56 us -> 3.24 us  [the longest x1 3.23 us: on_device(): lax.ppermute(updated, ('row', 'col'), [(i, (i - 1 + i % 2 * 2) % lines) f...]
    ppermute x2, waiting for transfers between devices: 5.15 us -> 6.87 us  [the longest x1 6.86 us: on_device(): lax.ppermute(updated, ('row', 'col'), [(i, (i - 1 + i % 2 * 2) % lines) f...]
  transfers between devices with their start and end apart: 5 -> 5, of which waited for: 3 -> 2; matrix products, arithmetic and copies ran while one was open for 0% -> 0% of each run, Pallas kernels for 7% -> 8%
where the time goes in v3:
time: 24.2 us; the launch traced here: 24 us
  waiting for transfers between devices  8.37 us (35%)
  starting transfers between devices  7.89 us (33%)
  Pallas kernels  7.76 us (32%)
    ppermute x1, waiting for transfers between devices, on_device(): lax.ppermute(updated, ('row', 'col'), [(i, (i - 1 + i % 2 * 2) % lines) f...  6.86 us
    ppermute x3, starting transfers between devices, around(): lax.ppermute(x, 'band', [(i, (i + shift) % count) for i in range(count)])  4.66 us
    pallas_call x1, Pallas kernels, on_device(): pl.pallas_call(functools.partial(denoise_kernel, tile), out_shape=jax.Sha...  3.76 us
    ppermute x1, starting transfers between devices, on_device(): lax.ppermute(updated, ('row', 'col'), [(i, (i - 1 + i % 2 * 2) % lines) f...  3.23 us
    pallas_call x1, Pallas kernels, on_device(): pl.pallas_call(weights_kernel, out_shape=(jax.ShapeDtypeStruct((16 * ch,...  1.85 us
    pallas_call x1, Pallas kernels, on_device(): pl.pallas_call(functools.partial(project_kernel, reach), out_shape=(jax.S...  1.62 us
    ppermute x3, waiting for transfers between devices, around(): lax.ppermute(x, 'band', [(i, (i + shift) % count) for i in range(count)])  1.5 us
    pallas_call x1, Pallas kernels, on_device(): pl.pallas_call(functools.partial(update_kernel, reach, len(far)), out_sha...  0.52 us
  transfers between devices with their start and end apart: 5, of which 2 were waited for; matrix products, arithmetic and copies ran while one was open for 0% of the time, Pallas kernels for 8%

profile of v3, /device:TPU:1, one launch (start us, length us, event | category | flops | bytes accessed | tf_op | source)
XLA Modules:
  0.0 24.0 jit_solution(9326758945607725057)
XLA Ops:
  0.0 1.6 %project.1 = (bf16[80,128]{1,0:T(8,128)(2,1)S(1)}, bf16[224,128]{1,0:T(8,128)(2,1)S(1)}, bf16[224,128]{1,0:T(8,128)(2,1)S(1)}, bf16[22,4096]{1,0:T(8,128)(2,1)S(...) custom-call(bf16[22,4096]{1,0:T(8,128)(2,1)} %bitcast.7, ...), custom_call_target="tpu_custom_call" | custom-call | tf_op jit(solution)/shard_map/project/pallas_call | solution.py:418
  1.6 2.2 %collective-permute-start = (bf16[224,128]{1,0:T(8,128)(2,1)S(1)}, bf16[224,128]{1,0:T(8,128)(2,1)S(1)}, u32[]{:S(2)}, u32[]{:S(2)}) collective-permute-start(bf16[224,128]{1,0:T(8,128)(2,1)S(1)} %get-tuple-element.25), channel_id=1, source_target_pairs={{0,8},{8,16},{16,24},{24,0},{1,9},{9,17},{17,25},{25,1},{2,10},{10... | collective-permute-start | bytes 172040 | tf_op jit(solution)/shard_map/ppermute | solution.py:437
  3.8 2.1 %collective-permute-start.1 = (bf16[224,128]{1,0:T(8,128)(2,1)S(1)}, bf16[224,128]{1,0:T(8,128)(2,1)S(1)}, u32[]{:S(2)}, u32[]{:S(2)}) collective-permute-start(bf16[224,128]{1,0:T(8,128)(2,1)S(1)} %get-tuple-element.26), channel_id=1, source_target_pairs={{0,24},{8,0},{16,8},{24,16},{1,25},{9,1},{17,9},{25,17},{2,26},{10... | collective-permute-start | bytes 172040 | tf_op jit(solution)/shard_map/ppermute | solution.py:437
  5.9 0.4 %collective-permute-start.2 = (bf16[80,128]{1,0:T(8,128)(2,1)S(1)}, bf16[80,128]{1,0:T(8,128)(2,1)S(1)}, u32[]{:S(2)}, u32[]{:S(2)}) collective-permute-start(bf16[80,128]{1,0:T(8,128)(2,1)S(1)} %get-tuple-element.18._.own_ref), channel_id=1, source_target_pairs={{0,16},{8,24},{16,0},{24,8},{1,17},{9,25},{17,1},{25,9},{2,18},{10... | collective-permute-start | bytes 61448 | tf_op jit(solution)/shard_map/ppermute | solution.py:437
  6.3 1.9 %weights.1 = (bf16[256,160]{1,0:T(8,128)(2,1)S(1)}, bf16[192,160]{1,0:T(8,128)(2,1)S(1)}, bf16[256,240]{1,0:T(8,128)(2,1)S(1)}, bf16[256,240]{1,0:T(8,128)(2,1)S(1)}, f32[128,128]{1,0:T(8,128)S(1)}) custom-call(bf16[80,128]{1,0:T(8,128)(2,1)S(1)} %get-tuple-element.18._.own_ref, bf16[16,9]{1,0:T(8,128)(2,1)} %sw_in.1, f32[1,16]{1,0:T(1,128)} %bitcast.10, ...), custom_call_target="tpu_custom_call" | custom-call | tf_op jit(solution)/shard_map/weights/pallas_call | solution.py:451
  8.2 1.5 %collective-permute-done.2.rest_refs_0_ = bf16[80,128]{1,0:T(8,128)(2,1)S(1)} collective-permute-done((bf16[80,128]{1,0:T(8,128)(2,1)S(1)}, bf16[80,128]{1,0:T(8,128)(2,1)S(1)}, u32[]{:S(2)}, u32[]{:S(2)}) %collective-permute-start.2) | collective-permute-done | bytes 20512 | tf_op jit(solution)/shard_map/ppermute | solution.py:437
  9.7 0.0 collective-permute-done.below_ref
  9.7 0.0 collective-permute-done.1.above_ref
  9.7 0.5 %update.1.mid_ref = bf16[32,4096]{1,0:T(8,128)(2,1)S(1)} custom-call(bf16[22,4096]{1,0:T(8,128)(2,1)S(1)} %get-tuple-element.20.cube_ref, s32[1,4096]{1,0:T(1,128)S(1)} %get-tuple-element.21.ap_ref, f32[1,4444]{1,0:T(1,128)S(1)} %get-tuple-element.22.meas_ref, s32[1,22]{1,0:T(1,128)S(1)} %get-tuple-element.23.shear_ref, ...), custom_call_target="tpu_custom_call" | custom-call | tf_op jit(solution)/shard_map/update/pallas_call | solution.py:468
  10.2 3.2 %collective-permute-start.4 = (bf16[32,4096]{1,0:T(8,128)(2,1)S(1)}, bf16[32,4096]{1,0:T(8,128)(2,1)S(1)}, u32[]{:S(2)}, u32[]{:S(2)}) collective-permute-start(bf16[32,4096]{1,0:T(8,128)(2,1)S(1)} %update.1.mid_ref), channel_id=1, source_target_pairs={{0,7},{1,2},{2,1},{3,4},{4,3},{5,6},{6,5},{7,0},{8,15},{9,10},{10,... | collective-permute-start | bytes 786440 | tf_op jit(solution)/shard_map/ppermute | solution.py:484
  13.4 0.0 collective-permute-start.3
  13.4 6.9 %collective-permute-done.4.dn_ref = bf16[32,4096]{1,0:T(8,128)(2,1)S(1)} collective-permute-done((bf16[32,4096]{1,0:T(8,128)(2,1)S(1)}, bf16[32,4096]{1,0:T(8,128)(2,1)S(1)}, u32[]{:S(2)}, u32[]{:S(2)}) %collective-permute-start.4) | collective-permute-done | bytes 262176 | tf_op jit(solution)/shard_map/ppermute | solution.py:484
  20.3 0.0 collective-permute-done.3.up_ref
  20.3 3.8 %denoise.1 = bf16[22,4096]{1,0:T(8,128)(2,1)} custom-call(f32[128,128]{1,0:T(8,128)S(1)} %get-tuple-element.19._.ow_ref, bf16[32,4096]{1,0:T(8,128)(2,1)S(1)} %collective-permute-done.3.up_ref, bf16[32,4096]{1,0:T(8,128)(2,1)S(1)} %update.1.mid_ref, bf16[32,4096]{1,0:T(8,128)(2,1)S(1)} %collective-permute-done.4.dn_ref, ...), custom_call_target="tpu_custom_call" | custom-call | tf_op jit(solution)/shard_map/denoise/pallas_call | solution.py:489
Async XLA Ops:
  1.6 8.0 %collective-permute-start = (bf16[224,128]{1,0:T(8,128)(2,1)S(1)}, bf16[224,128]{1,0:T(8,128)(2,1)S(1)}, u32[]{:S(2)}, u32[]{:S(2)}) collective-permute-start(bf16[224,128]{1,0:T(8,128)(2,1)S(1)} %get-tuple-element.25), channel_id=1, source_target_pairs={{0,8},{8,16},{16,24},{24,0},{1,9},{9,17},{17,25},{25,1},{2,10},{10... | collective-permute-start | bytes 172040 | tf_op jit(solution)/shard_map/ppermute | solution.py:437
  3.8 5.8 %collective-permute-start.1 = (bf16[224,128]{1,0:T(8,128)(2,1)S(1)}, bf16[224,128]{1,0:T(8,128)(2,1)S(1)}, u32[]{:S(2)}, u32[]{:S(2)}) collective-permute-start(bf16[224,128]{1,0:T(8,128)(2,1)S(1)} %get-tuple-element.26), channel_id=1, source_target_pairs={{0,24},{8,0},{16,8},{24,16},{1,25},{9,1},{17,9},{25,17},{2,26},{10... | collective-permute-start | bytes 172040 | tf_op jit(solution)/shard_map/ppermute | solution.py:437
  5.9 3.7 %collective-permute-start.2 = (bf16[80,128]{1,0:T(8,128)(2,1)S(1)}, bf16[80,128]{1,0:T(8,128)(2,1)S(1)}, u32[]{:S(2)}, u32[]{:S(2)}) collective-permute-start(bf16[80,128]{1,0:T(8,128)(2,1)S(1)} %get-tuple-element.18._.own_ref), channel_id=1, source_target_pairs={{0,16},{8,24},{16,0},{24,8},{1,17},{9,25},{17,1},{25,9},{2,18},{10... | collective-permute-start | bytes 61448 | tf_op jit(solution)/shard_map/ppermute | solution.py:437
  10.2 10.1 %collective-permute-start.4 = (bf16[32,4096]{1,0:T(8,128)(2,1)S(1)}, bf16[32,4096]{1,0:T(8,128)(2,1)S(1)}, u32[]{:S(2)}, u32[]{:S(2)}) collective-permute-start(bf16[32,4096]{1,0:T(8,128)(2,1)S(1)} %update.1.mid_ref), channel_id=1, source_target_pairs={{0,7},{1,2},{2,1},{3,4},{4,3},{5,6},{6,5},{7,0},{8,15},{9,10},{10,... | collective-permute-start | bytes 786440 | tf_op jit(solution)/shard_map/ppermute | solution.py:484
  13.4 6.9 %collective-permute-start.3 = (bf16[32,4096]{1,0:T(8,128)(2,1)S(1)}, bf16[32,4096]{1,0:T(8,128)(2,1)S(1)}, u32[]{:S(2)}, u32[]{:S(2)}) collective-permute-start(bf16[32,4096]{1,0:T(8,128)(2,1)S(1)} %update.1.mid_ref), channel_id=1, source_target_pairs={{0,1},{1,0},{2,3},{3,2},{4,5},{5,4},{6,7},{7,6},{8,9},{9,8},{10,11... | collective-permute-start | bytes 786440 | tf_op jit(solution)/shard_map/ppermute | solution.py:483

commit v4 on v3

--- a/solution.py
+++ b/solution.py
@@ -151,7 +151,7 @@
     *rest_refs,
 ):
     far_refs = rest_refs[:fars]
-    out_ref, raw, meas, rest_row = rest_refs[fars:]
+    out_ref, msg_ref, raw, meas, rest_row = rest_refs[fars:]
     bands, cols = cube_ref.shape
     groups = -(-bands // SUB)
     inner = cols // LANES
@@ -201,12 +201,14 @@
         index.append((lane + rest) & (LANES - 1))
         delay.append((s >> 7) + jnp.where(lane + rest >= LANES, 1, 0))
         steps.append(jnp.broadcast_to(step_cols[g], (SUB, LANES)))
+    tiles = []
     turned = [[] for _ in range(groups + 1)]
     for p in range(outer + 1):
         if p < outer:
             residual = jnp.broadcast_to(rest_row[p : p + 1, :], (SUB, LANES))
         else:
             residual = jnp.zeros((SUB, LANES), F32)
+        tiles.append(jnp.where(sub == 6, residual, 0.0))
         for g in range(groups + 1):
             turned[g].append(turn(residual, index[g]) if p < outer else residual)
         q = p - (reach - 1)
@@ -220,6 +222,10 @@
             base = raw[g * SUB : (g + 1) * SUB, here] if g < groups else halo(q)
             pieces.append(base + pulled * open_q * steps[g])
         out_ref[:, here] = jnp.concatenate(pieces, axis=0).astype(BF16)
+        tiles[q] = jnp.where(sub < 6, pieces[-1], jnp.where(sub == 6, tiles[q], open_q))
+    lost = rest_row[...]
+    lost = lost - lost.astype(BF16).astype(F32)
+    msg_ref[...] = jnp.concatenate(tiles + [lost], axis=0).astype(BF16)
 
 
 def weights_kernel(
@@ -303,27 +309,91 @@
 
 
 def denoise_kernel(
-    tile, ow_ref, up_ref, mid_ref, dn_ref, main_ref, halo_ref, first_ref, second_ref, out_ref, act
+    tile,
+    reach,
+    ow_ref,
+    mid_ref,
+    shear_ref,
+    step_ref,
+    raw0_ref,
+    msg0_ref,
+    raw1_ref,
+    msg1_ref,
+    main_ref,
+    halo_ref,
+    first_ref,
+    second_ref,
+    out_ref,
+    act,
+    near0,
+    near1,
+    words,
 ):
     bands, cols = out_ref.shape
     slots = 16
     ch = main_ref.shape[0] // slots
     tiles = cols // tile
+    inner = cols // LANES
     wide = tile + 2 * LANES
     split = act.shape[1] // 2
+    groups = -(-bands // SUB)
     ones = jnp.where(rows_of((slots, tile)) < 3, 1.0, 0.0).astype(BF16)
-    blank = jnp.zeros((32, LANES), F32)
+    blank = jnp.zeros((2 * slots, LANES), F32)
+    zero = jnp.zeros((SUB, LANES), F32)
+    shear_f = column(shear_ref[...].astype(F32), groups * SUB)
+    step_f = column(step_ref[...], groups * SUB)
+    lane = lanes_of()
+    index, delay, steps = [], [], []
+    for g in range(groups):
+        s = jnp.broadcast_to(shear_f[g * SUB : (g + 1) * SUB].astype(I32), (SUB, LANES))
+        rest = s & (LANES - 1)
+        index.append((lane + rest) & (LANES - 1))
+        delay.append((s >> 7) + jnp.where(lane + rest >= LANES, 1, 0))
+        steps.append(jnp.broadcast_to(step_f[g * SUB : (g + 1) * SUB], (SUB, LANES)))
+    rows_in = msg0_ref.shape[0]
+    chunks = inner + reach - 1
+    lost = rows_in - -(-chunks // SUB) * SUB
+    for n, msg_ref in enumerate((msg0_ref, msg1_ref)):
+        words[n * rows_in : (n + 1) * rows_in, :] = msg_ref[...].astype(F32)
+    turned = [[[] for _ in range(groups)] for _ in range(2)]
+
+    def neighbours(q):
+        for n, (raw_ref, near) in enumerate(((raw0_ref, near0), (raw1_ref, near1))):
+            base = n * rows_in
+            while len(turned[n][0]) < q + reach:
+                p = len(turned[n][0])
+                if p >= chunks:
+                    residual = zero
+                else:
+                    at = base + p * SUB + 6
+                    low = base + lost + p
+                    residual = jnp.broadcast_to(
+                        words[at : at + 1, :] + words[low : low + 1, :], (SUB, LANES)
+                    )
+                for g in range(groups):
+                    turned[n][g].append(turn(residual, index[g]))
+            at = base + q * SUB
+            open_q = jnp.broadcast_to(words[at + 7 : at + 8, :], (SUB, LANES))
+            raw = raw_ref[:, q * LANES : (q + 1) * LANES].astype(F32)
+            raw = jnp.concatenate([raw, jnp.zeros((groups * SUB - bands, LANES), F32)], axis=0)
+            pieces = [
+                raw[g * SUB : (g + 1) * SUB]
+                + choose(delay[g], turned[n][g][q : q + reach]) * open_q * steps[g]
+                for g in range(groups)
+            ]
+            pieces.append(words[at : at + SUB, :])
+            near[:, q * LANES : (q + 1) * LANES] = jnp.concatenate(pieces, axis=0).astype(BF16)
 
     def silu_twice(half):
         return half + half * jnp.tanh(half)
 
     def spatial(t):
         start = t * tile
+        end = start + tile
         patches = []
-        for ref in (up_ref, mid_ref, dn_ref):
+        for ref in (near0, mid_ref, near1):
             left = ref[:, start - LANES : start].astype(F32) if t else blank
-            here = ref[:, start : start + tile]
-            end = start + tile
+            here = ref[:, start:end]
             right = ref[:, end : end + LANES].astype(F32) if t < tiles - 1 else blank
             row = jnp.concatenate([left, here.astype(F32), right], axis=1)
             back = pltpu.roll(row, 1, 1)[:, LANES : LANES + tile].astype(BF16)
@@ -364,11 +434,15 @@
         center = mid_ref[:, start : start + tile].astype(F32)[0:bands]
         out_ref[:, start : start + tile] = (center + update).astype(BF16)
 
-    spatial(0)
-    for t in range(tiles):
-        if t + 1 < tiles:
-            spatial(t + 1)
-        spectral(t)
+    made = 0
+    for t in range(tiles + 1):
+        while t < tiles and made < min((t + 1) * tile // LANES + 1, inner):
+            neighbours(made)
+            made += 1
+        if t < tiles:
+            spatial(t)
+        if t:
+            spectral(t - 1)
 
 
 def vmem(n):
@@ -440,6 +514,12 @@
     above = around(dn, -1)
     far = [around(part, s) for s in range(2, count - 1)]
 
+    lines = lax.axis_size(("row", "col"))
+    pairs = [(i, i ^ 1) for i in range(lines)]
+    others = [(i, (i - 1 + i % 2 * 2) % lines) for i in range(lines)]
+    raw0 = lax.ppermute(kept[0], ("row", "col"), pairs)
+    raw1 = lax.ppermute(kept[0], ("row", "col"), others)
+
     small = (
         spatial_weight,
         spatial_bias.reshape(1, ch),
@@ -465,11 +545,15 @@
         name="weights",
     )(part, *in_hbm(small))
 
-    updated = pl.pallas_call(
+    words = (outer + 1) * SUB + tall
+    updated, message = pl.pallas_call(
         functools.partial(update_kernel, reach, len(far)),
-        out_shape=jax.ShapeDtypeStruct((slots, cols), BF16),
+        out_shape=(
+            jax.ShapeDtypeStruct((slots, cols), BF16),
+            jax.ShapeDtypeStruct((words, LANES), BF16),
+        ),
         in_specs=vmem(8) + [ANY] + vmem(len(far)),
-        out_specs=vmem(1)[0],
+        out_specs=tuple(vmem(2)),
         scratch_shapes=[
             pltpu.VMEM((groups * SUB, cols), F32),
             pltpu.VMEM((1, outer * LANES), F32),
@@ -479,22 +563,37 @@
         name="update",
     )(*kept, part, below, above, out_w, *far)
 
-    lines = lax.axis_size(("row", "col"))
-    partner = lax.ppermute(updated, ("row", "col"), [(i, i ^ 1) for i in range(lines)])
-    other = lax.ppermute(
-        updated, ("row", "col"), [(i, (i - 1 + i % 2 * 2) % lines) for i in range(lines)]
-    )
+    message0 = lax.ppermute(message, ("row", "col"), pairs)
+    message1 = lax.ppermute(message, ("row", "col"), others)
 
     tile = 512
     result = pl.pallas_call(
-        functools.partial(denoise_kernel, tile),
+        functools.partial(denoise_kernel, tile, reach),
         out_shape=jax.ShapeDtypeStruct((bands, cols), BF16),
-        in_specs=vmem(8),
+        in_specs=vmem(12),
         out_specs=vmem(1)[0],
-        scratch_shapes=[pltpu.VMEM((4, 28 * ch, tile), BF16)],
+        scratch_shapes=[
+            pltpu.VMEM((4, 28 * ch, tile), BF16),
+            pltpu.VMEM((slots, cols), BF16),
+            pltpu.VMEM((slots, cols), BF16),
+            pltpu.VMEM((2 * words, LANES), F32),
+        ],
         compiler_params=params,
         name="denoise",
-    )(out_w, partner, updated, other, main_w, halo_w, first_w, second_w)
+    )(
+        out_w,
+        updated,
+        kept[3],
+        kept[4],
+        raw0,
+        message0,
+        raw1,
+        message1,
+        main_w,
+        halo_w,
+        first_w,
+        second_w,
+    )
     return result.reshape(bands, 1, cols)
 
 

time: 24.2 us -> 24.6 us (1.017)
  the two profiles are of different devices: /device:TPU:1 before, /device:TPU:0 now
where the time goes in v4:
time: 24.6 us; the launch traced here: 24.4 us
  starting transfers between devices  9.37 us (38%)
  Pallas kernels  8.63 us (35%)
  waiting for transfers between devices  6.39 us (26%)
    pallas_call x1, Pallas kernels, on_device(): pl.pallas_call(functools.partial(denoise_kernel, tile, reach), out_shape=...  4.63 us
    ppermute x3, starting transfers between devices, around(): lax.ppermute(x, 'band', [(i, (i + shift) % count) for i in range(count)])  4.61 us
    ppermute x1, waiting for transfers between devices, on_device(): message1 = lax.ppermute(message, ('row', 'col'), others)  3.69 us
    ppermute x1, starting transfers between devices, on_device(): raw1 = lax.ppermute(kept[0], ('row', 'col'), others)  3.56 us
    ppermute x3, waiting for transfers between devices, around(): lax.ppermute(x, 'band', [(i, (i + shift) % count) for i in range(count)])  2.03 us
    pallas_call x1, Pallas kernels, on_device(): pl.pallas_call(weights_kernel, out_shape=(jax.ShapeDtypeStruct((16 * ch,...  1.85 us
    pallas_call x1, Pallas kernels, on_device(): pl.pallas_call(functools.partial(project_kernel, reach), out_shape=(jax.S...  1.63 us
    ppermute x1, waiting for transfers between devices, on_device(): message0 = lax.ppermute(message, ('row', 'col'), pairs)  0.66 us
  transfers between devices with their start and end apart: 7, of which 3 were waited for; matrix products, arithmetic and copies ran while one was open for 0% of the time, Pallas kernels for 10%

profile of v4, /device:TPU:0, one launch (start us, length us, event | category | flops | bytes accessed | tf_op | source)
XLA Modules:
  0.0 24.4 jit_solution(14921759592503186315)
XLA Ops:
  0.0 1.6 %project.1 = (bf16[80,128]{1,0:T(8,128)(2,1)S(1)}, bf16[224,128]{1,0:T(8,128)(2,1)S(1)}, bf16[224,128]{1,0:T(8,128)(2,1)S(1)}, bf16[22,4096]{1,0:T(8,128)(2,1)S(...) custom-call(bf16[22,4096]{1,0:T(8,128)(2,1)} %bitcast.7, ...), custom_call_target="tpu_custom_call" | custom-call | tf_op jit(solution)/shard_map/project/pallas_call | solution.py:492
  1.6 0.5 %collective-permute-start.3 = (bf16[22,4096]{1,0:T(8,128)(2,1)S(1)}, bf16[22,4096]{1,0:T(8,128)(2,1)S(1)}, u32[]{:S(2)}, u32[]{:S(2)}) collective-permute-start(bf16[22,4096]{1,0:T(8,128)(2,1)S(1)} %get-tuple-element.22.cube_ref), channel_id=1, source_target_pairs={{0,1},{1,0},{2,3},{3,2},{4,5},{5,4},{6,7},{7,6},{8,9},{9,8},{10,11... | collective-permute-start | bytes 540680 | tf_op jit(solution)/shard_map/ppermute | solution.py:520
  2.2 3.6 %collective-permute-start.5 = (bf16[22,4096]{1,0:T(8,128)(2,1)S(1)}, bf16[22,4096]{1,0:T(8,128)(2,1)S(1)}, u32[]{:S(2)}, u32[]{:S(2)}) collective-permute-start(bf16[22,4096]{1,0:T(8,128)(2,1)S(1)} %get-tuple-element.22.cube_ref), channel_id=1, source_target_pairs={{0,7},{1,2},{2,1},{3,4},{4,3},{5,6},{6,5},{7,0},{8,15},{9,10},{10,... | collective-permute-start | bytes 540680 | tf_op jit(solution)/shard_map/ppermute | solution.py:521
  5.7 1.6 %collective-permute-start = (bf16[224,128]{1,0:T(8,128)(2,1)S(1)}, bf16[224,128]{1,0:T(8,128)(2,1)S(1)}, u32[]{:S(2)}, u32[]{:S(2)}) collective-permute-start(bf16[224,128]{1,0:T(8,128)(2,1)S(1)} %get-tuple-element.27), channel_id=1, source_target_pairs={{0,8},{8,16},{16,24},{24,0},{1,9},{9,17},{17,25},{25,1},{2,10},{10... | collective-permute-start | bytes 172040 | tf_op jit(solution)/shard_map/ppermute | solution.py:511
  7.3 2.2 %collective-permute-start.1 = (bf16[224,128]{1,0:T(8,128)(2,1)S(1)}, bf16[224,128]{1,0:T(8,128)(2,1)S(1)}, u32[]{:S(2)}, u32[]{:S(2)}) collective-permute-start(bf16[224,128]{1,0:T(8,128)(2,1)S(1)} %get-tuple-element.28), channel_id=1, source_target_pairs={{0,24},{8,0},{16,8},{24,16},{1,25},{9,1},{17,9},{25,17},{2,26},{10... | collective-permute-start | bytes 172040 | tf_op jit(solution)/shard_map/ppermute | solution.py:511
  9.5 0.8 %collective-permute-start.2 = (bf16[80,128]{1,0:T(8,128)(2,1)S(1)}, bf16[80,128]{1,0:T(8,128)(2,1)S(1)}, u32[]{:S(2)}, u32[]{:S(2)}) collective-permute-start(bf16[80,128]{1,0:T(8,128)(2,1)S(1)} %get-tuple-element.20._.own_ref), channel_id=1, source_target_pairs={{0,16},{8,24},{16,0},{24,8},{1,17},{9,25},{17,1},{25,9},{2,18},{10... | collective-permute-start | bytes 61448 | tf_op jit(solution)/shard_map/ppermute | solution.py:511
  10.3 1.9 %weights.1 = (bf16[256,160]{1,0:T(8,128)(2,1)S(1)}, bf16[192,160]{1,0:T(8,128)(2,1)S(1)}, bf16[256,240]{1,0:T(8,128)(2,1)S(1)}, bf16[256,240]{1,0:T(8,128)(2,1)S(1)}, f32[128,128]{1,0:T(8,128)S(1)}) custom-call(bf16[80,128]{1,0:T(8,128)(2,1)S(1)} %get-tuple-element.20._.own_ref, bf16[16,9]{1,0:T(8,128)(2,1)} %sw_in.1, f32[1,16]{1,0:T(1,128)} %bitcast.10, ...), custom_call_target="tpu_custom_call" | custom-call | tf_op jit(solution)/shard_map/weights/pallas_call | solution.py:531
  12.2 2.0 %collective-permute-done.2.rest_refs_0_ = bf16[80,128]{1,0:T(8,128)(2,1)S(1)} collective-permute-done((bf16[80,128]{1,0:T(8,128)(2,1)S(1)}, bf16[80,128]{1,0:T(8,128)(2,1)S(1)}, u32[]{:S(2)}, u32[]{:S(2)}) %collective-permute-start.2) | collective-permute-done | bytes 20512 | tf_op jit(solution)/shard_map/ppermute | solution.py:511
  14.2 0.0 collective-permute-done.below_ref
  14.2 0.0 collective-permute-done.1.above_ref
  14.2 0.5 %update.1 = (bf16[32,4096]{1,0:T(8,128)(2,1)S(1)}, bf16[328,128]{1,0:T(8,128)(2,1)S(1)}) custom-call(bf16[22,4096]{1,0:T(8,128)(2,1)S(1)} %get-tuple-element.22.cube_ref, s32[1,4096]{1,0:T(1,128)S(1)} %get-tuple-element.23.ap_ref, f32[1,4444]{1,0:T(1,128)S(1)} %get-tuple-element.24.meas_ref, s32[1,22]{1,0:T(1,128)S(1)} %get-tuple-element.25.shear_ref, ...), custom_call_target="tpu_custom_call" | custom-call | tf_op jit(solution)/shard_map/update/pallas_call | solution.py:549
  14.7 0.1 collective-permute-start.4
  14.8 0.6 %collective-permute-start.6 = (bf16[328,128]{1,0:T(8,128)(2,1)S(1)}, bf16[328,128]{1,0:T(8,128)(2,1)S(1)}, u32[]{:S(2)}, u32[]{:S(2)}) collective-permute-start(bf16[328,128]{1,0:T(8,128)(2,1)S(1)} %get-tuple-element.30), channel_id=1, source_target_pairs={{0,7},{1,2},{2,1},{3,4},{4,3},{5,6},{6,5},{7,0},{8,15},{9,10},{10,... | collective-permute-start | bytes 251912 | tf_op jit(solution)/shard_map/ppermute | solution.py:567
  15.4 0.7 %collective-permute-done.4.msg0_ref = bf16[328,128]{1,0:T(8,128)(2,1)S(1)} collective-permute-done((bf16[328,128]{1,0:T(8,128)(2,1)S(1)}, bf16[328,128]{1,0:T(8,128)(2,1)S(1)}, u32[]{:S(2)}, u32[]{:S(2)}) %collective-permute-start.4) | collective-permute-done | bytes 84000 | tf_op jit(solution)/shard_map/ppermute | solution.py:566
  16.1 3.7 %collective-permute-done.6.msg1_ref = bf16[328,128]{1,0:T(8,128)(2,1)S(1)} collective-permute-done((bf16[328,128]{1,0:T(8,128)(2,1)S(1)}, bf16[328,128]{1,0:T(8,128)(2,1)S(1)}, u32[]{:S(2)}, u32[]{:S(2)}) %collective-permute-start.6) | collective-permute-done | bytes 84000 | tf_op jit(solution)/shard_map/ppermute | solution.py:567
  19.8 0.0 collective-permute-done.3.raw0_ref
  19.8 0.0 collective-permute-done.5.raw1_ref
  19.8 4.6 %denoise.1 = bf16[22,4096]{1,0:T(8,128)(2,1)} custom-call(f32[128,128]{1,0:T(8,128)S(1)} %get-tuple-element.21._.ow_ref, bf16[32,4096]{1,0:T(8,128)(2,1)S(1)} %get-tuple-element.29.mid_ref, s32[1,22]{1,0:T(1,128)S(1)} %get-tuple-element.25.shear_ref, f32[1,22]{1,0:T(1,128)S(1)} %get-tuple-element.26.step_ref, ...), custom_call_target="tpu_custom_call" | custom-call | tf_op jit(solution)/shard_map/denoise/pallas_call | solution.py:570
Async XLA Ops:
  1.6 18.1 %collective-permute-start.3 = (bf16[22,4096]{1,0:T(8,128)(2,1)S(1)}, bf16[22,4096]{1,0:T(8,128)(2,1)S(1)}, u32[]{:S(2)}, u32[]{:S(2)}) collective-permute-start(bf16[22,4096]{1,0:T(8,128)(2,1)S(1)} %get-tuple-element.22.cube_ref), channel_id=1, source_target_pairs={{0,1},{1,0},{2,3},{3,2},{4,5},{5,4},{6,7},{7,6},{8,9},{9,8},{10,11... | collective-permute-start | bytes 540680 | tf_op jit(solution)/shard_map/ppermute | solution.py:520
  2.2 17.6 %collective-permute-start.5 = (bf16[22,4096]{1,0:T(8,128)(2,1)S(1)}, bf16[22,4096]{1,0:T(8,128)(2,1)S(1)}, u32[]{:S(2)}, u32[]{:S(2)}) collective-permute-start(bf16[22,4096]{1,0:T(8,128)(2,1)S(1)} %get-tuple-element.22.cube_ref), channel_id=1, source_target_pairs={{0,7},{1,2},{2,1},{3,4},{4,3},{5,6},{6,5},{7,0},{8,15},{9,10},{10,... | collective-permute-start | bytes 540680 | tf_op jit(solution)/shard_map/ppermute | solution.py:521
  5.7 8.5 %collective-permute-start = (bf16[224,128]{1,0:T(8,128)(2,1)S(1)}, bf16[224,128]{1,0:T(8,128)(2,1)S(1)}, u32[]{:S(2)}, u32[]{:S(2)}) collective-permute-start(bf16[224,128]{1,0:T(8,128)(2,1)S(1)} %get-tuple-element.27), channel_id=1, source_target_pairs={{0,8},{8,16},{16,24},{24,0},{1,9},{9,17},{17,25},{25,1},{2,10},{10... | collective-permute-start | bytes 172040 | tf_op jit(solution)/shard_map/ppermute | solution.py:511
  7.3 6.9 %collective-permute-start.1 = (bf16[224,128]{1,0:T(8,128)(2,1)S(1)}, bf16[224,128]{1,0:T(8,128)(2,1)S(1)}, u32[]{:S(2)}, u32[]{:S(2)}) collective-permute-start(bf16[224,128]{1,0:T(8,128)(2,1)S(1)} %get-tuple-element.28), channel_id=1, source_target_pairs={{0,24},{8,0},{16,8},{24,16},{1,25},{9,1},{17,9},{25,17},{2,26},{10... | collective-permute-start | bytes 172040 | tf_op jit(solution)/shard_map/ppermute | solution.py:511
  9.5 4.7 %collective-permute-start.2 = (bf16[80,128]{1,0:T(8,128)(2,1)S(1)}, bf16[80,128]{1,0:T(8,128)(2,1)S(1)}, u32[]{:S(2)}, u32[]{:S(2)}) collective-permute-start(bf16[80,128]{1,0:T(8,128)(2,1)S(1)} %get-tuple-element.20._.own_ref), channel_id=1, source_target_pairs={{0,16},{8,24},{16,0},{24,8},{1,17},{9,25},{17,1},{25,9},{2,18},{10... | collective-permute-start | bytes 61448 | tf_op jit(solution)/shard_map/ppermute | solution.py:511
  14.7 1.3 %collective-permute-start.4 = (bf16[328,128]{1,0:T(8,128)(2,1)S(1)}, bf16[328,128]{1,0:T(8,128)(2,1)S(1)}, u32[]{:S(2)}, u32[]{:S(2)}) collective-permute-start(bf16[328,128]{1,0:T(8,128)(2,1)S(1)} %get-tuple-element.30), channel_id=1, source_target_pairs={{0,1},{1,0},{2,3},{3,2},{4,5},{5,4},{6,7},{7,6},{8,9},{9,8},{10,11... | collective-permute-start | bytes 251912 | tf_op jit(solution)/shard_map/ppermute | solution.py:566
  14.8 5.0 %collective-permute-start.6 = (bf16[328,128]{1,0:T(8,128)(2,1)S(1)}, bf16[328,128]{1,0:T(8,128)(2,1)S(1)}, u32[]{:S(2)}, u32[]{:S(2)}) collective-permute-start(bf16[328,128]{1,0:T(8,128)(2,1)S(1)} %get-tuple-element.30), channel_id=1, source_target_pairs={{0,7},{1,2},{2,1},{3,4},{4,3},{5,6},{6,5},{7,0},{8,15},{9,10},{10,... | collective-permute-start | bytes 251912 | tf_op jit(solution)/shard_map/ppermute | solution.py:567

commit v5 on v4

--- a/solution.py
+++ b/solution.py
@@ -228,33 +228,33 @@
     msg_ref[...] = jnp.concatenate(tiles + [lost], axis=0).astype(BF16)
 
 
-def weights_kernel(
-    _, sw_in, sb_in, cw_in, cb_in, ow_in, main_ref, halo_ref, first_ref, second_ref, out_w_ref, *rest
-):
-    local, sems = rest[:5], rest[5]
-    for copy in fetch((sw_in, sb_in, cw_in, cb_in, ow_in), local, sems):
+def spread(rows, ch, which):
+    return (which(rows_of((rows, ch))) == lanes_of((rows, ch))).astype(F32).astype(BF16)
+
+
+def picked(row_ref, rows, which):
+    ch = row_ref.shape[1]
+    pick = which(rows_of((rows, ch))) == lanes_of((rows, ch))
+    row = jnp.broadcast_to(row_ref[...], (rows, ch))
+    return jnp.sum(jnp.where(pick, row, 0.0), axis=1, keepdims=True)
+
+
+def with_bias(matrix, bias, start):
+    lane = lanes_of(matrix.shape)
+    for i, part in enumerate(split3(0.5 * bias)):
+        matrix = jnp.where(lane == start + i, part, matrix)
+    return matrix
+
+
+def spatial_weights_kernel(_, cube_ref, sw_in, sb_in, main_ref, halo_ref, same_ref, *rest):
+    local, sems = rest[:2], rest[2]
+    for copy in fetch((sw_in, sb_in), local, sems):
         copy.wait()
-    sw_ref, sb_ref, cw_ref, cb_ref, ow_ref = local
+    sw_ref, sb_ref = local
     ch, taps2 = sw_ref.shape
-    taps = cw_ref.shape[0]
     place = lax.axis_index("band")
     has_low = jnp.where(place > 0, 1, 0)
     has_high = jnp.where(place < lax.axis_size("band") - 1, 1, 0)
-
-    def spread(rows, which):
-        return (which(rows_of((rows, ch))) == lanes_of((rows, ch))).astype(F32).astype(BF16)
-
-    def bias_column(row_ref, rows, which):
-        pick = which(rows_of((rows, ch))) == lanes_of((rows, ch))
-        row = jnp.broadcast_to(row_ref[...], (rows, ch))
-        return 0.5 * jnp.sum(jnp.where(pick, row, 0.0), axis=1, keepdims=True)
-
-    def with_bias(matrix, bias, start):
-        lane = lanes_of(matrix.shape)
-        for i, part in enumerate(split3(bias)):
-            matrix = jnp.where(lane == start + i, part, matrix)
-        return matrix
-
     width = main_ref.shape[1]
     slots = 16
     line = lax.axis_index("row") * lax.axis_size("col") + lax.axis_index("col")
@@ -271,25 +271,32 @@
     ):
         rows = ref.shape[0]
         which = lambda r: r % ch
-        full = jnp.dot(spread(rows, which), flat, preferred_element_type=F32)
+        full = jnp.dot(spread(rows, ch, which), flat, preferred_element_type=F32)
         lane = lanes_of((rows, width))
         band = rows_of((rows, width)) // ch
         keep = (lane % slots == slot_of(band)) & (lane < taps2 * slots)
         matrix = with_bias(
-            jnp.where(keep, 0.5 * full, 0.0), bias_column(sb_ref, rows, which), taps2 * slots
+            jnp.where(keep, 0.5 * full, 0.0), picked(sb_ref, rows, which), taps2 * slots
         )
         if ref is halo_ref:
             valid = jnp.where(band < 3, has_low, jnp.where(band >= 9, has_high, 1))
             matrix = jnp.where(valid > 0, matrix, 0.0)
         ref[...] = matrix.astype(BF16)
 
+
+def spectral_weights_kernel(_, cw_in, cb_in, ow_in, first_ref, second_ref, out_w_ref, *rest):
+    local, sems = rest[:3], rest[3]
+    for copy in fetch((cw_in, cb_in, ow_in), local, sems):
+        copy.wait()
+    cw_ref, cb_ref, ow_ref = local
+    taps, ch = cw_ref.shape[:2]
     per = SUB
     rows = per * ch
     width = first_ref.shape[1]
     used = (per + taps - 1) * ch
     which = lambda r: r // per
     fan = (lanes_of((ch, width)) % ch == rows_of((ch, width))).astype(F32).astype(BF16)
-    picks = spread(rows, which)
+    picks = spread(rows, ch, which)
     lane = lanes_of((rows, width))
     ahead = jnp.where(lane < used, lane // ch - rows_of((rows, width)) % per, -LANES)
     shifts = (0, per, per - (per + taps - 1), 2 * per - (per + taps - 1))
@@ -298,14 +305,12 @@
         flat = jnp.dot(cw_ref[d], fan, preferred_element_type=F32).astype(BF16)
         full = 0.5 * jnp.dot(picks, flat, preferred_element_type=F32)
         blocks = [jnp.where(ahead == d + s, full, b) for s, b in zip(shifts, blocks)]
-    bias = bias_column(cb_ref, rows, which)
+    bias = picked(cb_ref, rows, which)
     for i, block in enumerate(blocks):
         block = block if i == 2 else with_bias(block, bias, used)
         ref = first_ref if i < 2 else second_ref
         ref[i % 2 * rows : (i % 2 + 1) * rows, :] = block.astype(BF16)
-    pick = which(rows_of((rows, ch))) == lanes_of((rows, ch))
-    scale = jnp.sum(jnp.where(pick, ow_ref[...], 0.0), axis=1, keepdims=True)
-    out_w_ref[...] = jnp.broadcast_to(scale, out_w_ref.shape)
+    out_w_ref[...] = jnp.broadcast_to(picked(ow_ref, rows, which), out_w_ref.shape)
 
 
 def denoise_kernel(
@@ -514,36 +519,46 @@
     above = around(dn, -1)
     far = [around(part, s) for s in range(2, count - 1)]
 
+    small = (spatial_weight, spatial_bias.reshape(1, ch))
+    main_w, halo_w, cube = pl.pallas_call(
+        spatial_weights_kernel,
+        out_shape=(
+            jax.ShapeDtypeStruct((16 * ch, taps2 * 16 + 16), BF16),
+            jax.ShapeDtypeStruct((12 * ch, taps2 * 16 + 16), BF16),
+            jax.ShapeDtypeStruct(cube.shape, BF16),
+        ),
+        in_specs=[ANY, ANY] + hbm(2),
+        out_specs=(*vmem(2), ANY),
+        scratch_shapes=[pltpu.VMEM(x.shape, x.dtype) for x in small]
+        + [pltpu.SemaphoreType.DMA((2,))],
+        input_output_aliases={1: 2},
+        compiler_params=params,
+        name="spatial_weights",
+    )(part, kept[0], *in_hbm(small))
+    kept[0] = cube
+
     lines = lax.axis_size(("row", "col"))
     pairs = [(i, i ^ 1) for i in range(lines)]
     others = [(i, (i - 1 + i % 2 * 2) % lines) for i in range(lines)]
-    raw0 = lax.ppermute(kept[0], ("row", "col"), pairs)
-    raw1 = lax.ppermute(kept[0], ("row", "col"), others)
-
-    small = (
-        spatial_weight,
-        spatial_bias.reshape(1, ch),
-        spectral_weight,
-        spectral_bias.reshape(1, ch),
-        out_weight.reshape(1, ch),
-    )
+    raw0 = lax.ppermute(cube, ("row", "col"), pairs)
+    raw1 = lax.ppermute(cube, ("row", "col"), others)
+
+    small = (spectral_weight, spectral_bias.reshape(1, ch), out_weight.reshape(1, ch))
     reached = (SUB + taps - 1) * ch
-    main_w, halo_w, first_w, second_w, out_w = pl.pallas_call(
-        weights_kernel,
+    first_w, second_w, out_w = pl.pallas_call(
+        spectral_weights_kernel,
         out_shape=(
-            jax.ShapeDtypeStruct((16 * ch, taps2 * 16 + 16), BF16),
-            jax.ShapeDtypeStruct((12 * ch, taps2 * 16 + 16), BF16),
             jax.ShapeDtypeStruct((2 * SUB * ch, reached + 16), BF16),
             jax.ShapeDtypeStruct((2 * SUB * ch, reached + 16), BF16),
             jax.ShapeDtypeStruct((SUB * ch, LANES), F32),
         ),
-        in_specs=[ANY] + hbm(5),
-        out_specs=tuple(vmem(5)),
+        in_specs=[ANY] + hbm(3),
+        out_specs=tuple(vmem(3)),
         scratch_shapes=[pltpu.VMEM(x.shape, x.dtype) for x in small]
-        + [pltpu.SemaphoreType.DMA((5,))],
+        + [pltpu.SemaphoreType.DMA((3,))],
         compiler_params=params,
-        name="weights",
-    )(part, *in_hbm(small))
+        name="spectral_weights",
+    )(halo_w, *in_hbm(small))
 
     words = (outer + 1) * SUB + tall
     updated, message = pl.pallas_call(
@@ -560,6 +575,9 @@
             pltpu.VMEM((tall, LANES), F32),
         ],
         compiler_params=params,
+        cost_estimate=pl.CostEstimate(
+            flops=10**10, bytes_accessed=4 * 10**7, transcendentals=0
+        ),
         name="update",
     )(*kept, part, below, above, out_w, *far)
 

time: 24.6 us -> 23.6 us (0.959)
  waiting for transfers between devices: 6.39 us -> 3.96 us
  Pallas kernels: 8.63 us -> 9.57 us
  starting transfers between devices: 9.37 us -> 9.82 us
    ppermute x3, waiting for transfers between devices: 2.03 us -> 0.01 us  [around(): lax.ppermute(x, 'band', [(i, (i + shift) % count) for i in range(count)])]
    ppermute x3, starting transfers between devices: 4.61 us -> 6.11 us  [around(): lax.ppermute(x, 'band', [(i, (i + shift) % count) for i in range(count)])]
    ppermute x2, starting transfers between devices: 4.07 us -> 2.62 us  [the longest x1 2.55 us: on_device(): raw1 = lax.ppermute(cube, ('row', 'col'), others)]
    pallas_call x1 -> x2, Pallas kernels: 1.85 us -> 2.75 us  [the longest x1 1.66 us: on_device(): pl.pallas_call(spectral_weights_kernel, out_shape=(jax.ShapeDtypeStruct((...]
    ppermute x1, starting transfers between devices: 0.61 us -> 1.01 us  [on_device(): message1 = lax.ppermute(message, ('row', 'col'), others)]
    ppermute x1, waiting for transfers between devices: 0.66 us -> 0.25 us  [on_device(): message0 = lax.ppermute(message, ('row', 'col'), pairs)]
  transfers between devices with their start and end apart: 7 -> 7, of which waited for: 3 -> 2; matrix products, arithmetic and copies ran while one was open for 0% -> 0% of each run, Pallas kernels for 10% -> 14%
where the time goes in v5:
time: 23.6 us; the launch traced here: 23.4 us
  starting transfers between devices  9.82 us (42%)
  Pallas kernels  9.57 us (41%)
  waiting for transfers between devices  3.96 us (17%)
    ppermute x3, starting transfers between devices, around(): lax.ppermute(x, 'band', [(i, (i + shift) % count) for i in range(count)])  6.11 us
    pallas_call x1, Pallas kernels, on_device(): pl.pallas_call(functools.partial(denoise_kernel, tile, reach), out_shape=...  4.68 us
    ppermute x1, waiting for transfers between devices, on_device(): message1 = lax.ppermute(message, ('row', 'col'), others)  3.69 us
    ppermute x1, starting transfers between devices, on_device(): raw1 = lax.ppermute(cube, ('row', 'col'), others)  2.55 us
    pallas_call x1, Pallas kernels, on_device(): pl.pallas_call(spectral_weights_kernel, out_shape=(jax.ShapeDtypeStruct((...  1.66 us
    pallas_call x1, Pallas kernels, on_device(): pl.pallas_call(functools.partial(project_kernel, reach), out_shape=(jax.S...  1.63 us
    pallas_call x1, Pallas kernels, on_device(): pl.pallas_call(spatial_weights_kernel, out_shape=(jax.ShapeDtypeStruct((1...  1.09 us
    ppermute x1, starting transfers between devices, on_device(): message1 = lax.ppermute(message, ('row', 'col'), others)  1.01 us
  transfers between devices with their start and end apart: 7, of which 2 were waited for; matrix products, arithmetic and copies ran while one was open for 0% of the time, Pallas kernels for 14%

profile of v5, /device:TPU:0, one launch (start us, length us, event | category | flops | bytes accessed | tf_op | source)
XLA Modules:
  0.0 23.4 jit_solution(16634939162642845076)
XLA Ops:
  0.0 1.6 %project.1 = (bf16[80,128]{1,0:T(8,128)(2,1)S(1)}, bf16[224,128]{1,0:T(8,128)(2,1)S(1)}, bf16[224,128]{1,0:T(8,128)(2,1)S(1)}, bf16[22,4096]{1,0:T(8,128)(2,1)S(...) custom-call(bf16[22,4096]{1,0:T(8,128)(2,1)} %bitcast.7, ...), custom_call_target="tpu_custom_call" | custom-call | tf_op jit(solution)/shard_map/project/pallas_call | solution.py:497
  1.6 3.1 %collective-permute-start = (bf16[224,128]{1,0:T(8,128)(2,1)S(1)}, bf16[224,128]{1,0:T(8,128)(2,1)S(1)}, u32[]{:S(2)}, u32[]{:S(2)}) collective-permute-start(bf16[224,128]{1,0:T(8,128)(2,1)S(1)} %get-tuple-element.30), channel_id=1, source_target_pairs={{0,8},{8,16},{16,24},{24,0},{1,9},{9,17},{17,25},{25,1},{2,10},{10... | collective-permute-start | bytes 172040 | tf_op jit(solution)/shard_map/ppermute | solution.py:516
  4.7 2.1 %collective-permute-start.1 = (bf16[224,128]{1,0:T(8,128)(2,1)S(1)}, bf16[224,128]{1,0:T(8,128)(2,1)S(1)}, u32[]{:S(2)}, u32[]{:S(2)}) collective-permute-start(bf16[224,128]{1,0:T(8,128)(2,1)S(1)} %get-tuple-element.31), channel_id=1, source_target_pairs={{0,24},{8,0},{16,8},{24,16},{1,25},{9,1},{17,9},{25,17},{2,26},{10... | collective-permute-start | bytes 172040 | tf_op jit(solution)/shard_map/ppermute | solution.py:516
  6.8 0.9 %collective-permute-start.2 = (bf16[80,128]{1,0:T(8,128)(2,1)S(1)}, bf16[80,128]{1,0:T(8,128)(2,1)S(1)}, u32[]{:S(2)}, u32[]{:S(2)}) collective-permute-start(bf16[80,128]{1,0:T(8,128)(2,1)S(1)} %get-tuple-element.21._.own_ref), channel_id=1, source_target_pairs={{0,16},{8,24},{16,0},{24,8},{1,17},{9,25},{17,1},{25,9},{2,18},{10... | collective-permute-start | bytes 61448 | tf_op jit(solution)/shard_map/ppermute | solution.py:516
  7.8 1.1 %spatial_weights.1 = (bf16[256,160]{1,0:T(8,128)(2,1)S(1)}, bf16[192,160]{1,0:T(8,128)(2,1)S(1)}, bf16[22,4096]{1,0:T(8,128)(2,1)S(1)}) custom-call(bf16[80,128]{1,0:T(8,128)(2,1)S(1)} %get-tuple-element.21._.own_ref, bf16[22,4096]{1,0:T(8,128)(2,1)S(1)} %get-tuple-element.22.cube_ref, bf16[16,9]{1,0:T(8,128)(2,1)} %sw_in.1, ...), custom_call_target="tpu_custom_call", output_to_operand_aliasing={{2}: (1, {})} | custom-call | tf_op jit(solution)/shard_map/spatial_weights/pallas_call | solution.py:523
  8.8 0.1 collective-permute-start.3
  8.9 2.6 %collective-permute-start.5 = (bf16[22,4096]{1,0:T(8,128)(2,1)S(1)}, bf16[22,4096]{1,0:T(8,128)(2,1)S(1)}, u32[]{:S(2)}, u32[]{:S(2)}) collective-permute-start(bf16[22,4096]{1,0:T(8,128)(2,1)S(1)} %get-tuple-element.25.cube_ref), channel_id=1, source_target_pairs={{0,7},{1,2},{2,1},{3,4},{4,3},{5,6},{6,5},{7,0},{8,15},{9,10},{10,... | collective-permute-start | bytes 540680 | tf_op jit(solution)/shard_map/ppermute | solution.py:544
  11.5 1.7 %spectral_weights.1 = (bf16[256,240]{1,0:T(8,128)(2,1)S(1)}, bf16[256,240]{1,0:T(8,128)(2,1)S(1)}, f32[128,128]{1,0:T(8,128)S(1)}) custom-call(bf16[192,160]{1,0:T(8,128)(2,1)S(1)} %get-tuple-element.23._.halo_ref, bf16[7,16,16]{2,1,0:T(8,128)(2,1)} %cw_in.1, f32[1,16]{1,0:T(1,128)} %bitcast.11, f32[1,16]{1,0:T(1,128)} %bitcast.12), custom_call_target="tpu_custom_call" | custom-call | tf_op jit(solution)/shard_map/spectral_weights/pallas_call | solution.py:548
  13.2 0.0 collective-permute-done.2.rest_refs_0_
  13.2 0.0 collective-permute-done.below_ref
  13.2 0.0 collective-permute-done.1.above_ref
  13.2 0.5 %update.1 = (bf16[32,4096]{1,0:T(8,128)(2,1)S(1)}, bf16[328,128]{1,0:T(8,128)(2,1)S(1)}) custom-call(bf16[22,4096]{1,0:T(8,128)(2,1)S(1)} %get-tuple-element.25.cube_ref, s32[1,4096]{1,0:T(1,128)S(1)} %get-tuple-element.26.ap_ref, f32[1,4444]{1,0:T(1,128)S(1)} %get-tuple-element.27.meas_ref, s32[1,22]{1,0:T(1,128)S(1)} %get-tuple-element.28.shear_ref, ...), custom_call_target="tpu_custom_call" | custom-call | flops 10000000000 | bytes 40000000 | tf_op jit(solution)/shard_map/update/pallas_call | solution.py:564
  13.7 0.1 collective-permute-start.4
  13.8 1.0 %collective-permute-start.6 = (bf16[328,128]{1,0:T(8,128)(2,1)S(1)}, bf16[328,128]{1,0:T(8,128)(2,1)S(1)}, u32[]{:S(2)}, u32[]{:S(2)}) collective-permute-start(bf16[328,128]{1,0:T(8,128)(2,1)S(1)} %get-tuple-element.33), channel_id=1, source_target_pairs={{0,7},{1,2},{2,1},{3,4},{4,3},{5,6},{6,5},{7,0},{8,15},{9,10},{10,... | collective-permute-start | bytes 251912 | tf_op jit(solution)/shard_map/ppermute | solution.py:585
  14.8 0.3 %collective-permute-done.4.msg0_ref = bf16[328,128]{1,0:T(8,128)(2,1)S(1)} collective-permute-done((bf16[328,128]{1,0:T(8,128)(2,1)S(1)}, bf16[328,128]{1,0:T(8,128)(2,1)S(1)}, u32[]{:S(2)}, u32[]{:S(2)}) %collective-permute-start.4) | collective-permute-done | bytes 84000 | tf_op jit(solution)/shard_map/ppermute | solution.py:584
  15.0 3.7 %collective-permute-done.6.msg1_ref = bf16[328,128]{1,0:T(8,128)(2,1)S(1)} collective-permute-done((bf16[328,128]{1,0:T(8,128)(2,1)S(1)}, bf16[328,128]{1,0:T(8,128)(2,1)S(1)}, u32[]{:S(2)}, u32[]{:S(2)}) %collective-permute-start.6) | collective-permute-done | bytes 84000 | tf_op jit(solution)/shard_map/ppermute | solution.py:585
  18.7 0.0 collective-permute-done.3.raw0_ref
  18.7 0.0 collective-permute-done.5.raw1_ref
  18.7 4.7 %denoise.1 = bf16[22,4096]{1,0:T(8,128)(2,1)} custom-call(f32[128,128]{1,0:T(8,128)S(1)} %get-tuple-element.24._.ow_ref, bf16[32,4096]{1,0:T(8,128)(2,1)S(1)} %get-tuple-element.32.mid_ref, s32[1,22]{1,0:T(1,128)S(1)} %get-tuple-element.28.shear_ref, f32[1,22]{1,0:T(1,128)S(1)} %get-tuple-element.29.step_ref, ...), custom_call_target="tpu_custom_call" | custom-call | tf_op jit(solution)/shard_map/denoise/pallas_call | solution.py:588
Async XLA Ops:
  1.6 11.5 %collective-permute-start = (bf16[224,128]{1,0:T(8,128)(2,1)S(1)}, bf16[224,128]{1,0:T(8,128)(2,1)S(1)}, u32[]{:S(2)}, u32[]{:S(2)}) collective-permute-start(bf16[224,128]{1,0:T(8,128)(2,1)S(1)} %get-tuple-element.30), channel_id=1, source_target_pairs={{0,8},{8,16},{16,24},{24,0},{1,9},{9,17},{17,25},{25,1},{2,10},{10... | collective-permute-start | bytes 172040 | tf_op jit(solution)/shard_map/ppermute | solution.py:516
  4.7 8.5 %collective-permute-start.1 = (bf16[224,128]{1,0:T(8,128)(2,1)S(1)}, bf16[224,128]{1,0:T(8,128)(2,1)S(1)}, u32[]{:S(2)}, u32[]{:S(2)}) collective-permute-start(bf16[224,128]{1,0:T(8,128)(2,1)S(1)} %get-tuple-element.31), channel_id=1, source_target_pairs={{0,24},{8,0},{16,8},{24,16},{1,25},{9,1},{17,9},{25,17},{2,26},{10... | collective-permute-start | bytes 172040 | tf_op jit(solution)/shard_map/ppermute | solution.py:516
  6.8 6.3 %collective-permute-start.2 = (bf16[80,128]{1,0:T(8,128)(2,1)S(1)}, bf16[80,128]{1,0:T(8,128)(2,1)S(1)}, u32[]{:S(2)}, u32[]{:S(2)}) collective-permute-start(bf16[80,128]{1,0:T(8,128)(2,1)S(1)} %get-tuple-element.21._.own_ref), channel_id=1, source_target_pairs={{0,16},{8,24},{16,0},{24,8},{1,17},{9,25},{17,1},{25,9},{2,18},{10... | collective-permute-start | bytes 61448 | tf_op jit(solution)/shard_map/ppermute | solution.py:516
  8.8 9.9 %collective-permute-start.3 = (bf16[22,4096]{1,0:T(8,128)(2,1)S(1)}, bf16[22,4096]{1,0:T(8,128)(2,1)S(1)}, u32[]{:S(2)}, u32[]{:S(2)}) collective-permute-start(bf16[22,4096]{1,0:T(8,128)(2,1)S(1)} %get-tuple-element.25.cube_ref), channel_id=1, source_target_pairs={{0,1},{1,0},{2,3},{3,2},{4,5},{5,4},{6,7},{7,6},{8,9},{9,8},{10,11... | collective-permute-start | bytes 540680 | tf_op jit(solution)/shard_map/ppermute | solution.py:543
  8.9 9.8 %collective-permute-start.5 = (bf16[22,4096]{1,0:T(8,128)(2,1)S(1)}, bf16[22,4096]{1,0:T(8,128)(2,1)S(1)}, u32[]{:S(2)}, u32[]{:S(2)}) collective-permute-start(bf16[22,4096]{1,0:T(8,128)(2,1)S(1)} %get-tuple-element.25.cube_ref), channel_id=1, source_target_pairs={{0,7},{1,2},{2,1},{3,4},{4,3},{5,6},{6,5},{7,0},{8,15},{9,10},{10,... | collective-permute-start | bytes 540680 | tf_op jit(solution)/shard_map/ppermute | solution.py:544
  13.7 1.3 %collective-permute-start.4 = (bf16[328,128]{1,0:T(8,128)(2,1)S(1)}, bf16[328,128]{1,0:T(8,128)(2,1)S(1)}, u32[]{:S(2)}, u32[]{:S(2)}) collective-permute-start(bf16[328,128]{1,0:T(8,128)(2,1)S(1)} %get-tuple-element.33), channel_id=1, source_target_pairs={{0,1},{1,0},{2,3},{3,2},{4,5},{5,4},{6,7},{7,6},{8,9},{9,8},{10,11... | collective-permute-start | bytes 251912 | tf_op jit(solution)/shard_map/ppermute | solution.py:584
  13.8 5.0 %collective-permute-start.6 = (bf16[328,128]{1,0:T(8,128)(2,1)S(1)}, bf16[328,128]{1,0:T(8,128)(2,1)S(1)}, u32[]{:S(2)}, u32[]{:S(2)}) collective-permute-start(bf16[328,128]{1,0:T(8,128)(2,1)S(1)} %get-tuple-element.33), channel_id=1, source_target_pairs={{0,7},{1,2},{2,1},{3,4},{4,3},{5,6},{6,5},{7,0},{8,15},{9,10},{10,... | collective-permute-start | bytes 251912 | tf_op jit(solution)/shard_map/ppermute | solution.py:585

commit v6 on v4

--- a/solution.py
+++ b/solution.py
@@ -57,9 +57,10 @@
 def project_kernel(
     reach, cube_in, ap_in, meas_in, shear_in, step_in, part_ref, up_ref, dn_ref, *rest_refs
 ):
-    kept, (raw, sems) = rest_refs[:5], rest_refs[5:]
-    cube_ref, ap_ref, meas_ref, shear_ref, step_ref = kept
-    copies = fetch((cube_in, ap_in, meas_in, shear_in, step_in), kept, sems)
+    line_ref, *kept = rest_refs[:5]
+    cube_ref, raw, sems = rest_refs[5:]
+    ap_ref, meas_ref, shear_ref, step_ref = kept
+    copies = fetch((cube_in, ap_in, meas_in, shear_in, step_in), (cube_ref, *kept), sems)
     for copy in copies:
         copy.wait()
     bands, cols = cube_ref.shape
@@ -97,6 +98,10 @@
             ]
             firsts.append(layers[0])
             lasts.append(layers[-1])
+            tagged = jnp.where(sub == bands % SUB, open_p, layers[-1])
+            line_ref[:, p * LANES : (p + 1) * LANES] = jnp.concatenate(
+                layers[:-1] + [tagged], axis=0
+            ).astype(BF16)
         for g in range(groups):
             if p < inner:
                 here = turn(layers[g] * open_p, index[g])
@@ -139,7 +144,7 @@
 def update_kernel(
     reach,
     fars,
-    cube_ref,
+    line_ref,
     ap_ref,
     meas_ref,
     shear_ref,
@@ -147,19 +152,17 @@
     own_ref,
     below_ref,
     above_ref,
-    _,
     *rest_refs,
 ):
     far_refs = rest_refs[:fars]
     out_ref, msg_ref, raw, meas, rest_row = rest_refs[fars:]
-    bands, cols = cube_ref.shape
-    groups = -(-bands // SUB)
+    groups = line_ref.shape[0] // SUB
+    cols = line_ref.shape[1]
     inner = cols // LANES
     half = inner // 2
     tall = own_ref.shape[0] // 2
     outer = -(-meas_ref.shape[1] // LANES)
-    raw[bands // SUB * SUB :, :] = jnp.zeros((raw.shape[0] - bands // SUB * SUB, cols), F32)
-    raw[0:bands, :] = cube_ref[...].astype(F32)
+    raw[...] = line_ref[...].astype(F32)
     meas[:, (outer - 1) * LANES :] = jnp.zeros((1, LANES), F32)
     meas[:, 0 : meas_ref.shape[1]] = meas_ref[...]
     shear_f = column(shear_ref[...].astype(F32), groups * SUB)
@@ -208,7 +211,8 @@
             residual = jnp.broadcast_to(rest_row[p : p + 1, :], (SUB, LANES))
         else:
             residual = jnp.zeros((SUB, LANES), F32)
-        tiles.append(jnp.where(sub == 6, residual, 0.0))
+        lost = residual - residual.astype(BF16).astype(F32)
+        tiles.append(jnp.where(sub < 7, residual, lost))
         for g in range(groups + 1):
             turned[g].append(turn(residual, index[g]) if p < outer else residual)
         q = p - (reach - 1)
@@ -222,10 +226,30 @@
             base = raw[g * SUB : (g + 1) * SUB, here] if g < groups else halo(q)
             pieces.append(base + pulled * open_q * steps[g])
         out_ref[:, here] = jnp.concatenate(pieces, axis=0).astype(BF16)
-        tiles[q] = jnp.where(sub < 6, pieces[-1], jnp.where(sub == 6, tiles[q], open_q))
-    lost = rest_row[...]
-    lost = lost - lost.astype(BF16).astype(F32)
-    msg_ref[...] = jnp.concatenate(tiles + [lost], axis=0).astype(BF16)
+        tiles[q] = jnp.where(sub < 6, pieces[-1], tiles[q])
+    msg_ref[...] = jnp.concatenate(tiles, axis=0).astype(BF16)
+
+
+def spread(rows, ch, which):
+    return (which(rows_of((rows, ch))) == lanes_of((rows, ch))).astype(F32).astype(BF16)
+
+
+def picked(row_ref, rows, which):
+    ch = row_ref.shape[1]
+    pick = which(rows_of((rows, ch))) == lanes_of((rows, ch))
+    row = jnp.broadcast_to(row_ref[...], (rows, ch))
+    return jnp.sum(jnp.where(pick, row, 0.0), axis=1, keepdims=True)
+
+
+def with_bias(matrix, bias, start):
+    lane = lanes_of(matrix.shape)
+    for i, part in enumerate(split3(0.5 * bias)):
+        matrix = jnp.where(lane == start + i, part, matrix)
+    return matrix
+
+
+def gate_kernel(_, line_ref, same_ref):
+    pass
 
 
 def weights_kernel(
@@ -240,21 +264,6 @@
     place = lax.axis_index("band")
     has_low = jnp.where(place > 0, 1, 0)
     has_high = jnp.where(place < lax.axis_size("band") - 1, 1, 0)
-
-    def spread(rows, which):
-        return (which(rows_of((rows, ch))) == lanes_of((rows, ch))).astype(F32).astype(BF16)
-
-    def bias_column(row_ref, rows, which):
-        pick = which(rows_of((rows, ch))) == lanes_of((rows, ch))
-        row = jnp.broadcast_to(row_ref[...], (rows, ch))
-        return 0.5 * jnp.sum(jnp.where(pick, row, 0.0), axis=1, keepdims=True)
-
-    def with_bias(matrix, bias, start):
-        lane = lanes_of(matrix.shape)
-        for i, part in enumerate(split3(bias)):
-            matrix = jnp.where(lane == start + i, part, matrix)
-        return matrix
-
     width = main_ref.shape[1]
     slots = 16
     line = lax.axis_index("row") * lax.axis_size("col") + lax.axis_index("col")
@@ -271,12 +280,12 @@
     ):
         rows = ref.shape[0]
         which = lambda r: r % ch
-        full = jnp.dot(spread(rows, which), flat, preferred_element_type=F32)
+        full = jnp.dot(spread(rows, ch, which), flat, preferred_element_type=F32)
         lane = lanes_of((rows, width))
         band = rows_of((rows, width)) // ch
         keep = (lane % slots == slot_of(band)) & (lane < taps2 * slots)
         matrix = with_bias(
-            jnp.where(keep, 0.5 * full, 0.0), bias_column(sb_ref, rows, which), taps2 * slots
+            jnp.where(keep, 0.5 * full, 0.0), picked(sb_ref, rows, which), taps2 * slots
         )
         if ref is halo_ref:
             valid = jnp.where(band < 3, has_low, jnp.where(band >= 9, has_high, 1))
@@ -289,7 +298,7 @@
     used = (per + taps - 1) * ch
     which = lambda r: r // per
     fan = (lanes_of((ch, width)) % ch == rows_of((ch, width))).astype(F32).astype(BF16)
-    picks = spread(rows, which)
+    picks = spread(rows, ch, which)
     lane = lanes_of((rows, width))
     ahead = jnp.where(lane < used, lane // ch - rows_of((rows, width)) % per, -LANES)
     shifts = (0, per, per - (per + taps - 1), 2 * per - (per + taps - 1))
@@ -298,14 +307,12 @@
         flat = jnp.dot(cw_ref[d], fan, preferred_element_type=F32).astype(BF16)
         full = 0.5 * jnp.dot(picks, flat, preferred_element_type=F32)
         blocks = [jnp.where(ahead == d + s, full, b) for s, b in zip(shifts, blocks)]
-    bias = bias_column(cb_ref, rows, which)
+    bias = picked(cb_ref, rows, which)
     for i, block in enumerate(blocks):
         block = block if i == 2 else with_bias(block, bias, used)
         ref = first_ref if i < 2 else second_ref
         ref[i % 2 * rows : (i % 2 + 1) * rows, :] = block.astype(BF16)
-    pick = which(rows_of((rows, ch))) == lanes_of((rows, ch))
-    scale = jnp.sum(jnp.where(pick, ow_ref[...], 0.0), axis=1, keepdims=True)
-    out_w_ref[...] = jnp.broadcast_to(scale, out_w_ref.shape)
+    out_w_ref[...] = jnp.broadcast_to(picked(ow_ref, rows, which), out_w_ref.shape)
 
 
 def denoise_kernel(
@@ -338,7 +345,7 @@
     split = act.shape[1] // 2
     groups = -(-bands // SUB)
     ones = jnp.where(rows_of((slots, tile)) < 3, 1.0, 0.0).astype(BF16)
-    blank = jnp.zeros((2 * slots, LANES), F32)
+    blank = jnp.zeros((2 * slots, LANES), BF16)
     zero = jnp.zeros((SUB, LANES), F32)
     shear_f = column(shear_ref[...].astype(F32), groups * SUB)
     step_f = column(step_ref[...], groups * SUB)
@@ -352,7 +359,6 @@
         steps.append(jnp.broadcast_to(step_f[g * SUB : (g + 1) * SUB], (SUB, LANES)))
     rows_in = msg0_ref.shape[0]
     chunks = inner + reach - 1
-    lost = rows_in - -(-chunks // SUB) * SUB
     for n, msg_ref in enumerate((msg0_ref, msg1_ref)):
         words[n * rows_in : (n + 1) * rows_in, :] = msg_ref[...].astype(F32)
     turned = [[[] for _ in range(groups)] for _ in range(2)]
@@ -366,16 +372,13 @@
                     residual = zero
                 else:
                     at = base + p * SUB + 6
-                    low = base + lost + p
-                    residual = jnp.broadcast_to(
-                        words[at : at + 1, :] + words[low : low + 1, :], (SUB, LANES)
-                    )
+                    residual = words[at : at + 1, :] + words[at + 1 : at + 2, :]
+                    residual = jnp.broadcast_to(residual, (SUB, LANES))
                 for g in range(groups):
                     turned[n][g].append(turn(residual, index[g]))
             at = base + q * SUB
-            open_q = jnp.broadcast_to(words[at + 7 : at + 8, :], (SUB, LANES))
             raw = raw_ref[:, q * LANES : (q + 1) * LANES].astype(F32)
-            raw = jnp.concatenate([raw, jnp.zeros((groups * SUB - bands, LANES), F32)], axis=0)
+            open_q = jnp.broadcast_to(raw[bands : bands + 1], (SUB, LANES))
             pieces = [
                 raw[g * SUB : (g + 1) * SUB]
                 + choose(delay[g], turned[n][g][q : q + reach]) * open_q * steps[g]
@@ -392,12 +395,12 @@
         end = start + tile
         patches = []
         for ref in (near0, mid_ref, near1):
-            left = ref[:, start - LANES : start].astype(F32) if t else blank
+            left = ref[:, start - LANES : start] if t else blank
             here = ref[:, start:end]
-            right = ref[:, end : end + LANES].astype(F32) if t < tiles - 1 else blank
-            row = jnp.concatenate([left, here.astype(F32), right], axis=1)
-            back = pltpu.roll(row, 1, 1)[:, LANES : LANES + tile].astype(BF16)
-            ahead = pltpu.roll(row, wide - 1, 1)[:, LANES : LANES + tile].astype(BF16)
+            right = ref[:, end : end + LANES] if t < tiles - 1 else blank
+            row = jnp.concatenate([left, here, right], axis=1)
+            back = pltpu.roll(row, 1, 1)[:, LANES : LANES + tile]
+            ahead = pltpu.roll(row, wide - 1, 1)[:, LANES : LANES + tile]
             patches += [back, here, ahead]
         buf = act.at[t % act.shape[0]]
         for part, w_ref in enumerate((main_ref, halo_ref)):
@@ -496,10 +499,12 @@
             jax.ShapeDtypeStruct((2 * tall + side, LANES), BF16),
             jax.ShapeDtypeStruct((2 * tall + side, LANES), BF16),
         )
-        + tuple(jax.ShapeDtypeStruct(x.shape, x.dtype) for x in inputs),
+        + (jax.ShapeDtypeStruct((groups * SUB, cols), BF16),)
+        + tuple(jax.ShapeDtypeStruct(x.shape, x.dtype) for x in inputs[1:]),
         in_specs=hbm(5),
         out_specs=tuple(vmem(8)),
         scratch_shapes=[
+            pltpu.VMEM((bands, cols), BF16),
             pltpu.VMEM((groups * SUB, cols), F32),
             pltpu.SemaphoreType.DMA((5,)),
         ],
@@ -514,11 +519,45 @@
     above = around(dn, -1)
     far = [around(part, s) for s in range(2, count - 1)]
 
+    line = pl.pallas_call(
+        gate_kernel,
+        out_shape=jax.ShapeDtypeStruct(kept[0].shape, BF16),
+        in_specs=[ANY, ANY],
+        out_specs=ANY,
+        input_output_aliases={1: 0},
+        name="gate",
+    )(part, kept[0])
+    kept[0] = line
+
     lines = lax.axis_size(("row", "col"))
     pairs = [(i, i ^ 1) for i in range(lines)]
     others = [(i, (i - 1 + i % 2 * 2) % lines) for i in range(lines)]
-    raw0 = lax.ppermute(kept[0], ("row", "col"), pairs)
-    raw1 = lax.ppermute(kept[0], ("row", "col"), others)
+    raw0 = lax.ppermute(line, ("row", "col"), pairs)
+    raw1 = lax.ppermute(line, ("row", "col"), others)
+
+    words = (outer + 1) * SUB
+    updated, message = pl.pallas_call(
+        functools.partial(update_kernel, reach, len(far)),
+        out_shape=(
+            jax.ShapeDtypeStruct((slots, cols), BF16),
+            jax.ShapeDtypeStruct((words, LANES), BF16),
+        ),
+        in_specs=vmem(8 + len(far)),
+        out_specs=tuple(vmem(2)),
+        scratch_shapes=[
+            pltpu.VMEM((groups * SUB, cols), F32),
+            pltpu.VMEM((1, outer * LANES), F32),
+            pltpu.VMEM((tall, LANES), F32),
+        ],
+        compiler_params=params,
+        cost_estimate=pl.CostEstimate(
+            flops=10**10, bytes_accessed=4 * 10**7, transcendentals=0
+        ),
+        name="update",
+    )(*kept, part, below, above, *far)
+
+    message0 = lax.ppermute(message, ("row", "col"), pairs)
+    message1 = lax.ppermute(message, ("row", "col"), others)
 
     small = (
         spatial_weight,
@@ -543,28 +582,7 @@
         + [pltpu.SemaphoreType.DMA((5,))],
         compiler_params=params,
         name="weights",
-    )(part, *in_hbm(small))
-
-    words = (outer + 1) * SUB + tall
-    updated, message = pl.pallas_call(
-        functools.partial(update_kernel, reach, len(far)),
-        out_shape=(
-            jax.ShapeDtypeStruct((slots, cols), BF16),
-            jax.ShapeDtypeStruct((words, LANES), BF16),
-        ),
-        in_specs=vmem(8) + [ANY] + vmem(len(far)),
-        out_specs=tuple(vmem(2)),
-        scratch_shapes=[
-            pltpu.VMEM((groups * SUB, cols), F32),
-            pltpu.VMEM((1, outer * LANES), F32),
-            pltpu.VMEM((tall, LANES), F32),
-        ],
-        compiler_params=params,
-        name="update",
-    )(*kept, part, below, above, out_w, *far)
-
-    message0 = lax.ppermute(message, ("row", "col"), pairs)
-    message1 = lax.ppermute(message, ("row", "col"), others)
+    )(message, *in_hbm(small))
 
     tile = 512
     result = pl.pallas_call(

time: 24.6 us -> 23.7 us (0.963)
  waiting for transfers between devices: 6.39 us -> 3.11 us
  local copies, waits for them, and re-layouts: 0 us -> 2.33 us
  Pallas kernels: 8.63 us -> 8.37 us
  starting transfers between devices: 9.37 us -> 9.62 us
    ppermute x1, waiting for transfers between devices: 3.69 us -> 1.07 us  [on_device(): message1 = lax.ppermute(message, ('row', 'col'), others)]
    ppermute x2, starting transfers between devices: 4.07 us -> 1.63 us  [the longest x1 1.05 us: on_device(): raw1 = lax.ppermute(line, ('row', 'col'), others)]
    unnamed x0 -> x8, local copies, waits for them, and re-layouts: none -> 2.33 us
    ppermute x3, starting transfers between devices: 4.61 us -> 6.06 us  [around(): lax.ppermute(x, 'band', [(i, (i + shift) % count) for i in range(count)])]
    ppermute x1, starting transfers between devices: 0.07 us -> 1.09 us  [on_device(): message0 = lax.ppermute(message, ('row', 'col'), pairs)]
    ppermute x1, waiting for transfers between devices: 0.66 us -> 0.01 us  [on_device(): message0 = lax.ppermute(message, ('row', 'col'), pairs)]
    pallas_call x1, Pallas kernels: 4.63 us -> 4.38 us  [on_device(): pl.pallas_call(functools.partial(denoise_kernel, tile, reach), out_shape=...]
  transfers between devices with their start and end apart: 7 -> 7, of which waited for: 3 -> 2; matrix products, arithmetic and copies ran while one was open for 0% -> 0% of each run, Pallas kernels for 10% -> 10%
where the time goes in v6:
time: 23.7 us; the launch traced here: 23.5 us
  starting transfers between devices  9.62 us (41%)
  Pallas kernels  8.37 us (35%)
  waiting for transfers between devices  3.11 us (13%)
  local copies, waits for them, and re-layouts  2.33 us (10%)
    ppermute x3, starting transfers between devices, around(): lax.ppermute(x, 'band', [(i, (i + shift) % count) for i in range(count)])  6.06 us
    pallas_call x1, Pallas kernels, on_device(): pl.pallas_call(functools.partial(denoise_kernel, tile, reach), out_shape=...  4.38 us
    unnamed x8, local copies, waits for them, and re-layouts  2.33 us
    ppermute x3, waiting for transfers between devices, around(): lax.ppermute(x, 'band', [(i, (i + shift) % count) for i in range(count)])  2.04 us
    pallas_call x1, Pallas kernels, on_device(): pl.pallas_call(weights_kernel, out_shape=(jax.ShapeDtypeStruct((16 * ch,...  1.85 us
    pallas_call x1, Pallas kernels, on_device(): pl.pallas_call(functools.partial(project_kernel, reach), out_shape=(jax.S...  1.63 us
    ppermute x1, starting transfers between devices, on_device(): message0 = lax.ppermute(message, ('row', 'col'), pairs)  1.09 us
    ppermute x1, waiting for transfers between devices, on_device(): message1 = lax.ppermute(message, ('row', 'col'), others)  1.07 us
  transfers between devices with their start and end apart: 7, of which 2 were waited for; matrix products, arithmetic and copies ran while one was open for 0% of the time, Pallas kernels for 10%

profile of v6, /device:TPU:0, one launch (start us, length us, event | category | flops | bytes accessed | tf_op | source)
XLA Modules:
  0.0 23.5 jit_solution(4571216811941879386)
XLA Ops:
  0.0 1.6 %project.1 = (bf16[80,128]{1,0:T(8,128)(2,1)S(1)}, bf16[224,128]{1,0:T(8,128)(2,1)S(1)}, bf16[224,128]{1,0:T(8,128)(2,1)S(1)}, bf16[24,4096]{1,0:T(8,128)(2,1)S(...) custom-call(bf16[22,4096]{1,0:T(8,128)(2,1)} %bitcast.7, ...), custom_call_target="tpu_custom_call" | custom-call | tf_op jit(solution)/shard_map/project/pallas_call | solution.py:495
  1.6 0.0 copy-start
  1.7 0.7 %copy-done = bf16[24,4096]{1,0:T(8,128)(2,1)} copy-done((bf16[24,4096]{1,0:T(8,128)(2,1)}, bf16[24,4096]{1,0:T(8,128)(2,1)S(1)}, u32[]{:S(2)}) %copy-start) | copy-done | bytes 196632
  2.3 0.0 copy-start.2
  2.3 3.0 %collective-permute-start = (bf16[224,128]{1,0:T(8,128)(2,1)S(1)}, bf16[224,128]{1,0:T(8,128)(2,1)S(1)}, u32[]{:S(2)}, u32[]{:S(2)}) collective-permute-start(bf16[224,128]{1,0:T(8,128)(2,1)S(1)} %get-tuple-element.26), channel_id=1, source_target_pairs={{0,8},{8,16},{16,24},{24,0},{1,9},{9,17},{17,25},{25,1},{2,10},{10... | collective-permute-start | bytes 172040 | tf_op jit(solution)/shard_map/ppermute | solution.py:516
  5.3 2.0 %collective-permute-start.1 = (bf16[224,128]{1,0:T(8,128)(2,1)S(1)}, bf16[224,128]{1,0:T(8,128)(2,1)S(1)}, u32[]{:S(2)}, u32[]{:S(2)}) collective-permute-start(bf16[224,128]{1,0:T(8,128)(2,1)S(1)} %get-tuple-element.27), channel_id=1, source_target_pairs={{0,24},{8,0},{16,8},{24,16},{1,25},{9,1},{17,9},{25,17},{2,26},{10... | collective-permute-start | bytes 172040 | tf_op jit(solution)/shard_map/ppermute | solution.py:516
  7.4 1.0 %collective-permute-start.2 = (bf16[80,128]{1,0:T(8,128)(2,1)S(1)}, bf16[80,128]{1,0:T(8,128)(2,1)S(1)}, u32[]{:S(2)}, u32[]{:S(2)}) collective-permute-start(bf16[80,128]{1,0:T(8,128)(2,1)S(1)} %get-tuple-element.20._.own_ref), channel_id=1, source_target_pairs={{0,16},{8,24},{16,0},{24,8},{1,17},{9,25},{17,1},{25,9},{2,18},{10... | collective-permute-start | bytes 61448 | tf_op jit(solution)/shard_map/ppermute | solution.py:516
  8.4 0.0 copy-done.2
  8.4 1.0 %collective-permute-start.5 = (bf16[24,4096]{1,0:T(8,128)(2,1)}, bf16[24,4096]{1,0:T(8,128)(2,1)S(1)}, u32[]{:S(2)}, u32[]{:S(2)}) collective-permute-start(bf16[24,4096]{1,0:T(8,128)(2,1)} %gate.1.line_ref), channel_id=1, source_target_pairs={{0,7},{1,2},{2,1},{3,4},{4,3},{5,6},{6,5},{7,0},{8,15},{9,10},{10,... | collective-permute-start | bytes 589832 | tf_op jit(solution)/shard_map/ppermute | solution.py:536
  9.4 0.6 %collective-permute-start.3 = (bf16[24,4096]{1,0:T(8,128)(2,1)}, bf16[24,4096]{1,0:T(8,128)(2,1)S(1)}, u32[]{:S(2)}, u32[]{:S(2)}) collective-permute-start(bf16[24,4096]{1,0:T(8,128)(2,1)} %gate.1.line_ref), channel_id=1, source_target_pairs={{0,1},{1,0},{2,3},{3,2},{4,5},{5,4},{6,7},{7,6},{8,9},{9,8},{10,11... | collective-permute-start | bytes 589832 | tf_op jit(solution)/shard_map/ppermute | solution.py:535
  10.0 2.0 %collective-permute-done.2.rest_refs_0_ = bf16[80,128]{1,0:T(8,128)(2,1)S(1)} collective-permute-done((bf16[80,128]{1,0:T(8,128)(2,1)S(1)}, bf16[80,128]{1,0:T(8,128)(2,1)S(1)}, u32[]{:S(2)}, u32[]{:S(2)}) %collective-permute-start.2) | collective-permute-done | bytes 20512 | tf_op jit(solution)/shard_map/ppermute | solution.py:516
  12.1 0.0 collective-permute-done.below_ref
  12.1 0.0 collective-permute-done.1.above_ref
  12.1 0.9 %copy-done.1 = bf16[24,4096]{1,0:T(8,128)(2,1)S(1)} copy-done((bf16[24,4096]{1,0:T(8,128)(2,1)S(1)}, bf16[24,4096]{1,0:T(8,128)(2,1)}, u32[]{:S(2)}) %copy-start.1) | copy-done | bytes 196632
  13.0 0.7 %copy-done.3 = bf16[80,128]{1,0:T(8,128)(2,1)S(1)} copy-done((bf16[80,128]{1,0:T(8,128)(2,1)S(1)}, bf16[80,128]{1,0:T(8,128)(2,1)}, u32[]{:S(2)}) %copy-start.3) | copy-done | bytes 20504
  13.7 0.5 %update.1 = (bf16[32,4096]{1,0:T(8,128)(2,1)S(1)}, bf16[288,128]{1,0:T(8,128)(2,1)S(1)}) custom-call(bf16[24,4096]{1,0:T(8,128)(2,1)S(1)} %copy-done.1, s32[1,4096]{1,0:T(1,128)S(1)} %get-tuple-element.22.ap_ref, f32[1,4444]{1,0:T(1,128)S(1)} %get-tuple-element.23.meas_ref, s32[1,22]{1,0:T(1,128)S(1)} %get-tuple-element.24.shear_ref, ...), custom_call_target="tpu_custom_call" | custom-call | flops 10000000000 | bytes 40000000 | tf_op jit(solution)/shard_map/update/pallas_call | solution.py:539
  14.2 0.8 %collective-permute-start.6 = (bf16[288,128]{1,0:T(8,128)(2,1)S(1)}, bf16[288,128]{1,0:T(8,128)(2,1)S(1)}, u32[]{:S(2)}, u32[]{:S(2)}) collective-permute-start(bf16[288,128]{1,0:T(8,128)(2,1)S(1)} %get-tuple-element.28._), channel_id=1, source_target_pairs={{0,7},{1,2},{2,1},{3,4},{4,3},{5,6},{6,5},{7,0},{8,15},{9,10},{10,... | collective-permute-start | bytes 221192 | tf_op jit(solution)/shard_map/ppermute | solution.py:560
  15.1 1.1 %collective-permute-start.4 = (bf16[288,128]{1,0:T(8,128)(2,1)S(1)}, bf16[288,128]{1,0:T(8,128)(2,1)S(1)}, u32[]{:S(2)}, u32[]{:S(2)}) collective-permute-start(bf16[288,128]{1,0:T(8,128)(2,1)S(1)} %get-tuple-element.28._), channel_id=1, source_target_pairs={{0,1},{1,0},{2,3},{3,2},{4,5},{5,4},{6,7},{7,6},{8,9},{9,8},{10,11... | collective-permute-start | bytes 221192 | tf_op jit(solution)/shard_map/ppermute | solution.py:559
  16.1 1.9 %weights.1 = (bf16[256,160]{1,0:T(8,128)(2,1)S(1)}, bf16[192,160]{1,0:T(8,128)(2,1)S(1)}, bf16[256,240]{1,0:T(8,128)(2,1)S(1)}, bf16[256,240]{1,0:T(8,128)(2,1)S(1)}, f32[128,128]{1,0:T(8,128)S(1)}) custom-call(bf16[288,128]{1,0:T(8,128)(2,1)S(1)} %get-tuple-element.28._, bf16[16,9]{1,0:T(8,128)(2,1)} %sw_in.1, f32[1,16]{1,0:T(1,128)} %bitcast.10, ...), custom_call_target="tpu_custom_call" | custom-call | tf_op jit(solution)/shard_map/weights/pallas_call | solution.py:570
  18.0 1.1 %collective-permute-done.6.msg1_ref = bf16[288,128]{1,0:T(8,128)(2,1)S(1)} collective-permute-done((bf16[288,128]{1,0:T(8,128)(2,1)S(1)}, bf16[288,128]{1,0:T(8,128)(2,1)S(1)}, u32[]{:S(2)}, u32[]{:S(2)}) %collective-permute-start.6) | collective-permute-done | bytes 73760 | tf_op jit(solution)/shard_map/ppermute | solution.py:560
  19.1 0.0 collective-permute-done.4.msg0_ref
  19.1 0.0 collective-permute-done.5.raw1_ref
  19.1 0.0 collective-permute-done.3.raw0_ref
  19.1 4.4 %denoise.1 = bf16[22,4096]{1,0:T(8,128)(2,1)} custom-call(f32[128,128]{1,0:T(8,128)S(1)} %get-tuple-element.29.ow_ref, bf16[32,4096]{1,0:T(8,128)(2,1)S(1)} %get-tuple-element.30.mid_ref, s32[1,22]{1,0:T(1,128)S(1)} %get-tuple-element.24.shear_ref, f32[1,22]{1,0:T(1,128)S(1)} %get-tuple-element.25.step_ref, ...), custom_call_target="tpu_custom_call" | custom-call | tf_op jit(solution)/shard_map/denoise/pallas_call | solution.py:588
  (3 shorter events, 0.0 us)
Async XLA Ops:
  1.6 0.7 %copy-start = (bf16[24,4096]{1,0:T(8,128)(2,1)}, bf16[24,4096]{1,0:T(8,128)(2,1)S(1)}, u32[]{:S(2)}) copy-start(bf16[24,4096]{1,0:T(8,128)(2,1)S(1)} %get-tuple-element.21.line_ref) | copy-start | bytes 589828
  2.3 6.1 %copy-start.2 = (bf16[80,128]{1,0:T(8,128)(2,1)}, bf16[80,128]{1,0:T(8,128)(2,1)S(1)}, u32[]{:S(2)}) copy-start(bf16[80,128]{1,0:T(8,128)(2,1)S(1)} %get-tuple-element.20._.own_ref) | copy-start | bytes 61444
  2.3 9.7 %collective-permute-start = (bf16[224,128]{1,0:T(8,128)(2,1)S(1)}, bf16[224,128]{1,0:T(8,128)(2,1)S(1)}, u32[]{:S(2)}, u32[]{:S(2)}) collective-permute-start(bf16[224,128]{1,0:T(8,128)(2,1)S(1)} %get-tuple-element.26), channel_id=1, source_target_pairs={{0,8},{8,16},{16,24},{24,0},{1,9},{9,17},{17,25},{25,1},{2,10},{10... | collective-permute-start | bytes 172040 | tf_op jit(solution)/shard_map/ppermute | solution.py:516
  5.3 6.7 %collective-permute-start.1 = (bf16[224,128]{1,0:T(8,128)(2,1)S(1)}, bf16[224,128]{1,0:T(8,128)(2,1)S(1)}, u32[]{:S(2)}, u32[]{:S(2)}) collective-permute-start(bf16[224,128]{1,0:T(8,128)(2,1)S(1)} %get-tuple-element.27), channel_id=1, source_target_pairs={{0,24},{8,0},{16,8},{24,16},{1,25},{9,1},{17,9},{25,17},{2,26},{10... | collective-permute-start | bytes 172040 | tf_op jit(solution)/shard_map/ppermute | solution.py:516
  7.4 4.7 %collective-permute-start.2 = (bf16[80,128]{1,0:T(8,128)(2,1)S(1)}, bf16[80,128]{1,0:T(8,128)(2,1)S(1)}, u32[]{:S(2)}, u32[]{:S(2)}) collective-permute-start(bf16[80,128]{1,0:T(8,128)(2,1)S(1)} %get-tuple-element.20._.own_ref), channel_id=1, source_target_pairs={{0,16},{8,24},{16,0},{24,8},{1,17},{9,25},{17,1},{25,9},{2,18},{10... | collective-permute-start | bytes 61448 | tf_op jit(solution)/shard_map/ppermute | solution.py:516
  8.4 10.7 %collective-permute-start.5 = (bf16[24,4096]{1,0:T(8,128)(2,1)}, bf16[24,4096]{1,0:T(8,128)(2,1)S(1)}, u32[]{:S(2)}, u32[]{:S(2)}) collective-permute-start(bf16[24,4096]{1,0:T(8,128)(2,1)} %gate.1.line_ref), channel_id=1, source_target_pairs={{0,7},{1,2},{2,1},{3,4},{4,3},{5,6},{6,5},{7,0},{8,15},{9,10},{10,... | collective-permute-start | bytes 589832 | tf_op jit(solution)/shard_map/ppermute | solution.py:536
  9.4 9.7 %collective-permute-start.3 = (bf16[24,4096]{1,0:T(8,128)(2,1)}, bf16[24,4096]{1,0:T(8,128)(2,1)S(1)}, u32[]{:S(2)}, u32[]{:S(2)}) collective-permute-start(bf16[24,4096]{1,0:T(8,128)(2,1)} %gate.1.line_ref), channel_id=1, source_target_pairs={{0,1},{1,0},{2,3},{3,2},{4,5},{5,4},{6,7},{7,6},{8,9},{9,8},{10,11... | collective-permute-start | bytes 589832 | tf_op jit(solution)/shard_map/ppermute | solution.py:535
  12.1 0.9 %copy-start.1 = (bf16[24,4096]{1,0:T(8,128)(2,1)S(1)}, bf16[24,4096]{1,0:T(8,128)(2,1)}, u32[]{:S(2)}) copy-start(bf16[24,4096]{1,0:T(8,128)(2,1)} %gate.1.line_ref) | copy-start | bytes 589828
  13.0 0.7 %copy-start.3 = (bf16[80,128]{1,0:T(8,128)(2,1)S(1)}, bf16[80,128]{1,0:T(8,128)(2,1)}, u32[]{:S(2)}) copy-start(bf16[80,128]{1,0:T(8,128)(2,1)} %copy-done.2) | copy-start | bytes 61444
  14.2 4.9 %collective-permute-start.6 = (bf16[288,128]{1,0:T(8,128)(2,1)S(1)}, bf16[288,128]{1,0:T(8,128)(2,1)S(1)}, u32[]{:S(2)}, u32[]{:S(2)}) collective-permute-start(bf16[288,128]{1,0:T(8,128)(2,1)S(1)} %get-tuple-element.28._), channel_id=1, source_target_pairs={{0,7},{1,2},{2,1},{3,4},{4,3},{5,6},{6,5},{7,0},{8,15},{9,10},{10,... | collective-permute-start | bytes 221192 | tf_op jit(solution)/shard_map/ppermute | solution.py:560
  15.1 4.0 %collective-permute-start.4 = (bf16[288,128]{1,0:T(8,128)(2,1)S(1)}, bf16[288,128]{1,0:T(8,128)(2,1)S(1)}, u32[]{:S(2)}, u32[]{:S(2)}) collective-permute-start(bf16[288,128]{1,0:T(8,128)(2,1)S(1)} %get-tuple-element.28._), channel_id=1, source_target_pairs={{0,1},{1,0},{2,3},{3,2},{4,5},{5,4},{6,7},{7,6},{8,9},{9,8},{10,11... | collective-permute-start | bytes 221192 | tf_op jit(solution)/shard_map/ppermute | solution.py:559

commit v7 on v6

--- a/solution.py
+++ b/solution.py
@@ -525,6 +525,7 @@
         in_specs=[ANY, ANY],
         out_specs=ANY,
         input_output_aliases={1: 0},
+        compiler_params=pltpu.CompilerParams(vmem_limit_bytes=2**20),
         name="gate",
     )(part, kept[0])
     kept[0] = line

time: 23.7 us -> 21.6 us (0.911)
  local copies, waits for them, and re-layouts: 2.33 us -> 0 us
    unnamed x8 -> x0, local copies, waits for them, and re-layouts: 2.33 us -> none
  transfers between devices with their start and end apart: 7 -> 7, of which waited for: 2 -> 2; matrix products, arithmetic and copies ran while one was open for 0% -> 0% of each run, Pallas kernels for 10% -> 11%
where the time goes in v7:
time: 21.6 us; the launch traced here: 21.4 us
  starting transfers between devices  9.61 us (44%)
  Pallas kernels  8.56 us (40%)
  waiting for transfers between devices  3.24 us (15%)
    ppermute x3, starting transfers between devices, around(): lax.ppermute(x, 'band', [(i, (i + shift) % count) for i in range(count)])  6.11 us
    pallas_call x1, Pallas kernels, on_device(): pl.pallas_call(functools.partial(denoise_kernel, tile, reach), out_shape=...  4.57 us
    ppermute x3, waiting for transfers between devices, around(): lax.ppermute(x, 'band', [(i, (i + shift) % count) for i in range(count)])  2.1 us
    pallas_call x1, Pallas kernels, on_device(): pl.pallas_call(weights_kernel, out_shape=(jax.ShapeDtypeStruct((16 * ch,...  1.85 us
    pallas_call x1, Pallas kernels, on_device(): pl.pallas_call(functools.partial(project_kernel, reach), out_shape=(jax.S...  1.63 us
    ppermute x1, waiting for transfers between devices, on_device(): message1 = lax.ppermute(message, ('row', 'col'), others)  1.13 us
    ppermute x1, starting transfers between devices, on_device(): message0 = lax.ppermute(message, ('row', 'col'), pairs)  1.08 us
    ppermute x1, starting transfers between devices, on_device(): raw1 = lax.ppermute(line, ('row', 'col'), others)  1.05 us
  transfers between devices with their start and end apart: 7, of which 2 were waited for; matrix products, arithmetic and copies ran while one was open for 0% of the time, Pallas kernels for 11%

profile of v7, /device:TPU:0, one launch (start us, length us, event | category | flops | bytes accessed | tf_op | source)
XLA Modules:
  0.0 21.4 jit_solution(8661952060880760937)
XLA Ops:
  0.0 1.6 %project.1 = (bf16[80,128]{1,0:T(8,128)(2,1)S(1)}, bf16[224,128]{1,0:T(8,128)(2,1)S(1)}, bf16[224,128]{1,0:T(8,128)(2,1)S(1)}, bf16[24,4096]{1,0:T(8,128)(2,1)S(...) custom-call(bf16[22,4096]{1,0:T(8,128)(2,1)} %bitcast.7, ...), custom_call_target="tpu_custom_call" | custom-call | tf_op jit(solution)/shard_map/project/pallas_call | solution.py:495
  1.6 3.1 %collective-permute-start = (bf16[224,128]{1,0:T(8,128)(2,1)S(1)}, bf16[224,128]{1,0:T(8,128)(2,1)S(1)}, u32[]{:S(2)}, u32[]{:S(2)}) collective-permute-start(bf16[224,128]{1,0:T(8,128)(2,1)S(1)} %get-tuple-element.26), channel_id=1, source_target_pairs={{0,8},{8,16},{16,24},{24,0},{1,9},{9,17},{17,25},{25,1},{2,10},{10... | collective-permute-start | bytes 172040 | tf_op jit(solution)/shard_map/ppermute | solution.py:516
  4.7 2.1 %collective-permute-start.1 = (bf16[224,128]{1,0:T(8,128)(2,1)S(1)}, bf16[224,128]{1,0:T(8,128)(2,1)S(1)}, u32[]{:S(2)}, u32[]{:S(2)}) collective-permute-start(bf16[224,128]{1,0:T(8,128)(2,1)S(1)} %get-tuple-element.27), channel_id=1, source_target_pairs={{0,24},{8,0},{16,8},{24,16},{1,25},{9,1},{17,9},{25,17},{2,26},{10... | collective-permute-start | bytes 172040 | tf_op jit(solution)/shard_map/ppermute | solution.py:516
  6.8 0.9 %collective-permute-start.2 = (bf16[80,128]{1,0:T(8,128)(2,1)S(1)}, bf16[80,128]{1,0:T(8,128)(2,1)S(1)}, u32[]{:S(2)}, u32[]{:S(2)}) collective-permute-start(bf16[80,128]{1,0:T(8,128)(2,1)S(1)} %get-tuple-element.20._.own_ref), channel_id=1, source_target_pairs={{0,16},{8,24},{16,0},{24,8},{1,17},{9,25},{17,1},{25,9},{2,18},{10... | collective-permute-start | bytes 61448 | tf_op jit(solution)/shard_map/ppermute | solution.py:516
  7.8 1.0 %collective-permute-start.5 = (bf16[24,4096]{1,0:T(8,128)(2,1)S(1)}, bf16[24,4096]{1,0:T(8,128)(2,1)S(1)}, u32[]{:S(2)}, u32[]{:S(2)}) collective-permute-start(bf16[24,4096]{1,0:T(8,128)(2,1)S(1)} %gate.1.line_ref), channel_id=1, source_target_pairs={{0,7},{1,2},{2,1},{3,4},{4,3},{5,6},{6,5},{7,0},{8,15},{9,10},{10,... | collective-permute-start | bytes 589832 | tf_op jit(solution)/shard_map/ppermute | solution.py:537
  8.8 0.6 %collective-permute-start.3 = (bf16[24,4096]{1,0:T(8,128)(2,1)S(1)}, bf16[24,4096]{1,0:T(8,128)(2,1)S(1)}, u32[]{:S(2)}, u32[]{:S(2)}) collective-permute-start(bf16[24,4096]{1,0:T(8,128)(2,1)S(1)} %gate.1.line_ref), channel_id=1, source_target_pairs={{0,1},{1,0},{2,3},{3,2},{4,5},{5,4},{6,7},{7,6},{8,9},{9,8},{10,11... | collective-permute-start | bytes 589832 | tf_op jit(solution)/shard_map/ppermute | solution.py:536
  9.4 2.1 %collective-permute-done.2.rest_refs_0_ = bf16[80,128]{1,0:T(8,128)(2,1)S(1)} collective-permute-done((bf16[80,128]{1,0:T(8,128)(2,1)S(1)}, bf16[80,128]{1,0:T(8,128)(2,1)S(1)}, u32[]{:S(2)}, u32[]{:S(2)}) %collective-permute-start.2) | collective-permute-done | bytes 20512 | tf_op jit(solution)/shard_map/ppermute | solution.py:516
  11.5 0.0 collective-permute-done.below_ref
  11.5 0.0 collective-permute-done.1.above_ref
  11.5 0.5 %update.1 = (bf16[32,4096]{1,0:T(8,128)(2,1)S(1)}, bf16[288,128]{1,0:T(8,128)(2,1)S(1)}) custom-call(bf16[24,4096]{1,0:T(8,128)(2,1)S(1)} %gate.1.line_ref, s32[1,4096]{1,0:T(1,128)S(1)} %get-tuple-element.22.ap_ref, f32[1,4444]{1,0:T(1,128)S(1)} %get-tuple-element.23.meas_ref, s32[1,22]{1,0:T(1,128)S(1)} %get-tuple-element.24.shear_ref, ...), custom_call_target="tpu_custom_call" | custom-call | flops 10000000000 | bytes 40000000 | tf_op jit(solution)/shard_map/update/pallas_call | solution.py:540
  12.0 0.8 %collective-permute-start.6 = (bf16[288,128]{1,0:T(8,128)(2,1)S(1)}, bf16[288,128]{1,0:T(8,128)(2,1)S(1)}, u32[]{:S(2)}, u32[]{:S(2)}) collective-permute-start(bf16[288,128]{1,0:T(8,128)(2,1)S(1)} %get-tuple-element.28._), channel_id=1, source_target_pairs={{0,7},{1,2},{2,1},{3,4},{4,3},{5,6},{6,5},{7,0},{8,15},{9,10},{10,... | collective-permute-start | bytes 221192 | tf_op jit(solution)/shard_map/ppermute | solution.py:561
  12.8 1.1 %collective-permute-start.4 = (bf16[288,128]{1,0:T(8,128)(2,1)S(1)}, bf16[288,128]{1,0:T(8,128)(2,1)S(1)}, u32[]{:S(2)}, u32[]{:S(2)}) collective-permute-start(bf16[288,128]{1,0:T(8,128)(2,1)S(1)} %get-tuple-element.28._), channel_id=1, source_target_pairs={{0,1},{1,0},{2,3},{3,2},{4,5},{5,4},{6,7},{7,6},{8,9},{9,8},{10,11... | collective-permute-start | bytes 221192 | tf_op jit(solution)/shard_map/ppermute | solution.py:560
  13.9 1.9 %weights.1 = (bf16[256,160]{1,0:T(8,128)(2,1)S(1)}, bf16[192,160]{1,0:T(8,128)(2,1)S(1)}, bf16[256,240]{1,0:T(8,128)(2,1)S(1)}, bf16[256,240]{1,0:T(8,128)(2,1)S(1)}, f32[128,128]{1,0:T(8,128)S(1)}) custom-call(bf16[288,128]{1,0:T(8,128)(2,1)S(1)} %get-tuple-element.28._, bf16[16,9]{1,0:T(8,128)(2,1)} %sw_in.1, f32[1,16]{1,0:T(1,128)} %bitcast.10, ...), custom_call_target="tpu_custom_call" | custom-call | tf_op jit(solution)/shard_map/weights/pallas_call | solution.py:571
  15.7 1.1 %collective-permute-done.6.msg1_ref = bf16[288,128]{1,0:T(8,128)(2,1)S(1)} collective-permute-done((bf16[288,128]{1,0:T(8,128)(2,1)S(1)}, bf16[288,128]{1,0:T(8,128)(2,1)S(1)}, u32[]{:S(2)}, u32[]{:S(2)}) %collective-permute-start.6) | collective-permute-done | bytes 73760 | tf_op jit(solution)/shard_map/ppermute | solution.py:561
  16.9 0.0 collective-permute-done.4.msg0_ref
  16.9 0.0 collective-permute-done.5.raw1_ref
  16.9 0.0 collective-permute-done.3.raw0_ref
  16.9 4.6 %denoise.1 = bf16[22,4096]{1,0:T(8,128)(2,1)} custom-call(f32[128,128]{1,0:T(8,128)S(1)} %get-tuple-element.29.ow_ref, bf16[32,4096]{1,0:T(8,128)(2,1)S(1)} %get-tuple-element.30.mid_ref, s32[1,22]{1,0:T(1,128)S(1)} %get-tuple-element.24.shear_ref, f32[1,22]{1,0:T(1,128)S(1)} %get-tuple-element.25.step_ref, ...), custom_call_target="tpu_custom_call" | custom-call | tf_op jit(solution)/shard_map/denoise/pallas_call | solution.py:589
  (1 shorter events, 0.0 us)
Async XLA Ops:
  1.6 9.9 %collective-permute-start = (bf16[224,128]{1,0:T(8,128)(2,1)S(1)}, bf16[224,128]{1,0:T(8,128)(2,1)S(1)}, u32[]{:S(2)}, u32[]{:S(2)}) collective-permute-start(bf16[224,128]{1,0:T(8,128)(2,1)S(1)} %get-tuple-element.26), channel_id=1, source_target_pairs={{0,8},{8,16},{16,24},{24,0},{1,9},{9,17},{17,25},{25,1},{2,10},{10... | collective-permute-start | bytes 172040 | tf_op jit(solution)/shard_map/ppermute | solution.py:516
  4.7 6.8 %collective-permute-start.1 = (bf16[224,128]{1,0:T(8,128)(2,1)S(1)}, bf16[224,128]{1,0:T(8,128)(2,1)S(1)}, u32[]{:S(2)}, u32[]{:S(2)}) collective-permute-start(bf16[224,128]{1,0:T(8,128)(2,1)S(1)} %get-tuple-element.27), channel_id=1, source_target_pairs={{0,24},{8,0},{16,8},{24,16},{1,25},{9,1},{17,9},{25,17},{2,26},{10... | collective-permute-start | bytes 172040 | tf_op jit(solution)/shard_map/ppermute | solution.py:516
  6.8 4.7 %collective-permute-start.2 = (bf16[80,128]{1,0:T(8,128)(2,1)S(1)}, bf16[80,128]{1,0:T(8,128)(2,1)S(1)}, u32[]{:S(2)}, u32[]{:S(2)}) collective-permute-start(bf16[80,128]{1,0:T(8,128)(2,1)S(1)} %get-tuple-element.20._.own_ref), channel_id=1, source_target_pairs={{0,16},{8,24},{16,0},{24,8},{1,17},{9,25},{17,1},{25,9},{2,18},{10... | collective-permute-start | bytes 61448 | tf_op jit(solution)/shard_map/ppermute | solution.py:516
  7.8 9.1 %collective-permute-start.5 = (bf16[24,4096]{1,0:T(8,128)(2,1)S(1)}, bf16[24,4096]{1,0:T(8,128)(2,1)S(1)}, u32[]{:S(2)}, u32[]{:S(2)}) collective-permute-start(bf16[24,4096]{1,0:T(8,128)(2,1)S(1)} %gate.1.line_ref), channel_id=1, source_target_pairs={{0,7},{1,2},{2,1},{3,4},{4,3},{5,6},{6,5},{7,0},{8,15},{9,10},{10,... | collective-permute-start | bytes 589832 | tf_op jit(solution)/shard_map/ppermute | solution.py:537
  8.8 8.1 %collective-permute-start.3 = (bf16[24,4096]{1,0:T(8,128)(2,1)S(1)}, bf16[24,4096]{1,0:T(8,128)(2,1)S(1)}, u32[]{:S(2)}, u32[]{:S(2)}) collective-permute-start(bf16[24,4096]{1,0:T(8,128)(2,1)S(1)} %gate.1.line_ref), channel_id=1, source_target_pairs={{0,1},{1,0},{2,3},{3,2},{4,5},{5,4},{6,7},{7,6},{8,9},{9,8},{10,11... | collective-permute-start | bytes 589832 | tf_op jit(solution)/shard_map/ppermute | solution.py:536
  12.0 4.8 %collective-permute-start.6 = (bf16[288,128]{1,0:T(8,128)(2,1)S(1)}, bf16[288,128]{1,0:T(8,128)(2,1)S(1)}, u32[]{:S(2)}, u32[]{:S(2)}) collective-permute-start(bf16[288,128]{1,0:T(8,128)(2,1)S(1)} %get-tuple-element.28._), channel_id=1, source_target_pairs={{0,7},{1,2},{2,1},{3,4},{4,3},{5,6},{6,5},{7,0},{8,15},{9,10},{10,... | collective-permute-start | bytes 221192 | tf_op jit(solution)/shard_map/ppermute | solution.py:561
  12.8 4.1 %collective-permute-start.4 = (bf16[288,128]{1,0:T(8,128)(2,1)S(1)}, bf16[288,128]{1,0:T(8,128)(2,1)S(1)}, u32[]{:S(2)}, u32[]{:S(2)}) collective-permute-start(bf16[288,128]{1,0:T(8,128)(2,1)S(1)} %get-tuple-element.28._), channel_id=1, source_target_pairs={{0,1},{1,0},{2,3},{3,2},{4,5},{5,4},{6,7},{7,6},{8,9},{9,8},{10,11... | collective-permute-start | bytes 221192 | tf_op jit(solution)/shard_map/ppermute | solution.py:560

commit v8 on v7

--- a/solution.py
+++ b/solution.py
@@ -532,7 +532,7 @@
 
     lines = lax.axis_size(("row", "col"))
     pairs = [(i, i ^ 1) for i in range(lines)]
-    others = [(i, (i - 1 + i % 2 * 2) % lines) for i in range(lines)]
+    others = [(i, min(max(i - 1 + i % 2 * 2, 0), lines - 1)) for i in range(lines)]
     raw0 = lax.ppermute(line, ("row", "col"), pairs)
     raw1 = lax.ppermute(line, ("row", "col"), others)
 
@@ -585,7 +585,7 @@
         name="weights",
     )(message, *in_hbm(small))
 
-    tile = 512
+    tile = 256
     result = pl.pallas_call(
         functools.partial(denoise_kernel, tile, reach),
         out_shape=jax.ShapeDtypeStruct((bands, cols), BF16),

time: 21.6 us -> 22.6 us (1.046)
  starting transfers between devices: 9.61 us -> 13.5 us
  waiting for transfers between devices: 3.24 us -> 0.14 us
    ppermute x1, starting transfers between devices: 0.59 us -> 2.94 us  [on_device(): raw0 = lax.ppermute(line, ('row', 'col'), pairs)]
    ppermute x1, starting transfers between devices: 1.08 us -> 3.1 us  [on_device(): message0 = lax.ppermute(message, ('row', 'col'), pairs)]
    ppermute x3, waiting for transfers between devices: 2.1 us -> 0.13 us  [around(): lax.ppermute(x, 'band', [(i, (i + shift) % count) for i in range(count)])]
    ppermute x1, waiting for transfers between devices: 1.13 us -> 0.01 us  [on_device(): message1 = lax.ppermute(message, ('row', 'col'), others)]
    ppermute x1, starting transfers between devices: 1.05 us -> 0.66 us  [on_device(): raw1 = lax.ppermute(line, ('row', 'col'), others)]
  transfers between devices with their start and end apart: 7 -> 7, of which waited for: 2 -> 1; matrix products, arithmetic and copies ran while one was open for 0% -> 0% of each run, Pallas kernels for 11% -> 11%
where the time goes in v8:
time: 22.6 us; the launch traced here: 22.4 us
  starting transfers between devices  13.5 us (60%)
  Pallas kernels  8.71 us (39%)
    ppermute x3, starting transfers between devices, around(): lax.ppermute(x, 'band', [(i, (i + shift) % count) for i in range(count)])  6.11 us
    pallas_call x1, Pallas kernels, on_device(): pl.pallas_call(functools.partial(denoise_kernel, tile, reach), out_shape=...  4.72 us
    ppermute x1, starting transfers between devices, on_device(): message0 = lax.ppermute(message, ('row', 'col'), pairs)  3.1 us
    ppermute x1, starting transfers between devices, on_device(): raw0 = lax.ppermute(line, ('row', 'col'), pairs)  2.94 us
    pallas_call x1, Pallas kernels, on_device(): pl.pallas_call(weights_kernel, out_shape=(jax.ShapeDtypeStruct((16 * ch,...  1.85 us
    pallas_call x1, Pallas kernels, on_device(): pl.pallas_call(functools.partial(project_kernel, reach), out_shape=(jax.S...  1.63 us
    ppermute x1, starting transfers between devices, on_device(): message1 = lax.ppermute(message, ('row', 'col'), others)  0.67 us
    ppermute x1, starting transfers between devices, on_device(): raw1 = lax.ppermute(line, ('row', 'col'), others)  0.66 us
  transfers between devices with their start and end apart: 7, of which 1 were waited for; matrix products, arithmetic and copies ran while one was open for 0% of the time, Pallas kernels for 11%

profile of v8, /device:TPU:0, one launch (start us, length us, event | category | flops | bytes accessed | tf_op | source)
XLA Modules:
  0.0 22.4 jit_solution(11721118742650709903)
XLA Ops:
  0.0 1.6 %project.1 = (bf16[80,128]{1,0:T(8,128)(2,1)S(1)}, bf16[224,128]{1,0:T(8,128)(2,1)S(1)}, bf16[224,128]{1,0:T(8,128)(2,1)S(1)}, bf16[24,4096]{1,0:T(8,128)(2,1)S(...) custom-call(bf16[22,4096]{1,0:T(8,128)(2,1)} %bitcast.7, ...), custom_call_target="tpu_custom_call" | custom-call | tf_op jit(solution)/shard_map/project/pallas_call | solution.py:495
  1.6 3.1 %collective-permute-start = (bf16[224,128]{1,0:T(8,128)(2,1)S(1)}, bf16[224,128]{1,0:T(8,128)(2,1)S(1)}, u32[]{:S(2)}, u32[]{:S(2)}) collective-permute-start(bf16[224,128]{1,0:T(8,128)(2,1)S(1)} %get-tuple-element.26), channel_id=1, source_target_pairs={{0,8},{8,16},{16,24},{24,0},{1,9},{9,17},{17,25},{25,1},{2,10},{10... | collective-permute-start | bytes 172040 | tf_op jit(solution)/shard_map/ppermute | solution.py:516
  4.7 2.1 %collective-permute-start.1 = (bf16[224,128]{1,0:T(8,128)(2,1)S(1)}, bf16[224,128]{1,0:T(8,128)(2,1)S(1)}, u32[]{:S(2)}, u32[]{:S(2)}) collective-permute-start(bf16[224,128]{1,0:T(8,128)(2,1)S(1)} %get-tuple-element.27), channel_id=1, source_target_pairs={{0,24},{8,0},{16,8},{24,16},{1,25},{9,1},{17,9},{25,17},{2,26},{10... | collective-permute-start | bytes 172040 | tf_op jit(solution)/shard_map/ppermute | solution.py:516
  6.8 0.9 %collective-permute-start.2 = (bf16[80,128]{1,0:T(8,128)(2,1)S(1)}, bf16[80,128]{1,0:T(8,128)(2,1)S(1)}, u32[]{:S(2)}, u32[]{:S(2)}) collective-permute-start(bf16[80,128]{1,0:T(8,128)(2,1)S(1)} %get-tuple-element.20._.own_ref), channel_id=1, source_target_pairs={{0,16},{8,24},{16,0},{24,8},{1,17},{9,25},{17,1},{25,9},{2,18},{10... | collective-permute-start | bytes 61448 | tf_op jit(solution)/shard_map/ppermute | solution.py:516
  7.8 0.7 %collective-permute-start.5 = (bf16[24,4096]{1,0:T(8,128)(2,1)S(1)}, bf16[24,4096]{1,0:T(8,128)(2,1)S(1)}, u32[]{:S(2)}, u32[]{:S(2)}) collective-permute-start(bf16[24,4096]{1,0:T(8,128)(2,1)S(1)} %gate.1.line_ref), channel_id=1, source_target_pairs={{0,0},{1,2},{2,1},{3,4},{4,3},{5,6},{6,5},{7,7},{8,8},{9,10},{10,9... | collective-permute-start | bytes 589832 | tf_op jit(solution)/shard_map/ppermute | solution.py:537
  8.4 2.9 %collective-permute-start.3 = (bf16[24,4096]{1,0:T(8,128)(2,1)S(1)}, bf16[24,4096]{1,0:T(8,128)(2,1)S(1)}, u32[]{:S(2)}, u32[]{:S(2)}) collective-permute-start(bf16[24,4096]{1,0:T(8,128)(2,1)S(1)} %gate.1.line_ref), channel_id=1, source_target_pairs={{0,1},{1,0},{2,3},{3,2},{4,5},{5,4},{6,7},{7,6},{8,9},{9,8},{10,11... | collective-permute-start | bytes 589832 | tf_op jit(solution)/shard_map/ppermute | solution.py:536
  11.4 0.1 collective-permute-done.2.rest_refs_0_
  11.5 0.0 collective-permute-done.below_ref
  11.5 0.0 collective-permute-done.1.above_ref
  11.5 0.5 %update.1 = (bf16[32,4096]{1,0:T(8,128)(2,1)S(1)}, bf16[288,128]{1,0:T(8,128)(2,1)S(1)}) custom-call(bf16[24,4096]{1,0:T(8,128)(2,1)S(1)} %gate.1.line_ref, s32[1,4096]{1,0:T(1,128)S(1)} %get-tuple-element.22.ap_ref, f32[1,4444]{1,0:T(1,128)S(1)} %get-tuple-element.23.meas_ref, s32[1,22]{1,0:T(1,128)S(1)} %get-tuple-element.24.shear_ref, ...), custom_call_target="tpu_custom_call" | custom-call | flops 10000000000 | bytes 40000000 | tf_op jit(solution)/shard_map/update/pallas_call | solution.py:540
  12.0 0.7 %collective-permute-start.6 = (bf16[288,128]{1,0:T(8,128)(2,1)S(1)}, bf16[288,128]{1,0:T(8,128)(2,1)S(1)}, u32[]{:S(2)}, u32[]{:S(2)}) collective-permute-start(bf16[288,128]{1,0:T(8,128)(2,1)S(1)} %get-tuple-element.28._), channel_id=1, source_target_pairs={{0,0},{1,2},{2,1},{3,4},{4,3},{5,6},{6,5},{7,7},{8,8},{9,10},{10,9... | collective-permute-start | bytes 221192 | tf_op jit(solution)/shard_map/ppermute | solution.py:561
  12.7 3.1 %collective-permute-start.4 = (bf16[288,128]{1,0:T(8,128)(2,1)S(1)}, bf16[288,128]{1,0:T(8,128)(2,1)S(1)}, u32[]{:S(2)}, u32[]{:S(2)}) collective-permute-start(bf16[288,128]{1,0:T(8,128)(2,1)S(1)} %get-tuple-element.28._), channel_id=1, source_target_pairs={{0,1},{1,0},{2,3},{3,2},{4,5},{5,4},{6,7},{7,6},{8,9},{9,8},{10,11... | collective-permute-start | bytes 221192 | tf_op jit(solution)/shard_map/ppermute | solution.py:560
  15.8 1.9 %weights.1 = (bf16[256,160]{1,0:T(8,128)(2,1)S(1)}, bf16[192,160]{1,0:T(8,128)(2,1)S(1)}, bf16[256,240]{1,0:T(8,128)(2,1)S(1)}, bf16[256,240]{1,0:T(8,128)(2,1)S(1)}, f32[128,128]{1,0:T(8,128)S(1)}) custom-call(bf16[288,128]{1,0:T(8,128)(2,1)S(1)} %get-tuple-element.28._, bf16[16,9]{1,0:T(8,128)(2,1)} %sw_in.1, f32[1,16]{1,0:T(1,128)} %bitcast.10, ...), custom_call_target="tpu_custom_call" | custom-call | tf_op jit(solution)/shard_map/weights/pallas_call | solution.py:571
  17.6 0.0 collective-permute-done.6.msg1_ref
  17.7 0.0 collective-permute-done.4.msg0_ref
  17.7 0.0 collective-permute-done.5.raw1_ref
  17.7 0.0 collective-permute-done.3.raw0_ref
  17.7 4.7 %denoise.1 = bf16[22,4096]{1,0:T(8,128)(2,1)} custom-call(f32[128,128]{1,0:T(8,128)S(1)} %get-tuple-element.29.ow_ref, bf16[32,4096]{1,0:T(8,128)(2,1)S(1)} %get-tuple-element.30.mid_ref, s32[1,22]{1,0:T(1,128)S(1)} %get-tuple-element.24.shear_ref, f32[1,22]{1,0:T(1,128)S(1)} %get-tuple-element.25.step_ref, ...), custom_call_target="tpu_custom_call" | custom-call | tf_op jit(solution)/shard_map/denoise/pallas_call | solution.py:589
  (1 shorter events, 0.0 us)
Async XLA Ops:
  1.6 9.9 %collective-permute-start = (bf16[224,128]{1,0:T(8,128)(2,1)S(1)}, bf16[224,128]{1,0:T(8,128)(2,1)S(1)}, u32[]{:S(2)}, u32[]{:S(2)}) collective-permute-start(bf16[224,128]{1,0:T(8,128)(2,1)S(1)} %get-tuple-element.26), channel_id=1, source_target_pairs={{0,8},{8,16},{16,24},{24,0},{1,9},{9,17},{17,25},{25,1},{2,10},{10... | collective-permute-start | bytes 172040 | tf_op jit(solution)/shard_map/ppermute | solution.py:516
  4.7 6.8 %collective-permute-start.1 = (bf16[224,128]{1,0:T(8,128)(2,1)S(1)}, bf16[224,128]{1,0:T(8,128)(2,1)S(1)}, u32[]{:S(2)}, u32[]{:S(2)}) collective-permute-start(bf16[224,128]{1,0:T(8,128)(2,1)S(1)} %get-tuple-element.27), channel_id=1, source_target_pairs={{0,24},{8,0},{16,8},{24,16},{1,25},{9,1},{17,9},{25,17},{2,26},{10... | collective-permute-start | bytes 172040 | tf_op jit(solution)/shard_map/ppermute | solution.py:516
  6.8 4.7 %collective-permute-start.2 = (bf16[80,128]{1,0:T(8,128)(2,1)S(1)}, bf16[80,128]{1,0:T(8,128)(2,1)S(1)}, u32[]{:S(2)}, u32[]{:S(2)}) collective-permute-start(bf16[80,128]{1,0:T(8,128)(2,1)S(1)} %get-tuple-element.20._.own_ref), channel_id=1, source_target_pairs={{0,16},{8,24},{16,0},{24,8},{1,17},{9,25},{17,1},{25,9},{2,18},{10... | collective-permute-start | bytes 61448 | tf_op jit(solution)/shard_map/ppermute | solution.py:516
  7.8 9.9 %collective-permute-start.5 = (bf16[24,4096]{1,0:T(8,128)(2,1)S(1)}, bf16[24,4096]{1,0:T(8,128)(2,1)S(1)}, u32[]{:S(2)}, u32[]{:S(2)}) collective-permute-start(bf16[24,4096]{1,0:T(8,128)(2,1)S(1)} %gate.1.line_ref), channel_id=1, source_target_pairs={{0,0},{1,2},{2,1},{3,4},{4,3},{5,6},{6,5},{7,7},{8,8},{9,10},{10,9... | collective-permute-start | bytes 589832 | tf_op jit(solution)/shard_map/ppermute | solution.py:537
  8.4 9.3 %collective-permute-start.3 = (bf16[24,4096]{1,0:T(8,128)(2,1)S(1)}, bf16[24,4096]{1,0:T(8,128)(2,1)S(1)}, u32[]{:S(2)}, u32[]{:S(2)}) collective-permute-start(bf16[24,4096]{1,0:T(8,128)(2,1)S(1)} %gate.1.line_ref), channel_id=1, source_target_pairs={{0,1},{1,0},{2,3},{3,2},{4,5},{5,4},{6,7},{7,6},{8,9},{9,8},{10,11... | collective-permute-start | bytes 589832 | tf_op jit(solution)/shard_map/ppermute | solution.py:536
  12.0 5.6 %collective-permute-start.6 = (bf16[288,128]{1,0:T(8,128)(2,1)S(1)}, bf16[288,128]{1,0:T(8,128)(2,1)S(1)}, u32[]{:S(2)}, u32[]{:S(2)}) collective-permute-start(bf16[288,128]{1,0:T(8,128)(2,1)S(1)} %get-tuple-element.28._), channel_id=1, source_target_pairs={{0,0},{1,2},{2,1},{3,4},{4,3},{5,6},{6,5},{7,7},{8,8},{9,10},{10,9... | collective-permute-start | bytes 221192 | tf_op jit(solution)/shard_map/ppermute | solution.py:561
  12.7 5.0 %collective-permute-start.4 = (bf16[288,128]{1,0:T(8,128)(2,1)S(1)}, bf16[288,128]{1,0:T(8,128)(2,1)S(1)}, u32[]{:S(2)}, u32[]{:S(2)}) collective-permute-start(bf16[288,128]{1,0:T(8,128)(2,1)S(1)} %get-tuple-element.28._), channel_id=1, source_target_pairs={{0,1},{1,0},{2,3},{3,2},{4,5},{5,4},{6,7},{7,6},{8,9},{9,8},{10,11... | collective-permute-start | bytes 221192 | tf_op jit(solution)/shard_map/ppermute | solution.py:560

commit v9 on v7

--- a/solution.py
+++ b/solution.py
@@ -301,17 +301,17 @@
     picks = spread(rows, ch, which)
     lane = lanes_of((rows, width))
     ahead = jnp.where(lane < used, lane // ch - rows_of((rows, width)) % per, -LANES)
-    shifts = (0, per, per - (per + taps - 1), 2 * per - (per + taps - 1))
-    blocks = [jnp.zeros((rows, width), F32) for _ in shifts]
+    matrix = jnp.zeros((rows, width), F32)
     for d in range(taps):
         flat = jnp.dot(cw_ref[d], fan, preferred_element_type=F32).astype(BF16)
         full = 0.5 * jnp.dot(picks, flat, preferred_element_type=F32)
-        blocks = [jnp.where(ahead == d + s, full, b) for s, b in zip(shifts, blocks)]
+        matrix = jnp.where(ahead == d, full, matrix)
     bias = picked(cb_ref, rows, which)
-    for i, block in enumerate(blocks):
-        block = block if i == 2 else with_bias(block, bias, used)
-        ref = first_ref if i < 2 else second_ref
-        ref[i % 2 * rows : (i % 2 + 1) * rows, :] = block.astype(BF16)
+    first_ref[...] = with_bias(matrix, bias, used).astype(BF16)
+    short = second_ref.shape[1]
+    start = short - 16
+    matrix = jnp.where(lanes_of((rows, short)) < start, matrix[:, 0:short], 0.0)
+    second_ref[...] = with_bias(matrix, bias, start).astype(BF16)
     out_w_ref[...] = jnp.broadcast_to(picked(ow_ref, rows, which), out_w_ref.shape)
 
 
@@ -342,7 +342,6 @@
     tiles = cols // tile
     inner = cols // LANES
     wide = tile + 2 * LANES
-    split = act.shape[1] // 2
     groups = -(-bands // SUB)
     ones = jnp.where(rows_of((slots, tile)) < 3, 1.0, 0.0).astype(BF16)
     blank = jnp.zeros((2 * slots, LANES), BF16)
@@ -418,12 +417,12 @@
     def spectral(t):
         start = t * tile
         buf = act.at[t % act.shape[0]]
-        halves = []
-        for part, w_ref in enumerate((first_ref, second_ref)):
-            x = jnp.concatenate([buf[part * split : (part + 1) * split, :], ones], axis=0)
-            halves.append(jnp.dot(w_ref[...], x, preferred_element_type=F32))
-        rows = SUB * ch
-        blocks = [halves[0][0:rows], halves[0][rows:] + halves[1][0:rows], halves[1][rows:]]
+        blocks = []
+        for i in range(groups):
+            w_ref = second_ref if i == groups - 1 else first_ref
+            first = i * SUB * ch
+            x = jnp.concatenate([buf[first : first + w_ref.shape[1] - slots, :], ones], axis=0)
+            blocks.append(jnp.dot(w_ref[...], x, preferred_element_type=F32))
         pieces = []
         for half in blocks:
             total = None
@@ -568,13 +567,14 @@
         out_weight.reshape(1, ch),
     )
     reached = (SUB + taps - 1) * ch
+    last = (bands - (groups - 1) * SUB + taps - 1) * ch
     main_w, halo_w, first_w, second_w, out_w = pl.pallas_call(
         weights_kernel,
         out_shape=(
             jax.ShapeDtypeStruct((16 * ch, taps2 * 16 + 16), BF16),
             jax.ShapeDtypeStruct((12 * ch, taps2 * 16 + 16), BF16),
-            jax.ShapeDtypeStruct((2 * SUB * ch, reached + 16), BF16),
-            jax.ShapeDtypeStruct((2 * SUB * ch, reached + 16), BF16),
+            jax.ShapeDtypeStruct((SUB * ch, reached + 16), BF16),
+            jax.ShapeDtypeStruct((SUB * ch, last + 16), BF16),
             jax.ShapeDtypeStruct((SUB * ch, LANES), F32),
         ),
         in_specs=[ANY] + hbm(5),

time: 21.6 us -> 21.5 us (level)
  no operation moved by 1% of the time
where the time goes in v9:
time: 21.5 us; the launch traced here: 21.3 us
  starting transfers between devices  9.61 us (45%)
  Pallas kernels  8.37 us (39%)
  waiting for transfers between devices  3.3 us (15%)
    ppermute x3, starting transfers between devices, around(): lax.ppermute(x, 'band', [(i, (i + shift) % count) for i in range(count)])  6.11 us
    pallas_call x1, Pallas kernels, on_device(): pl.pallas_call(functools.partial(denoise_kernel, tile, reach), out_shape=...  4.44 us
    ppermute x3, waiting for transfers between devices, around(): lax.ppermute(x, 'band', [(i, (i + shift) % count) for i in range(count)])  2.1 us
    pallas_call x1, Pallas kernels, on_device(): pl.pallas_call(weights_kernel, out_shape=(jax.ShapeDtypeStruct((16 * ch,...  1.79 us
    pallas_call x1, Pallas kernels, on_device(): pl.pallas_call(functools.partial(project_kernel, reach), out_shape=(jax.S...  1.63 us
    ppermute x1, waiting for transfers between devices, on_device(): message1 = lax.ppermute(message, ('row', 'col'), others)  1.19 us
    ppermute x1, starting transfers between devices, on_device(): message0 = lax.ppermute(message, ('row', 'col'), pairs)  1.08 us
    ppermute x1, starting transfers between devices, on_device(): raw1 = lax.ppermute(line, ('row', 'col'), others)  1.05 us
  transfers between devices with their start and end apart: 7, of which 2 were waited for; matrix products, arithmetic and copies ran while one was open for 0% of the time, Pallas kernels for 11%

profile of v9, /device:TPU:0, one launch (start us, length us, event | category | flops | bytes accessed | tf_op | source)
XLA Modules:
  0.0 21.3 jit_solution(7625722368287269202)
XLA Ops:
  0.0 1.6 %project.1 = (bf16[80,128]{1,0:T(8,128)(2,1)S(1)}, bf16[224,128]{1,0:T(8,128)(2,1)S(1)}, bf16[224,128]{1,0:T(8,128)(2,1)S(1)}, bf16[24,4096]{1,0:T(8,128)(2,1)S(...) custom-call(bf16[22,4096]{1,0:T(8,128)(2,1)} %bitcast.7, ...), custom_call_target="tpu_custom_call" | custom-call | tf_op jit(solution)/shard_map/project/pallas_call | solution.py:494
  1.6 3.1 %collective-permute-start = (bf16[224,128]{1,0:T(8,128)(2,1)S(1)}, bf16[224,128]{1,0:T(8,128)(2,1)S(1)}, u32[]{:S(2)}, u32[]{:S(2)}) collective-permute-start(bf16[224,128]{1,0:T(8,128)(2,1)S(1)} %get-tuple-element.26), channel_id=1, source_target_pairs={{0,8},{8,16},{16,24},{24,0},{1,9},{9,17},{17,25},{25,1},{2,10},{10... | collective-permute-start | bytes 172040 | tf_op jit(solution)/shard_map/ppermute | solution.py:515
  4.7 2.1 %collective-permute-start.1 = (bf16[224,128]{1,0:T(8,128)(2,1)S(1)}, bf16[224,128]{1,0:T(8,128)(2,1)S(1)}, u32[]{:S(2)}, u32[]{:S(2)}) collective-permute-start(bf16[224,128]{1,0:T(8,128)(2,1)S(1)} %get-tuple-element.27), channel_id=1, source_target_pairs={{0,24},{8,0},{16,8},{24,16},{1,25},{9,1},{17,9},{25,17},{2,26},{10... | collective-permute-start | bytes 172040 | tf_op jit(solution)/shard_map/ppermute | solution.py:515
  6.8 0.9 %collective-permute-start.2 = (bf16[80,128]{1,0:T(8,128)(2,1)S(1)}, bf16[80,128]{1,0:T(8,128)(2,1)S(1)}, u32[]{:S(2)}, u32[]{:S(2)}) collective-permute-start(bf16[80,128]{1,0:T(8,128)(2,1)S(1)} %get-tuple-element.20._.own_ref), channel_id=1, source_target_pairs={{0,16},{8,24},{16,0},{24,8},{1,17},{9,25},{17,1},{25,9},{2,18},{10... | collective-permute-start | bytes 61448 | tf_op jit(solution)/shard_map/ppermute | solution.py:515
  7.8 1.0 %collective-permute-start.5 = (bf16[24,4096]{1,0:T(8,128)(2,1)S(1)}, bf16[24,4096]{1,0:T(8,128)(2,1)S(1)}, u32[]{:S(2)}, u32[]{:S(2)}) collective-permute-start(bf16[24,4096]{1,0:T(8,128)(2,1)S(1)} %gate.1.line_ref), channel_id=1, source_target_pairs={{0,7},{1,2},{2,1},{3,4},{4,3},{5,6},{6,5},{7,0},{8,15},{9,10},{10,... | collective-permute-start | bytes 589832 | tf_op jit(solution)/shard_map/ppermute | solution.py:536
  8.8 0.6 %collective-permute-start.3 = (bf16[24,4096]{1,0:T(8,128)(2,1)S(1)}, bf16[24,4096]{1,0:T(8,128)(2,1)S(1)}, u32[]{:S(2)}, u32[]{:S(2)}) collective-permute-start(bf16[24,4096]{1,0:T(8,128)(2,1)S(1)} %gate.1.line_ref), channel_id=1, source_target_pairs={{0,1},{1,0},{2,3},{3,2},{4,5},{5,4},{6,7},{7,6},{8,9},{9,8},{10,11... | collective-permute-start | bytes 589832 | tf_op jit(solution)/shard_map/ppermute | solution.py:535
  9.4 2.1 %collective-permute-done.2.rest_refs_0_ = bf16[80,128]{1,0:T(8,128)(2,1)S(1)} collective-permute-done((bf16[80,128]{1,0:T(8,128)(2,1)S(1)}, bf16[80,128]{1,0:T(8,128)(2,1)S(1)}, u32[]{:S(2)}, u32[]{:S(2)}) %collective-permute-start.2) | collective-permute-done | bytes 20512 | tf_op jit(solution)/shard_map/ppermute | solution.py:515
  11.5 0.0 collective-permute-done.below_ref
  11.5 0.0 collective-permute-done.1.above_ref
  11.5 0.5 %update.1 = (bf16[32,4096]{1,0:T(8,128)(2,1)S(1)}, bf16[288,128]{1,0:T(8,128)(2,1)S(1)}) custom-call(bf16[24,4096]{1,0:T(8,128)(2,1)S(1)} %gate.1.line_ref, s32[1,4096]{1,0:T(1,128)S(1)} %get-tuple-element.22.ap_ref, f32[1,4444]{1,0:T(1,128)S(1)} %get-tuple-element.23.meas_ref, s32[1,22]{1,0:T(1,128)S(1)} %get-tuple-element.24.shear_ref, ...), custom_call_target="tpu_custom_call" | custom-call | flops 10000000000 | bytes 40000000 | tf_op jit(solution)/shard_map/update/pallas_call | solution.py:539
  12.0 0.8 %collective-permute-start.6 = (bf16[288,128]{1,0:T(8,128)(2,1)S(1)}, bf16[288,128]{1,0:T(8,128)(2,1)S(1)}, u32[]{:S(2)}, u32[]{:S(2)}) collective-permute-start(bf16[288,128]{1,0:T(8,128)(2,1)S(1)} %get-tuple-element.28._), channel_id=1, source_target_pairs={{0,7},{1,2},{2,1},{3,4},{4,3},{5,6},{6,5},{7,0},{8,15},{9,10},{10,... | collective-permute-start | bytes 221192 | tf_op jit(solution)/shard_map/ppermute | solution.py:560
  12.8 1.1 %collective-permute-start.4 = (bf16[288,128]{1,0:T(8,128)(2,1)S(1)}, bf16[288,128]{1,0:T(8,128)(2,1)S(1)}, u32[]{:S(2)}, u32[]{:S(2)}) collective-permute-start(bf16[288,128]{1,0:T(8,128)(2,1)S(1)} %get-tuple-element.28._), channel_id=1, source_target_pairs={{0,1},{1,0},{2,3},{3,2},{4,5},{5,4},{6,7},{7,6},{8,9},{9,8},{10,11... | collective-permute-start | bytes 221192 | tf_op jit(solution)/shard_map/ppermute | solution.py:559
  13.9 1.8 %weights.1 = (bf16[256,160]{1,0:T(8,128)(2,1)S(1)}, bf16[192,160]{1,0:T(8,128)(2,1)S(1)}, bf16[128,240]{1,0:T(8,128)(2,1)S(1)}, bf16[128,208]{1,0:T(8,128)(2,1)S(1)}, f32[128,128]{1,0:T(8,128)S(1)}) custom-call(bf16[288,128]{1,0:T(8,128)(2,1)S(1)} %get-tuple-element.28._, bf16[16,9]{1,0:T(8,128)(2,1)} %sw_in.1, f32[1,16]{1,0:T(1,128)} %bitcast.10, ...), custom_call_target="tpu_custom_call" | custom-call | tf_op jit(solution)/shard_map/weights/pallas_call | solution.py:571
  15.7 1.2 %collective-permute-done.6.msg1_ref = bf16[288,128]{1,0:T(8,128)(2,1)S(1)} collective-permute-done((bf16[288,128]{1,0:T(8,128)(2,1)S(1)}, bf16[288,128]{1,0:T(8,128)(2,1)S(1)}, u32[]{:S(2)}, u32[]{:S(2)}) %collective-permute-start.6) | collective-permute-done | bytes 73760 | tf_op jit(solution)/shard_map/ppermute | solution.py:560
  16.9 0.0 collective-permute-done.4.msg0_ref
  16.9 0.0 collective-permute-done.5.raw1_ref
  16.9 0.0 collective-permute-done.3.raw0_ref
  16.9 4.4 %denoise.1 = bf16[22,4096]{1,0:T(8,128)(2,1)} custom-call(f32[128,128]{1,0:T(8,128)S(1)} %get-tuple-element.29.ow_ref, bf16[32,4096]{1,0:T(8,128)(2,1)S(1)} %get-tuple-element.30.mid_ref, s32[1,22]{1,0:T(1,128)S(1)} %get-tuple-element.24.shear_ref, f32[1,22]{1,0:T(1,128)S(1)} %get-tuple-element.25.step_ref, ...), custom_call_target="tpu_custom_call" | custom-call | tf_op jit(solution)/shard_map/denoise/pallas_call | solution.py:589
  (1 shorter events, 0.0 us)
Async XLA Ops:
  1.6 9.9 %collective-permute-start = (bf16[224,128]{1,0:T(8,128)(2,1)S(1)}, bf16[224,128]{1,0:T(8,128)(2,1)S(1)}, u32[]{:S(2)}, u32[]{:S(2)}) collective-permute-start(bf16[224,128]{1,0:T(8,128)(2,1)S(1)} %get-tuple-element.26), channel_id=1, source_target_pairs={{0,8},{8,16},{16,24},{24,0},{1,9},{9,17},{17,25},{25,1},{2,10},{10... | collective-permute-start | bytes 172040 | tf_op jit(solution)/shard_map/ppermute | solution.py:515
  4.7 6.8 %collective-permute-start.1 = (bf16[224,128]{1,0:T(8,128)(2,1)S(1)}, bf16[224,128]{1,0:T(8,128)(2,1)S(1)}, u32[]{:S(2)}, u32[]{:S(2)}) collective-permute-start(bf16[224,128]{1,0:T(8,128)(2,1)S(1)} %get-tuple-element.27), channel_id=1, source_target_pairs={{0,24},{8,0},{16,8},{24,16},{1,25},{9,1},{17,9},{25,17},{2,26},{10... | collective-permute-start | bytes 172040 | tf_op jit(solution)/shard_map/ppermute | solution.py:515
  6.8 4.7 %collective-permute-start.2 = (bf16[80,128]{1,0:T(8,128)(2,1)S(1)}, bf16[80,128]{1,0:T(8,128)(2,1)S(1)}, u32[]{:S(2)}, u32[]{:S(2)}) collective-permute-start(bf16[80,128]{1,0:T(8,128)(2,1)S(1)} %get-tuple-element.20._.own_ref), channel_id=1, source_target_pairs={{0,16},{8,24},{16,0},{24,8},{1,17},{9,25},{17,1},{25,9},{2,18},{10... | collective-permute-start | bytes 61448 | tf_op jit(solution)/shard_map/ppermute | solution.py:515
  7.8 9.1 %collective-permute-start.5 = (bf16[24,4096]{1,0:T(8,128)(2,1)S(1)}, bf16[24,4096]{1,0:T(8,128)(2,1)S(1)}, u32[]{:S(2)}, u32[]{:S(2)}) collective-permute-start(bf16[24,4096]{1,0:T(8,128)(2,1)S(1)} %gate.1.line_ref), channel_id=1, source_target_pairs={{0,7},{1,2},{2,1},{3,4},{4,3},{5,6},{6,5},{7,0},{8,15},{9,10},{10,... | collective-permute-start | bytes 589832 | tf_op jit(solution)/shard_map/ppermute | solution.py:536
  8.8 8.1 %collective-permute-start.3 = (bf16[24,4096]{1,0:T(8,128)(2,1)S(1)}, bf16[24,4096]{1,0:T(8,128)(2,1)S(1)}, u32[]{:S(2)}, u32[]{:S(2)}) collective-permute-start(bf16[24,4096]{1,0:T(8,128)(2,1)S(1)} %gate.1.line_ref), channel_id=1, source_target_pairs={{0,1},{1,0},{2,3},{3,2},{4,5},{5,4},{6,7},{7,6},{8,9},{9,8},{10,11... | collective-permute-start | bytes 589832 | tf_op jit(solution)/shard_map/ppermute | solution.py:535
  12.0 4.8 %collective-permute-start.6 = (bf16[288,128]{1,0:T(8,128)(2,1)S(1)}, bf16[288,128]{1,0:T(8,128)(2,1)S(1)}, u32[]{:S(2)}, u32[]{:S(2)}) collective-permute-start(bf16[288,128]{1,0:T(8,128)(2,1)S(1)} %get-tuple-element.28._), channel_id=1, source_target_pairs={{0,7},{1,2},{2,1},{3,4},{4,3},{5,6},{6,5},{7,0},{8,15},{9,10},{10,... | collective-permute-start | bytes 221192 | tf_op jit(solution)/shard_map/ppermute | solution.py:560
  12.8 4.1 %collective-permute-start.4 = (bf16[288,128]{1,0:T(8,128)(2,1)S(1)}, bf16[288,128]{1,0:T(8,128)(2,1)S(1)}, u32[]{:S(2)}, u32[]{:S(2)}) collective-permute-start(bf16[288,128]{1,0:T(8,128)(2,1)S(1)} %get-tuple-element.28._), channel_id=1, source_target_pairs={{0,1},{1,0},{2,3},{3,2},{4,5},{5,4},{6,7},{7,6},{8,9},{9,8},{10,11... | collective-permute-start | bytes 221192 | tf_op jit(solution)/shard_map/ppermute | solution.py:559

commit v10 on v9

--- a/solution.py
+++ b/solution.py
@@ -389,10 +389,19 @@
     def silu_twice(half):
         return half + half * jnp.tanh(half)
 
-    def spatial(t):
+    inputs, halves, blocks, sums = {}, {}, {}, {}
+    made = 0
+
+    def update_up_to(t):
+        nonlocal made
+        while made < min((t + 1) * tile // LANES + 1, inner):
+            neighbours(made)
+            made += 1
+
+    def patches(t):
         start = t * tile
         end = start + tile
-        patches = []
+        parts = []
         for ref in (near0, mid_ref, near1):
             left = ref[:, start - LANES : start] if t else blank
             here = ref[:, start:end]
@@ -400,51 +409,76 @@
             row = jnp.concatenate([left, here, right], axis=1)
             back = pltpu.roll(row, 1, 1)[:, LANES : LANES + tile]
             ahead = pltpu.roll(row, wide - 1, 1)[:, LANES : LANES + tile]
-            patches += [back, here, ahead]
+            parts += [back, here, ahead]
+        for part in range(2):
+            inputs[t, part] = jnp.concatenate(
+                [p[part * slots : (part + 1) * slots] for p in parts] + [ones], axis=0
+            )
+
+    def spatial(t, part):
+        w_ref = halo_ref if part else main_ref
+        halves[t, part] = jnp.dot(
+            w_ref[...], inputs.pop((t, part)), preferred_element_type=F32
+        )
+
+    def activate(t, part):
         buf = act.at[t % act.shape[0]]
-        for part, w_ref in enumerate((main_ref, halo_ref)):
-            x = jnp.concatenate(
-                [p[part * slots : (part + 1) * slots] for p in patches] + [ones], axis=0
-            )
-            half = jnp.dot(w_ref[...], x, preferred_element_type=F32)
-            value = silu_twice(half).astype(BF16)
-            if part == 0:
-                buf[3 * ch : 19 * ch, :] = value
-            else:
-                buf[0 : 3 * ch, :] = value[0 : 3 * ch]
-                buf[19 * ch : 28 * ch, :] = value[3 * ch :]
-
-    def spectral(t):
-        start = t * tile
+        value = silu_twice(halves.pop((t, part))).astype(BF16)
+        if part == 0:
+            buf[3 * ch : 19 * ch, :] = value
+        else:
+            buf[0 : 3 * ch, :] = value[0 : 3 * ch]
+            buf[19 * ch : 28 * ch, :] = value[3 * ch :]
+
+    def spectral(t, i):
         buf = act.at[t % act.shape[0]]
-        blocks = []
-        for i in range(groups):
-            w_ref = second_ref if i == groups - 1 else first_ref
-            first = i * SUB * ch
-            x = jnp.concatenate([buf[first : first + w_ref.shape[1] - slots, :], ones], axis=0)
-            blocks.append(jnp.dot(w_ref[...], x, preferred_element_type=F32))
-        pieces = []
-        for half in blocks:
-            total = None
-            for k in range(ch):
-                weight = ow_ref[k * SUB : (k + 1) * SUB, :]
-                weight = jnp.concatenate([weight] * (tile // LANES), axis=1)
-                term = weight * silu_twice(half[k * SUB : (k + 1) * SUB])
-                total = term if total is None else total + term
-            pieces.append(total)
-        update = jnp.concatenate(pieces, axis=0)[0:bands]
-        center = mid_ref[:, start : start + tile].astype(F32)[0:bands]
-        out_ref[:, start : start + tile] = (center + update).astype(BF16)
-
-    made = 0
-    for t in range(tiles + 1):
-        while t < tiles and made < min((t + 1) * tile // LANES + 1, inner):
-            neighbours(made)
-            made += 1
-        if t < tiles:
-            spatial(t)
+        w_ref = second_ref if i == groups - 1 else first_ref
+        first = i * SUB * ch
+        x = jnp.concatenate([buf[first : first + w_ref.shape[1] - slots, :], ones], axis=0)
+        blocks[t, i] = jnp.dot(w_ref[...], x, preferred_element_type=F32)
+
+    def project(t, i):
+        half = blocks.pop((t, i))
+        total = None
+        for k in range(ch):
+            weight = ow_ref[k * SUB : (k + 1) * SUB, :]
+            weight = jnp.concatenate([weight] * (tile // LANES), axis=1)
+            term = weight * silu_twice(half[k * SUB : (k + 1) * SUB])
+            total = term if total is None else total + term
+        sums[t, i] = total
+        if i == groups - 1:
+            start = t * tile
+            update = jnp.concatenate([sums.pop((t, n)) for n in range(groups)], axis=0)[0:bands]
+            center = mid_ref[:, start : start + tile].astype(F32)[0:bands]
+            out_ref[:, start : start + tile] = (center + update).astype(BF16)
+
+    update_up_to(0)
+    patches(0)
+    spatial(0, 0)
+    spatial(0, 1)
+    update_up_to(1)
+    activate(0, 0)
+    patches(1)
+    activate(0, 1)
+    for t in range(tiles):
+        if t + 1 < tiles:
+            spatial(t + 1, 0)
         if t:
-            spectral(t - 1)
+            project(t - 1, groups - 1)
+        if t + 2 < tiles:
+            update_up_to(t + 2)
+        if t + 1 < tiles:
+            spatial(t + 1, 1)
+            activate(t + 1, 0)
+        spectral(t, 0)
+        if t + 1 < tiles:
+            activate(t + 1, 1)
+        for i in range(1, groups):
+            spectral(t, i)
+            project(t, i - 1)
+        if t + 2 < tiles:
+            patches(t + 2)
+    project(tiles - 1, groups - 1)
 
 
 def vmem(n):

time: 21.5 us -> 21.5 us (level)
  no operation moved by 1% of the time
where the time goes in v10:
time: 21.5 us; the launch traced here: 21.3 us
  starting transfers between devices  9.61 us (45%)
  Pallas kernels  8.35 us (39%)
  waiting for transfers between devices  3.3 us (15%)
    ppermute x3, starting transfers between devices, around(): lax.ppermute(x, 'band', [(i, (i + shift) % count) for i in range(count)])  6.11 us
    pallas_call x1, Pallas kernels, on_device(): pl.pallas_call(functools.partial(denoise_kernel, tile, reach), out_shape=...  4.42 us
    ppermute x3, waiting for transfers between devices, around(): lax.ppermute(x, 'band', [(i, (i + shift) % count) for i in range(count)])  2.1 us
    pallas_call x1, Pallas kernels, on_device(): pl.pallas_call(weights_kernel, out_shape=(jax.ShapeDtypeStruct((16 * ch,...  1.79 us
    pallas_call x1, Pallas kernels, on_device(): pl.pallas_call(functools.partial(project_kernel, reach), out_shape=(jax.S...  1.63 us
    ppermute x1, waiting for transfers between devices, on_device(): message1 = lax.ppermute(message, ('row', 'col'), others)  1.19 us
    ppermute x1, starting transfers between devices, on_device(): message0 = lax.ppermute(message, ('row', 'col'), pairs)  1.08 us
    ppermute x1, starting transfers between devices, on_device(): raw1 = lax.ppermute(line, ('row', 'col'), others)  1.05 us
  transfers between devices with their start and end apart: 7, of which 2 were waited for; matrix products, arithmetic and copies ran while one was open for 0% of the time, Pallas kernels for 11%

profile of v10, /device:TPU:0, one launch (start us, length us, event | category | flops | bytes accessed | tf_op | source)
XLA Modules:
  0.0 21.3 jit_solution(17803771251362594685)
XLA Ops:
  0.0 1.6 %project.1 = (bf16[80,128]{1,0:T(8,128)(2,1)S(1)}, bf16[224,128]{1,0:T(8,128)(2,1)S(1)}, bf16[224,128]{1,0:T(8,128)(2,1)S(1)}, bf16[24,4096]{1,0:T(8,128)(2,1)S(...) custom-call(bf16[22,4096]{1,0:T(8,128)(2,1)} %bitcast.7, ...), custom_call_target="tpu_custom_call" | custom-call | tf_op jit(solution)/shard_map/project/pallas_call | solution.py:528
  1.6 3.1 %collective-permute-start = (bf16[224,128]{1,0:T(8,128)(2,1)S(1)}, bf16[224,128]{1,0:T(8,128)(2,1)S(1)}, u32[]{:S(2)}, u32[]{:S(2)}) collective-permute-start(bf16[224,128]{1,0:T(8,128)(2,1)S(1)} %get-tuple-element.26), channel_id=1, source_target_pairs={{0,8},{8,16},{16,24},{24,0},{1,9},{9,17},{17,25},{25,1},{2,10},{10... | collective-permute-start | bytes 172040 | tf_op jit(solution)/shard_map/ppermute | solution.py:549
  4.7 2.1 %collective-permute-start.1 = (bf16[224,128]{1,0:T(8,128)(2,1)S(1)}, bf16[224,128]{1,0:T(8,128)(2,1)S(1)}, u32[]{:S(2)}, u32[]{:S(2)}) collective-permute-start(bf16[224,128]{1,0:T(8,128)(2,1)S(1)} %get-tuple-element.27), channel_id=1, source_target_pairs={{0,24},{8,0},{16,8},{24,16},{1,25},{9,1},{17,9},{25,17},{2,26},{10... | collective-permute-start | bytes 172040 | tf_op jit(solution)/shard_map/ppermute | solution.py:549
  6.8 0.9 %collective-permute-start.2 = (bf16[80,128]{1,0:T(8,128)(2,1)S(1)}, bf16[80,128]{1,0:T(8,128)(2,1)S(1)}, u32[]{:S(2)}, u32[]{:S(2)}) collective-permute-start(bf16[80,128]{1,0:T(8,128)(2,1)S(1)} %get-tuple-element.20._.own_ref), channel_id=1, source_target_pairs={{0,16},{8,24},{16,0},{24,8},{1,17},{9,25},{17,1},{25,9},{2,18},{10... | collective-permute-start | bytes 61448 | tf_op jit(solution)/shard_map/ppermute | solution.py:549
  7.8 1.0 %collective-permute-start.5 = (bf16[24,4096]{1,0:T(8,128)(2,1)S(1)}, bf16[24,4096]{1,0:T(8,128)(2,1)S(1)}, u32[]{:S(2)}, u32[]{:S(2)}) collective-permute-start(bf16[24,4096]{1,0:T(8,128)(2,1)S(1)} %gate.1.line_ref), channel_id=1, source_target_pairs={{0,7},{1,2},{2,1},{3,4},{4,3},{5,6},{6,5},{7,0},{8,15},{9,10},{10,... | collective-permute-start | bytes 589832 | tf_op jit(solution)/shard_map/ppermute | solution.py:570
  8.8 0.6 %collective-permute-start.3 = (bf16[24,4096]{1,0:T(8,128)(2,1)S(1)}, bf16[24,4096]{1,0:T(8,128)(2,1)S(1)}, u32[]{:S(2)}, u32[]{:S(2)}) collective-permute-start(bf16[24,4096]{1,0:T(8,128)(2,1)S(1)} %gate.1.line_ref), channel_id=1, source_target_pairs={{0,1},{1,0},{2,3},{3,2},{4,5},{5,4},{6,7},{7,6},{8,9},{9,8},{10,11... | collective-permute-start | bytes 589832 | tf_op jit(solution)/shard_map/ppermute | solution.py:569
  9.4 2.1 %collective-permute-done.2.rest_refs_0_ = bf16[80,128]{1,0:T(8,128)(2,1)S(1)} collective-permute-done((bf16[80,128]{1,0:T(8,128)(2,1)S(1)}, bf16[80,128]{1,0:T(8,128)(2,1)S(1)}, u32[]{:S(2)}, u32[]{:S(2)}) %collective-permute-start.2) | collective-permute-done | bytes 20512 | tf_op jit(solution)/shard_map/ppermute | solution.py:549
  11.5 0.0 collective-permute-done.below_ref
  11.5 0.0 collective-permute-done.1.above_ref
  11.5 0.5 %update.1 = (bf16[32,4096]{1,0:T(8,128)(2,1)S(1)}, bf16[288,128]{1,0:T(8,128)(2,1)S(1)}) custom-call(bf16[24,4096]{1,0:T(8,128)(2,1)S(1)} %gate.1.line_ref, s32[1,4096]{1,0:T(1,128)S(1)} %get-tuple-element.22.ap_ref, f32[1,4444]{1,0:T(1,128)S(1)} %get-tuple-element.23.meas_ref, s32[1,22]{1,0:T(1,128)S(1)} %get-tuple-element.24.shear_ref, ...), custom_call_target="tpu_custom_call" | custom-call | flops 10000000000 | bytes 40000000 | tf_op jit(solution)/shard_map/update/pallas_call | solution.py:573
  12.0 0.8 %collective-permute-start.6 = (bf16[288,128]{1,0:T(8,128)(2,1)S(1)}, bf16[288,128]{1,0:T(8,128)(2,1)S(1)}, u32[]{:S(2)}, u32[]{:S(2)}) collective-permute-start(bf16[288,128]{1,0:T(8,128)(2,1)S(1)} %get-tuple-element.28._), channel_id=1, source_target_pairs={{0,7},{1,2},{2,1},{3,4},{4,3},{5,6},{6,5},{7,0},{8,15},{9,10},{10,... | collective-permute-start | bytes 221192 | tf_op jit(solution)/shard_map/ppermute | solution.py:594
  12.8 1.1 %collective-permute-start.4 = (bf16[288,128]{1,0:T(8,128)(2,1)S(1)}, bf16[288,128]{1,0:T(8,128)(2,1)S(1)}, u32[]{:S(2)}, u32[]{:S(2)}) collective-permute-start(bf16[288,128]{1,0:T(8,128)(2,1)S(1)} %get-tuple-element.28._), channel_id=1, source_target_pairs={{0,1},{1,0},{2,3},{3,2},{4,5},{5,4},{6,7},{7,6},{8,9},{9,8},{10,11... | collective-permute-start | bytes 221192 | tf_op jit(solution)/shard_map/ppermute | solution.py:593
  13.9 1.8 %weights.1 = (bf16[256,160]{1,0:T(8,128)(2,1)S(1)}, bf16[192,160]{1,0:T(8,128)(2,1)S(1)}, bf16[128,240]{1,0:T(8,128)(2,1)S(1)}, bf16[128,208]{1,0:T(8,128)(2,1)S(1)}, f32[128,128]{1,0:T(8,128)S(1)}) custom-call(bf16[288,128]{1,0:T(8,128)(2,1)S(1)} %get-tuple-element.28._, bf16[16,9]{1,0:T(8,128)(2,1)} %sw_in.1, f32[1,16]{1,0:T(1,128)} %bitcast.10, ...), custom_call_target="tpu_custom_call" | custom-call | tf_op jit(solution)/shard_map/weights/pallas_call | solution.py:605
  15.7 1.2 %collective-permute-done.6.msg1_ref = bf16[288,128]{1,0:T(8,128)(2,1)S(1)} collective-permute-done((bf16[288,128]{1,0:T(8,128)(2,1)S(1)}, bf16[288,128]{1,0:T(8,128)(2,1)S(1)}, u32[]{:S(2)}, u32[]{:S(2)}) %collective-permute-start.6) | collective-permute-done | bytes 73760 | tf_op jit(solution)/shard_map/ppermute | solution.py:594
  16.9 0.0 collective-permute-done.4.msg0_ref
  16.9 0.0 collective-permute-done.5.raw1_ref
  16.9 0.0 collective-permute-done.3.raw0_ref
  16.9 4.4 %denoise.1 = bf16[22,4096]{1,0:T(8,128)(2,1)} custom-call(f32[128,128]{1,0:T(8,128)S(1)} %get-tuple-element.29.ow_ref, bf16[32,4096]{1,0:T(8,128)(2,1)S(1)} %get-tuple-element.30.mid_ref, s32[1,22]{1,0:T(1,128)S(1)} %get-tuple-element.24.shear_ref, f32[1,22]{1,0:T(1,128)S(1)} %get-tuple-element.25.step_ref, ...), custom_call_target="tpu_custom_call" | custom-call | tf_op jit(solution)/shard_map/denoise/pallas_call | solution.py:623
  (1 shorter events, 0.0 us)
Async XLA Ops:
  1.6 9.9 %collective-permute-start = (bf16[224,128]{1,0:T(8,128)(2,1)S(1)}, bf16[224,128]{1,0:T(8,128)(2,1)S(1)}, u32[]{:S(2)}, u32[]{:S(2)}) collective-permute-start(bf16[224,128]{1,0:T(8,128)(2,1)S(1)} %get-tuple-element.26), channel_id=1, source_target_pairs={{0,8},{8,16},{16,24},{24,0},{1,9},{9,17},{17,25},{25,1},{2,10},{10... | collective-permute-start | bytes 172040 | tf_op jit(solution)/shard_map/ppermute | solution.py:549
  4.7 6.8 %collective-permute-start.1 = (bf16[224,128]{1,0:T(8,128)(2,1)S(1)}, bf16[224,128]{1,0:T(8,128)(2,1)S(1)}, u32[]{:S(2)}, u32[]{:S(2)}) collective-permute-start(bf16[224,128]{1,0:T(8,128)(2,1)S(1)} %get-tuple-element.27), channel_id=1, source_target_pairs={{0,24},{8,0},{16,8},{24,16},{1,25},{9,1},{17,9},{25,17},{2,26},{10... | collective-permute-start | bytes 172040 | tf_op jit(solution)/shard_map/ppermute | solution.py:549
  6.8 4.7 %collective-permute-start.2 = (bf16[80,128]{1,0:T(8,128)(2,1)S(1)}, bf16[80,128]{1,0:T(8,128)(2,1)S(1)}, u32[]{:S(2)}, u32[]{:S(2)}) collective-permute-start(bf16[80,128]{1,0:T(8,128)(2,1)S(1)} %get-tuple-element.20._.own_ref), channel_id=1, source_target_pairs={{0,16},{8,24},{16,0},{24,8},{1,17},{9,25},{17,1},{25,9},{2,18},{10... | collective-permute-start | bytes 61448 | tf_op jit(solution)/shard_map/ppermute | solution.py:549
  7.8 9.1 %collective-permute-start.5 = (bf16[24,4096]{1,0:T(8,128)(2,1)S(1)}, bf16[24,4096]{1,0:T(8,128)(2,1)S(1)}, u32[]{:S(2)}, u32[]{:S(2)}) collective-permute-start(bf16[24,4096]{1,0:T(8,128)(2,1)S(1)} %gate.1.line_ref), channel_id=1, source_target_pairs={{0,7},{1,2},{2,1},{3,4},{4,3},{5,6},{6,5},{7,0},{8,15},{9,10},{10,... | collective-permute-start | bytes 589832 | tf_op jit(solution)/shard_map/ppermute | solution.py:570
  8.8 8.1 %collective-permute-start.3 = (bf16[24,4096]{1,0:T(8,128)(2,1)S(1)}, bf16[24,4096]{1,0:T(8,128)(2,1)S(1)}, u32[]{:S(2)}, u32[]{:S(2)}) collective-permute-start(bf16[24,4096]{1,0:T(8,128)(2,1)S(1)} %gate.1.line_ref), channel_id=1, source_target_pairs={{0,1},{1,0},{2,3},{3,2},{4,5},{5,4},{6,7},{7,6},{8,9},{9,8},{10,11... | collective-permute-start | bytes 589832 | tf_op jit(solution)/shard_map/ppermute | solution.py:569
  12.0 4.8 %collective-permute-start.6 = (bf16[288,128]{1,0:T(8,128)(2,1)S(1)}, bf16[288,128]{1,0:T(8,128)(2,1)S(1)}, u32[]{:S(2)}, u32[]{:S(2)}) collective-permute-start(bf16[288,128]{1,0:T(8,128)(2,1)S(1)} %get-tuple-element.28._), channel_id=1, source_target_pairs={{0,7},{1,2},{2,1},{3,4},{4,3},{5,6},{6,5},{7,0},{8,15},{9,10},{10,... | collective-permute-start | bytes 221192 | tf_op jit(solution)/shard_map/ppermute | solution.py:594
  12.8 4.1 %collective-permute-start.4 = (bf16[288,128]{1,0:T(8,128)(2,1)S(1)}, bf16[288,128]{1,0:T(8,128)(2,1)S(1)}, u32[]{:S(2)}, u32[]{:S(2)}) collective-permute-start(bf16[288,128]{1,0:T(8,128)(2,1)S(1)} %get-tuple-element.28._), channel_id=1, source_target_pairs={{0,1},{1,0},{2,3},{3,2},{4,5},{5,4},{6,7},{7,6},{8,9},{9,8},{10,11... | collective-permute-start | bytes 221192 | tf_op jit(solution)/shard_map/ppermute | solution.py:593

commit v11 on v9

--- a/solution.py
+++ b/solution.py
@@ -163,6 +163,9 @@
     tall = own_ref.shape[0] // 2
     outer = -(-meas_ref.shape[1] // LANES)
     raw[...] = line_ref[...].astype(F32)
+    blank = jnp.zeros((out_ref.shape[0], LANES), BF16)
+    out_ref[:, 0:LANES] = blank
+    out_ref[:, cols + LANES :] = blank
     meas[:, (outer - 1) * LANES :] = jnp.zeros((1, LANES), F32)
     meas[:, 0 : meas_ref.shape[1]] = meas_ref[...]
     shear_f = column(shear_ref[...].astype(F32), groups * SUB)
@@ -225,7 +228,9 @@
             pulled = choose(delay[g], turned[g][q : q + reach])
             base = raw[g * SUB : (g + 1) * SUB, here] if g < groups else halo(q)
             pieces.append(base + pulled * open_q * steps[g])
-        out_ref[:, here] = jnp.concatenate(pieces, axis=0).astype(BF16)
+        out_ref[:, (q + 1) * LANES : (q + 2) * LANES] = jnp.concatenate(pieces, axis=0).astype(
+            BF16
+        )
         tiles[q] = jnp.where(sub < 6, pieces[-1], tiles[q])
     msg_ref[...] = jnp.concatenate(tiles, axis=0).astype(BF16)
 
@@ -345,7 +350,9 @@
     groups = -(-bands // SUB)
     ones = jnp.where(rows_of((slots, tile)) < 3, 1.0, 0.0).astype(BF16)
     blank = jnp.zeros((2 * slots, LANES), BF16)
-    zero = jnp.zeros((SUB, LANES), F32)
+    for near in (near0, near1):
+        near[:, 0:LANES] = blank
+        near[:, cols + LANES :] = blank
     shear_f = column(shear_ref[...].astype(F32), groups * SUB)
     step_f = column(step_ref[...], groups * SUB)
     lane = lanes_of()
@@ -357,94 +364,114 @@
         delay.append((s >> 7) + jnp.where(lane + rest >= LANES, 1, 0))
         steps.append(jnp.broadcast_to(step_f[g * SUB : (g + 1) * SUB], (SUB, LANES)))
     rows_in = msg0_ref.shape[0]
-    chunks = inner + reach - 1
     for n, msg_ref in enumerate((msg0_ref, msg1_ref)):
         words[n * rows_in : (n + 1) * rows_in, :] = msg_ref[...].astype(F32)
-    turned = [[[] for _ in range(groups)] for _ in range(2)]
-
-    def neighbours(q):
+    step = tile // LANES
+
+    def neighbours(t):
         for n, (raw_ref, near) in enumerate(((raw0_ref, near0), (raw1_ref, near1))):
             base = n * rows_in
-            while len(turned[n][0]) < q + reach:
-                p = len(turned[n][0])
-                if p >= chunks:
-                    residual = zero
-                else:
-                    at = base + p * SUB + 6
-                    residual = words[at : at + 1, :] + words[at + 1 : at + 2, :]
-                    residual = jnp.broadcast_to(residual, (SUB, LANES))
+            turned = [[] for _ in range(groups)]
+            edges = []
+            for p in range(step + reach - 1):
+                at = pl.multiple_of(base + (t * step + p) * SUB, SUB)
+                word = words[pl.ds(at, SUB), :]
+                edges.append(word)
+                residual = jnp.broadcast_to(word[6:7] + word[7:8], (SUB, LANES))
                 for g in range(groups):
-                    turned[n][g].append(turn(residual, index[g]))
-            at = base + q * SUB
-            raw = raw_ref[:, q * LANES : (q + 1) * LANES].astype(F32)
-            open_q = jnp.broadcast_to(raw[bands : bands + 1], (SUB, LANES))
-            pieces = [
-                raw[g * SUB : (g + 1) * SUB]
-                + choose(delay[g], turned[n][g][q : q + reach]) * open_q * steps[g]
-                for g in range(groups)
-            ]
-            pieces.append(words[at : at + SUB, :])
-            near[:, q * LANES : (q + 1) * LANES] = jnp.concatenate(pieces, axis=0).astype(BF16)
+                    turned[g].append(turn(residual, index[g]))
+            start = pl.multiple_of(t * tile, LANES)
+            raw = raw_ref[:, pl.ds(start, tile)].astype(F32)
+            made = []
+            for q in range(step):
+                here = raw[:, q * LANES : (q + 1) * LANES]
+                open_q = jnp.broadcast_to(here[bands : bands + 1], (SUB, LANES))
+                pieces = [
+                    here[g * SUB : (g + 1) * SUB]
+                    + choose(delay[g], turned[g][q : q + reach]) * open_q * steps[g]
+                    for g in range(groups)
+                ]
+                made.append(jnp.concatenate(pieces + [edges[q]], axis=0).astype(BF16))
+            start = pl.multiple_of(t * tile + LANES, LANES)
+            near[:, pl.ds(start, tile)] = jnp.concatenate(made, axis=1)
 
     def silu_twice(half):
         return half + half * jnp.tanh(half)
 
-    def spatial(t):
-        start = t * tile
-        end = start + tile
-        patches = []
+    def patches(t):
+        parts = []
         for ref in (near0, mid_ref, near1):
-            left = ref[:, start - LANES : start] if t else blank
-            here = ref[:, start:end]
-            right = ref[:, end : end + LANES] if t < tiles - 1 else blank
-            row = jnp.concatenate([left, here, right], axis=1)
+            row = ref[:, pl.ds(pl.multiple_of(t * tile, LANES), wide)]
             back = pltpu.roll(row, 1, 1)[:, LANES : LANES + tile]
             ahead = pltpu.roll(row, wide - 1, 1)[:, LANES : LANES + tile]
-            patches += [back, here, ahead]
-        buf = act.at[t % act.shape[0]]
-        for part, w_ref in enumerate((main_ref, halo_ref)):
-            x = jnp.concatenate(
-                [p[part * slots : (part + 1) * slots] for p in patches] + [ones], axis=0
-            )
-            half = jnp.dot(w_ref[...], x, preferred_element_type=F32)
-            value = silu_twice(half).astype(BF16)
-            if part == 0:
-                buf[3 * ch : 19 * ch, :] = value
-            else:
-                buf[0 : 3 * ch, :] = value[0 : 3 * ch]
-                buf[19 * ch : 28 * ch, :] = value[3 * ch :]
-
-    def spectral(t):
-        start = t * tile
-        buf = act.at[t % act.shape[0]]
-        blocks = []
-        for i in range(groups):
-            w_ref = second_ref if i == groups - 1 else first_ref
-            first = i * SUB * ch
-            x = jnp.concatenate([buf[first : first + w_ref.shape[1] - slots, :], ones], axis=0)
-            blocks.append(jnp.dot(w_ref[...], x, preferred_element_type=F32))
-        pieces = []
-        for half in blocks:
-            total = None
-            for k in range(ch):
-                weight = ow_ref[k * SUB : (k + 1) * SUB, :]
-                weight = jnp.concatenate([weight] * (tile // LANES), axis=1)
-                term = weight * silu_twice(half[k * SUB : (k + 1) * SUB])
-                total = term if total is None else total + term
-            pieces.append(total)
-        update = jnp.concatenate(pieces, axis=0)[0:bands]
-        center = mid_ref[:, start : start + tile].astype(F32)[0:bands]
-        out_ref[:, start : start + tile] = (center + update).astype(BF16)
-
-    made = 0
-    for t in range(tiles + 1):
-        while t < tiles and made < min((t + 1) * tile // LANES + 1, inner):
-            neighbours(made)
-            made += 1
-        if t < tiles:
-            spatial(t)
-        if t:
-            spectral(t - 1)
+            parts += [back, row[:, LANES : LANES + tile], ahead]
+        return [
+            jnp.concatenate([p[at : at + slots] for p in parts] + [ones], axis=0)
+            for at in (0, slots)
+        ]
+
+    def activate(part, half):
+        value = silu_twice(half).astype(BF16)
+        if part == 0:
+            act[3 * ch : 19 * ch, :] = value
+        else:
+            act[0 : 3 * ch, :] = value[0 : 3 * ch]
+            act[19 * ch : 28 * ch, :] = value[3 * ch :]
+
+    def spatial(part, inputs):
+        w_ref = halo_ref if part else main_ref
+        return jnp.dot(w_ref[...], inputs[part], preferred_element_type=F32)
+
+    def spectral(i):
+        w_ref = second_ref if i == groups - 1 else first_ref
+        first = i * SUB * ch
+        x = jnp.concatenate([act[first : first + w_ref.shape[1] - slots, :], ones], axis=0)
+        return jnp.dot(w_ref[...], x, preferred_element_type=F32)
+
+    def project(half):
+        total = None
+        for k in range(ch):
+            weight = ow_ref[k * SUB : (k + 1) * SUB, :]
+            weight = jnp.concatenate([weight] * (tile // LANES), axis=1)
+            term = weight * silu_twice(half[k * SUB : (k + 1) * SUB])
+            total = term if total is None else total + term
+        return total
+
+    def finish(t, sums):
+        update = jnp.concatenate(sums, axis=0)[0:bands]
+        center = mid_ref[:, pl.ds(pl.multiple_of(t * tile + LANES, LANES), tile)]
+        result = center.astype(F32)[0:bands] + update
+        out_ref[:, pl.ds(pl.multiple_of(t * tile, LANES), tile)] = result.astype(BF16)
+
+    ahead_by = 3
+
+    def prepare(t, carry):
+        neighbours(t)
+        return carry
+
+    lax.fori_loop(0, min(ahead_by, tiles), prepare, 0)
+    start_inputs = patches(0)
+    for part in range(2):
+        activate(part, spatial(part, start_inputs))
+
+    def body(t, carry):
+        blocks = [spectral(0)]
+        inputs = patches(t + 1)
+        sums = []
+        for i in range(1, groups):
+            blocks.append(spectral(i))
+            sums.append(project(blocks[i - 1]))
+        half0 = spatial(0, inputs)
+        sums.append(project(blocks[groups - 1]))
+        half1 = spatial(1, inputs)
+        finish(t, sums)
+        activate(0, half0)
+        neighbours(jnp.minimum(t + ahead_by, tiles - 1))
+        activate(1, half1)
+        return carry
+
+    lax.fori_loop(0, tiles - 1, body, 0)
+    finish(tiles - 1, [project(spectral(i)) for i in range(groups)])
 
 
 def vmem(n):
@@ -539,7 +566,7 @@
     updated, message = pl.pallas_call(
         functools.partial(update_kernel, reach, len(far)),
         out_shape=(
-            jax.ShapeDtypeStruct((slots, cols), BF16),
+            jax.ShapeDtypeStruct((slots, cols + 2 * LANES), BF16),
             jax.ShapeDtypeStruct((words, LANES), BF16),
         ),
         in_specs=vmem(8 + len(far)),
@@ -592,9 +619,9 @@
         in_specs=vmem(12),
         out_specs=vmem(1)[0],
         scratch_shapes=[
-            pltpu.VMEM((4, 28 * ch, tile), BF16),
-            pltpu.VMEM((slots, cols), BF16),
-            pltpu.VMEM((slots, cols), BF16),
+            pltpu.VMEM((28 * ch, tile), BF16),
+            pltpu.VMEM((slots, cols + 2 * LANES), BF16),
+            pltpu.VMEM((slots, cols + 2 * LANES), BF16),
             pltpu.VMEM((2 * words, LANES), F32),
         ],
         compiler_params=params,

time: 21.5 us -> 22.4 us (1.042)
  Pallas kernels: 8.37 us -> 9.29 us
    pallas_call x1, Pallas kernels: 4.44 us -> 5.36 us  [on_device(): pl.pallas_call(functools.partial(denoise_kernel, tile, reach), out_shape=...]
  transfers between devices with their start and end apart: 7 -> 7, of which waited for: 2 -> 2; matrix products, arithmetic and copies ran while one was open for 0% -> 0% of each run, Pallas kernels for 11% -> 10%
where the time goes in v11:
time: 22.4 us; the launch traced here: 22.2 us
  starting transfers between devices  9.61 us (43%)
  Pallas kernels  9.29 us (41%)
  waiting for transfers between devices  3.3 us (15%)
    ppermute x3, starting transfers between devices, around(): lax.ppermute(x, 'band', [(i, (i + shift) % count) for i in range(count)])  6.11 us
    pallas_call x1, Pallas kernels, on_device(): pl.pallas_call(functools.partial(denoise_kernel, tile, reach), out_shape=...  5.36 us
    ppermute x3, waiting for transfers between devices, around(): lax.ppermute(x, 'band', [(i, (i + shift) % count) for i in range(count)])  2.1 us
    pallas_call x1, Pallas kernels, on_device(): pl.pallas_call(weights_kernel, out_shape=(jax.ShapeDtypeStruct((16 * ch,...  1.79 us
    pallas_call x1, Pallas kernels, on_device(): pl.pallas_call(functools.partial(project_kernel, reach), out_shape=(jax.S...  1.63 us
    ppermute x1, waiting for transfers between devices, on_device(): message1 = lax.ppermute(message, ('row', 'col'), others)  1.19 us
    ppermute x1, starting transfers between devices, on_device(): message0 = lax.ppermute(message, ('row', 'col'), pairs)  1.08 us
    ppermute x1, starting transfers between devices, on_device(): raw1 = lax.ppermute(line, ('row', 'col'), others)  1.05 us
  transfers between devices with their start and end apart: 7, of which 2 were waited for; matrix products, arithmetic and copies ran while one was open for 0% of the time, Pallas kernels for 10%

profile of v11, /device:TPU:0, one launch (start us, length us, event | category | flops | bytes accessed | tf_op | source)
XLA Modules:
  0.0 22.2 jit_solution(14881150395100800838)
XLA Ops:
  0.0 1.6 %project.1 = (bf16[80,128]{1,0:T(8,128)(2,1)S(1)}, bf16[224,128]{1,0:T(8,128)(2,1)S(1)}, bf16[224,128]{1,0:T(8,128)(2,1)S(1)}, bf16[24,4096]{1,0:T(8,128)(2,1)S(...) custom-call(bf16[22,4096]{1,0:T(8,128)(2,1)} %bitcast.7, ...), custom_call_target="tpu_custom_call" | custom-call | tf_op jit(solution)/shard_map/project/pallas_call | solution.py:521
  1.6 3.1 %collective-permute-start = (bf16[224,128]{1,0:T(8,128)(2,1)S(1)}, bf16[224,128]{1,0:T(8,128)(2,1)S(1)}, u32[]{:S(2)}, u32[]{:S(2)}) collective-permute-start(bf16[224,128]{1,0:T(8,128)(2,1)S(1)} %get-tuple-element.26), channel_id=1, source_target_pairs={{0,8},{8,16},{16,24},{24,0},{1,9},{9,17},{17,25},{25,1},{2,10},{10... | collective-permute-start | bytes 172040 | tf_op jit(solution)/shard_map/ppermute | solution.py:542
  4.7 2.1 %collective-permute-start.1 = (bf16[224,128]{1,0:T(8,128)(2,1)S(1)}, bf16[224,128]{1,0:T(8,128)(2,1)S(1)}, u32[]{:S(2)}, u32[]{:S(2)}) collective-permute-start(bf16[224,128]{1,0:T(8,128)(2,1)S(1)} %get-tuple-element.27), channel_id=1, source_target_pairs={{0,24},{8,0},{16,8},{24,16},{1,25},{9,1},{17,9},{25,17},{2,26},{10... | collective-permute-start | bytes 172040 | tf_op jit(solution)/shard_map/ppermute | solution.py:542
  6.8 0.9 %collective-permute-start.2 = (bf16[80,128]{1,0:T(8,128)(2,1)S(1)}, bf16[80,128]{1,0:T(8,128)(2,1)S(1)}, u32[]{:S(2)}, u32[]{:S(2)}) collective-permute-start(bf16[80,128]{1,0:T(8,128)(2,1)S(1)} %get-tuple-element.20._.own_ref), channel_id=1, source_target_pairs={{0,16},{8,24},{16,0},{24,8},{1,17},{9,25},{17,1},{25,9},{2,18},{10... | collective-permute-start | bytes 61448 | tf_op jit(solution)/shard_map/ppermute | solution.py:542
  7.8 1.0 %collective-permute-start.5 = (bf16[24,4096]{1,0:T(8,128)(2,1)S(1)}, bf16[24,4096]{1,0:T(8,128)(2,1)S(1)}, u32[]{:S(2)}, u32[]{:S(2)}) collective-permute-start(bf16[24,4096]{1,0:T(8,128)(2,1)S(1)} %gate.1.line_ref), channel_id=1, source_target_pairs={{0,7},{1,2},{2,1},{3,4},{4,3},{5,6},{6,5},{7,0},{8,15},{9,10},{10,... | collective-permute-start | bytes 589832 | tf_op jit(solution)/shard_map/ppermute | solution.py:563
  8.8 0.6 %collective-permute-start.3 = (bf16[24,4096]{1,0:T(8,128)(2,1)S(1)}, bf16[24,4096]{1,0:T(8,128)(2,1)S(1)}, u32[]{:S(2)}, u32[]{:S(2)}) collective-permute-start(bf16[24,4096]{1,0:T(8,128)(2,1)S(1)} %gate.1.line_ref), channel_id=1, source_target_pairs={{0,1},{1,0},{2,3},{3,2},{4,5},{5,4},{6,7},{7,6},{8,9},{9,8},{10,11... | collective-permute-start | bytes 589832 | tf_op jit(solution)/shard_map/ppermute | solution.py:562
  9.4 2.1 %collective-permute-done.2.rest_refs_0_ = bf16[80,128]{1,0:T(8,128)(2,1)S(1)} collective-permute-done((bf16[80,128]{1,0:T(8,128)(2,1)S(1)}, bf16[80,128]{1,0:T(8,128)(2,1)S(1)}, u32[]{:S(2)}, u32[]{:S(2)}) %collective-permute-start.2) | collective-permute-done | bytes 20512 | tf_op jit(solution)/shard_map/ppermute | solution.py:542
  11.5 0.0 collective-permute-done.below_ref
  11.5 0.0 collective-permute-done.1.above_ref
  11.5 0.5 %update.1 = (bf16[32,4352]{1,0:T(8,128)(2,1)S(1)}, bf16[288,128]{1,0:T(8,128)(2,1)S(1)}) custom-call(bf16[24,4096]{1,0:T(8,128)(2,1)S(1)} %gate.1.line_ref, s32[1,4096]{1,0:T(1,128)S(1)} %get-tuple-element.22.ap_ref, f32[1,4444]{1,0:T(1,128)S(1)} %get-tuple-element.23.meas_ref, s32[1,22]{1,0:T(1,128)S(1)} %get-tuple-element.24.shear_ref, ...), custom_call_target="tpu_custom_call" | custom-call | flops 10000000000 | bytes 40000000 | tf_op jit(solution)/shard_map/update/pallas_call | solution.py:566
  12.0 0.8 %collective-permute-start.6 = (bf16[288,128]{1,0:T(8,128)(2,1)S(1)}, bf16[288,128]{1,0:T(8,128)(2,1)S(1)}, u32[]{:S(2)}, u32[]{:S(2)}) collective-permute-start(bf16[288,128]{1,0:T(8,128)(2,1)S(1)} %get-tuple-element.28._), channel_id=1, source_target_pairs={{0,7},{1,2},{2,1},{3,4},{4,3},{5,6},{6,5},{7,0},{8,15},{9,10},{10,... | collective-permute-start | bytes 221192 | tf_op jit(solution)/shard_map/ppermute | solution.py:587
  12.8 1.1 %collective-permute-start.4 = (bf16[288,128]{1,0:T(8,128)(2,1)S(1)}, bf16[288,128]{1,0:T(8,128)(2,1)S(1)}, u32[]{:S(2)}, u32[]{:S(2)}) collective-permute-start(bf16[288,128]{1,0:T(8,128)(2,1)S(1)} %get-tuple-element.28._), channel_id=1, source_target_pairs={{0,1},{1,0},{2,3},{3,2},{4,5},{5,4},{6,7},{7,6},{8,9},{9,8},{10,11... | collective-permute-start | bytes 221192 | tf_op jit(solution)/shard_map/ppermute | solution.py:586
  13.9 1.8 %weights.1 = (bf16[256,160]{1,0:T(8,128)(2,1)S(1)}, bf16[192,160]{1,0:T(8,128)(2,1)S(1)}, bf16[128,240]{1,0:T(8,128)(2,1)S(1)}, bf16[128,208]{1,0:T(8,128)(2,1)S(1)}, f32[128,128]{1,0:T(8,128)S(1)}) custom-call(bf16[288,128]{1,0:T(8,128)(2,1)S(1)} %get-tuple-element.28._, bf16[16,9]{1,0:T(8,128)(2,1)} %sw_in.1, f32[1,16]{1,0:T(1,128)} %bitcast.10, ...), custom_call_target="tpu_custom_call" | custom-call | tf_op jit(solution)/shard_map/weights/pallas_call | solution.py:598
  15.7 1.2 %collective-permute-done.6.msg1_ref = bf16[288,128]{1,0:T(8,128)(2,1)S(1)} collective-permute-done((bf16[288,128]{1,0:T(8,128)(2,1)S(1)}, bf16[288,128]{1,0:T(8,128)(2,1)S(1)}, u32[]{:S(2)}, u32[]{:S(2)}) %collective-permute-start.6) | collective-permute-done | bytes 73760 | tf_op jit(solution)/shard_map/ppermute | solution.py:587
  16.9 0.0 collective-permute-done.4.msg0_ref
  16.9 0.0 collective-permute-done.5.raw1_ref
  16.9 0.0 collective-permute-done.3.raw0_ref
  16.9 5.4 %denoise.1 = bf16[22,4096]{1,0:T(8,128)(2,1)} custom-call(f32[128,128]{1,0:T(8,128)S(1)} %get-tuple-element.29.ow_ref, bf16[32,4352]{1,0:T(8,128)(2,1)S(1)} %get-tuple-element.30.mid_ref, s32[1,22]{1,0:T(1,128)S(1)} %get-tuple-element.24.shear_ref, f32[1,22]{1,0:T(1,128)S(1)} %get-tuple-element.25.step_ref, ...), custom_call_target="tpu_custom_call" | custom-call | tf_op jit(solution)/shard_map/denoise/pallas_call | solution.py:616
  (1 shorter events, 0.0 us)
Async XLA Ops:
  1.6 9.9 %collective-permute-start = (bf16[224,128]{1,0:T(8,128)(2,1)S(1)}, bf16[224,128]{1,0:T(8,128)(2,1)S(1)}, u32[]{:S(2)}, u32[]{:S(2)}) collective-permute-start(bf16[224,128]{1,0:T(8,128)(2,1)S(1)} %get-tuple-element.26), channel_id=1, source_target_pairs={{0,8},{8,16},{16,24},{24,0},{1,9},{9,17},{17,25},{25,1},{2,10},{10... | collective-permute-start | bytes 172040 | tf_op jit(solution)/shard_map/ppermute | solution.py:542
  4.7 6.8 %collective-permute-start.1 = (bf16[224,128]{1,0:T(8,128)(2,1)S(1)}, bf16[224,128]{1,0:T(8,128)(2,1)S(1)}, u32[]{:S(2)}, u32[]{:S(2)}) collective-permute-start(bf16[224,128]{1,0:T(8,128)(2,1)S(1)} %get-tuple-element.27), channel_id=1, source_target_pairs={{0,24},{8,0},{16,8},{24,16},{1,25},{9,1},{17,9},{25,17},{2,26},{10... | collective-permute-start | bytes 172040 | tf_op jit(solution)/shard_map/ppermute | solution.py:542
  6.8 4.7 %collective-permute-start.2 = (bf16[80,128]{1,0:T(8,128)(2,1)S(1)}, bf16[80,128]{1,0:T(8,128)(2,1)S(1)}, u32[]{:S(2)}, u32[]{:S(2)}) collective-permute-start(bf16[80,128]{1,0:T(8,128)(2,1)S(1)} %get-tuple-element.20._.own_ref), channel_id=1, source_target_pairs={{0,16},{8,24},{16,0},{24,8},{1,17},{9,25},{17,1},{25,9},{2,18},{10... | collective-permute-start | bytes 61448 | tf_op jit(solution)/shard_map/ppermute | solution.py:542
  7.8 9.1 %collective-permute-start.5 = (bf16[24,4096]{1,0:T(8,128)(2,1)S(1)}, bf16[24,4096]{1,0:T(8,128)(2,1)S(1)}, u32[]{:S(2)}, u32[]{:S(2)}) collective-permute-start(bf16[24,4096]{1,0:T(8,128)(2,1)S(1)} %gate.1.line_ref), channel_id=1, source_target_pairs={{0,7},{1,2},{2,1},{3,4},{4,3},{5,6},{6,5},{7,0},{8,15},{9,10},{10,... | collective-permute-start | bytes 589832 | tf_op jit(solution)/shard_map/ppermute | solution.py:563
  8.8 8.1 %collective-permute-start.3 = (bf16[24,4096]{1,0:T(8,128)(2,1)S(1)}, bf16[24,4096]{1,0:T(8,128)(2,1)S(1)}, u32[]{:S(2)}, u32[]{:S(2)}) collective-permute-start(bf16[24,4096]{1,0:T(8,128)(2,1)S(1)} %gate.1.line_ref), channel_id=1, source_target_pairs={{0,1},{1,0},{2,3},{3,2},{4,5},{5,4},{6,7},{7,6},{8,9},{9,8},{10,11... | collective-permute-start | bytes 589832 | tf_op jit(solution)/shard_map/ppermute | solution.py:562
  12.0 4.8 %collective-permute-start.6 = (bf16[288,128]{1,0:T(8,128)(2,1)S(1)}, bf16[288,128]{1,0:T(8,128)(2,1)S(1)}, u32[]{:S(2)}, u32[]{:S(2)}) collective-permute-start(bf16[288,128]{1,0:T(8,128)(2,1)S(1)} %get-tuple-element.28._), channel_id=1, source_target_pairs={{0,7},{1,2},{2,1},{3,4},{4,3},{5,6},{6,5},{7,0},{8,15},{9,10},{10,... | collective-permute-start | bytes 221192 | tf_op jit(solution)/shard_map/ppermute | solution.py:587
  12.8 4.1 %collective-permute-start.4 = (bf16[288,128]{1,0:T(8,128)(2,1)S(1)}, bf16[288,128]{1,0:T(8,128)(2,1)S(1)}, u32[]{:S(2)}, u32[]{:S(2)}) collective-permute-start(bf16[288,128]{1,0:T(8,128)(2,1)S(1)} %get-tuple-element.28._), channel_id=1, source_target_pairs={{0,1},{1,0},{2,3},{3,2},{4,5},{5,4},{6,7},{7,6},{8,9},{9,8},{10,11... | collective-permute-start | bytes 221192 | tf_op jit(solution)/shard_map/ppermute | solution.py:586

commit v12 on v10

--- a/solution.py
+++ b/solution.py
@@ -12,6 +12,8 @@
 F32 = jnp.float32
 BF16 = jnp.bfloat16
 I32 = jnp.int32
+COUNTER = 512.0
+EXTRA = 16
 
 
 def lanes_of(shape=(SUB, LANES)):
@@ -82,13 +84,10 @@
         delay.append((s >> 7) + jnp.where(lane < rest, 1, 0))
     zero = jnp.zeros((SUB, LANES), F32)
     turned = [[zero] * (reach - 1) for _ in range(groups)]
-    opened = [[zero] * (reach - 1) for _ in range(groups)]
     sums = [zero] * (tall // SUB)
-    counts = [zero] * (tall // SUB)
     firsts, lasts = [], []
     for p in range(outer):
         total = zero
-        count = zero
         if p < inner:
             open_p = jnp.broadcast_to(
                 ap_ref[:, p * LANES : (p + 1) * LANES].astype(F32), (SUB, LANES)
@@ -104,22 +103,19 @@
             ).astype(BF16)
         for g in range(groups):
             if p < inner:
-                here = turn(layers[g] * open_p, index[g])
-                here_open = turn(open_p, index[g])
+                here = (layers[g] + COUNTER) * open_p
+                if (g + 1) * SUB > bands:
+                    here = jnp.where(sub < bands - g * SUB, here, 0.0)
+                here = turn(here, index[g])
             else:
-                here = here_open = zero
+                here = zero
             options = [here] + turned[g]
-            options_open = [here_open] + opened[g]
             turned[g] = options[:-1]
-            opened[g] = options_open[:-1]
             total = total + choose(delay[g], options)
-            part = choose(delay[g], options_open)
-            if (g + 1) * SUB > bands:
-                part = jnp.where(sub < bands - g * SUB, part, 0.0)
-            count = count + part
         v, at = divmod(p, SUB)
         sums[v] = jnp.where(sub == at, jnp.sum(total, axis=0, keepdims=True), sums[v])
-        counts[v] = jnp.where(sub == at, jnp.sum(count, axis=0, keepdims=True), counts[v])
+    counts = [jnp.floor(x * (1.0 / COUNTER) + 0.5) for x in sums]
+    sums = [x - COUNTER * n for x, n in zip(sums, counts)]
     sides = []
     for g in (0, groups - 1):
         s = shear_i[g * SUB : (g + 1) * SUB]
@@ -152,10 +148,11 @@
     own_ref,
     below_ref,
     above_ref,
+    _,
     *rest_refs,
 ):
     far_refs = rest_refs[:fars]
-    out_ref, msg_ref, raw, meas, rest_row = rest_refs[fars:]
+    out_ref, msg_ref, long_ref, raw, meas, rest_row = rest_refs[fars:]
     groups = line_ref.shape[0] // SUB
     cols = line_ref.shape[1]
     inner = cols // LANES
@@ -227,7 +224,11 @@
             pieces.append(base + pulled * open_q * steps[g])
         out_ref[:, here] = jnp.concatenate(pieces, axis=0).astype(BF16)
         tiles[q] = jnp.where(sub < 6, pieces[-1], tiles[q])
-    msg_ref[...] = jnp.concatenate(tiles, axis=0).astype(BF16)
+    words = jnp.concatenate(tiles, axis=0).astype(BF16)
+    msg_ref[...] = words
+    long_ref[0 : words.shape[0], :] = words
+    rest = (long_ref.shape[0] - words.shape[0], LANES)
+    long_ref[words.shape[0] :, :] = jnp.zeros(rest, BF16)
 
 
 def spread(rows, ch, which):
@@ -315,6 +316,55 @@
     out_w_ref[...] = jnp.broadcast_to(picked(ow_ref, rows, which), out_w_ref.shape)
 
 
+def neighbour_chunks(reach, bands, shear_ref, step_ref, raw_ref, msg_ref, near, words):
+    inner = raw_ref.shape[1] // LANES
+    groups = -(-bands // SUB)
+    zero = jnp.zeros((SUB, LANES), F32)
+    shear_f = column(shear_ref[...].astype(F32), groups * SUB)
+    step_f = column(step_ref[...], groups * SUB)
+    lane = lanes_of()
+    index, delay, steps = [], [], []
+    for g in range(groups):
+        s = jnp.broadcast_to(shear_f[g * SUB : (g + 1) * SUB].astype(I32), (SUB, LANES))
+        rest = s & (LANES - 1)
+        index.append((lane + rest) & (LANES - 1))
+        delay.append((s >> 7) + jnp.where(lane + rest >= LANES, 1, 0))
+        steps.append(jnp.broadcast_to(step_f[g * SUB : (g + 1) * SUB], (SUB, LANES)))
+    chunks = inner + reach - 1
+    words[...] = msg_ref[0 : words.shape[0], :].astype(F32)
+    turned = [[] for _ in range(groups)]
+
+    def make(q):
+        while len(turned[0]) < q + reach:
+            p = len(turned[0])
+            if p >= chunks:
+                residual = zero
+            else:
+                at = p * SUB + 6
+                residual = words[at : at + 1, :] + words[at + 1 : at + 2, :]
+                residual = jnp.broadcast_to(residual, (SUB, LANES))
+            for g in range(groups):
+                turned[g].append(turn(residual, index[g]))
+        raw = raw_ref[:, q * LANES : (q + 1) * LANES].astype(F32)
+        open_q = jnp.broadcast_to(raw[bands : bands + 1], (SUB, LANES))
+        pieces = [
+            raw[g * SUB : (g + 1) * SUB]
+            + choose(delay[g], turned[g][q : q + reach]) * open_q * steps[g]
+            for g in range(groups)
+        ]
+        pieces.append(words[q * SUB : (q + 1) * SUB, :])
+        near[:, q * LANES : (q + 1) * LANES] = jnp.concatenate(pieces, axis=0).astype(BF16)
+
+    return make
+
+
+def neighbour_kernel(reach, shear_ref, step_ref, raw_ref, msg_ref, _, near, words):
+    bands = shear_ref.shape[1]
+    make = neighbour_chunks(reach, bands, shear_ref, step_ref, raw_ref, msg_ref, near, words)
+    for q in range(near.shape[1] // LANES):
+        make(q)
+
+
 def denoise_kernel(
     tile,
     reach,
@@ -322,17 +372,15 @@
     mid_ref,
     shear_ref,
     step_ref,
-    raw0_ref,
-    msg0_ref,
-    raw1_ref,
-    msg1_ref,
+    near0,
+    raw_ref,
+    msg_ref,
     main_ref,
     halo_ref,
     first_ref,
     second_ref,
     out_ref,
     act,
-    near0,
     near1,
     words,
 ):
@@ -345,46 +393,9 @@
     groups = -(-bands // SUB)
     ones = jnp.where(rows_of((slots, tile)) < 3, 1.0, 0.0).astype(BF16)
     blank = jnp.zeros((2 * slots, LANES), BF16)
-    zero = jnp.zeros((SUB, LANES), F32)
-    shear_f = column(shear_ref[...].astype(F32), groups * SUB)
-    step_f = column(step_ref[...], groups * SUB)
-    lane = lanes_of()
-    index, delay, steps = [], [], []
-    for g in range(groups):
-        s = jnp.broadcast_to(shear_f[g * SUB : (g + 1) * SUB].astype(I32), (SUB, LANES))
-        rest = s & (LANES - 1)
-        index.append((lane + rest) & (LANES - 1))
-        delay.append((s >> 7) + jnp.where(lane + rest >= LANES, 1, 0))
-        steps.append(jnp.broadcast_to(step_f[g * SUB : (g + 1) * SUB], (SUB, LANES)))
-    rows_in = msg0_ref.shape[0]
-    chunks = inner + reach - 1
-    for n, msg_ref in enumerate((msg0_ref, msg1_ref)):
-        words[n * rows_in : (n + 1) * rows_in, :] = msg_ref[...].astype(F32)
-    turned = [[[] for _ in range(groups)] for _ in range(2)]
-
-    def neighbours(q):
-        for n, (raw_ref, near) in enumerate(((raw0_ref, near0), (raw1_ref, near1))):
-            base = n * rows_in
-            while len(turned[n][0]) < q + reach:
-                p = len(turned[n][0])
-                if p >= chunks:
-                    residual = zero
-                else:
-                    at = base + p * SUB + 6
-                    residual = words[at : at + 1, :] + words[at + 1 : at + 2, :]
-                    residual = jnp.broadcast_to(residual, (SUB, LANES))
-                for g in range(groups):
-                    turned[n][g].append(turn(residual, index[g]))
-            at = base + q * SUB
-            raw = raw_ref[:, q * LANES : (q + 1) * LANES].astype(F32)
-            open_q = jnp.broadcast_to(raw[bands : bands + 1], (SUB, LANES))
-            pieces = [
-                raw[g * SUB : (g + 1) * SUB]
-                + choose(delay[g], turned[n][g][q : q + reach]) * open_q * steps[g]
-                for g in range(groups)
-            ]
-            pieces.append(words[at : at + SUB, :])
-            near[:, q * LANES : (q + 1) * LANES] = jnp.concatenate(pieces, axis=0).astype(BF16)
+    neighbours = neighbour_chunks(
+        reach, bands, shear_ref, step_ref, raw_ref, msg_ref, near1, words
+    )
 
     def silu_twice(half):
         return half + half * jnp.tanh(half)
@@ -569,30 +580,6 @@
     raw0 = lax.ppermute(line, ("row", "col"), pairs)
     raw1 = lax.ppermute(line, ("row", "col"), others)
 
-    words = (outer + 1) * SUB
-    updated, message = pl.pallas_call(
-        functools.partial(update_kernel, reach, len(far)),
-        out_shape=(
-            jax.ShapeDtypeStruct((slots, cols), BF16),
-            jax.ShapeDtypeStruct((words, LANES), BF16),
-        ),
-        in_specs=vmem(8 + len(far)),
-        out_specs=tuple(vmem(2)),
-        scratch_shapes=[
-            pltpu.VMEM((groups * SUB, cols), F32),
-            pltpu.VMEM((1, outer * LANES), F32),
-            pltpu.VMEM((tall, LANES), F32),
-        ],
-        compiler_params=params,
-        cost_estimate=pl.CostEstimate(
-            flops=10**10, bytes_accessed=4 * 10**7, transcendentals=0
-        ),
-        name="update",
-    )(*kept, part, below, above, *far)
-
-    message0 = lax.ppermute(message, ("row", "col"), pairs)
-    message1 = lax.ppermute(message, ("row", "col"), others)
-
     small = (
         spatial_weight,
         spatial_bias.reshape(1, ch),
@@ -617,19 +604,54 @@
         + [pltpu.SemaphoreType.DMA((5,))],
         compiler_params=params,
         name="weights",
-    )(message, *in_hbm(small))
+    )(line, *in_hbm(small))
+
+    words = (outer + 1) * SUB
+    updated, message, longer = pl.pallas_call(
+        functools.partial(update_kernel, reach, len(far)),
+        out_shape=(
+            jax.ShapeDtypeStruct((slots, cols), BF16),
+            jax.ShapeDtypeStruct((words, LANES), BF16),
+            jax.ShapeDtypeStruct((words + EXTRA, LANES), BF16),
+        ),
+        in_specs=vmem(8) + [ANY] + vmem(len(far)),
+        out_specs=tuple(vmem(3)),
+        scratch_shapes=[
+            pltpu.VMEM((groups * SUB, cols), F32),
+            pltpu.VMEM((1, outer * LANES), F32),
+            pltpu.VMEM((tall, LANES), F32),
+        ],
+        compiler_params=params,
+        cost_estimate=pl.CostEstimate(
+            flops=10**10, bytes_accessed=4 * 10**7, transcendentals=0
+        ),
+        name="update",
+    )(*kept, part, below, above, out_w, *far)
+
+    message0 = lax.ppermute(message, ("row", "col"), pairs)
+    message1 = lax.ppermute(longer, ("row", "col"), others)
+
+    near0 = pl.pallas_call(
+        functools.partial(neighbour_kernel, reach),
+        out_shape=jax.ShapeDtypeStruct((slots, cols), BF16),
+        in_specs=vmem(4) + [ANY],
+        out_specs=vmem(1)[0],
+        scratch_shapes=[pltpu.VMEM((words, LANES), F32)],
+        compiler_params=params,
+        cost_estimate=pl.CostEstimate(flops=1, bytes_accessed=1, transcendentals=0),
+        name="partner",
+    )(kept[3], kept[4], raw0, message0, message)
 
     tile = 512
     result = pl.pallas_call(
         functools.partial(denoise_kernel, tile, reach),
         out_shape=jax.ShapeDtypeStruct((bands, cols), BF16),
-        in_specs=vmem(12),
+        in_specs=vmem(11),
         out_specs=vmem(1)[0],
         scratch_shapes=[
             pltpu.VMEM((4, 28 * ch, tile), BF16),
             pltpu.VMEM((slots, cols), BF16),
-            pltpu.VMEM((slots, cols), BF16),
-            pltpu.VMEM((2 * words, LANES), F32),
+            pltpu.VMEM((words, LANES), F32),
         ],
         compiler_params=params,
         name="denoise",
@@ -638,8 +660,7 @@
         updated,
         kept[3],
         kept[4],
-        raw0,
-        message0,
+        near0,
         raw1,
         message1,
         main_w,

time: 21.5 us -> 21.4 us (level)
  Pallas kernels: 8.35 us -> 8.05 us
  starting transfers between devices: 9.61 us -> 9.88 us
    ppermute x3, waiting for transfers between devices: 2.1 us -> 0.01 us  [around(): lax.ppermute(x, 'band', [(i, (i + shift) % count) for i in range(count)])]
    ppermute x1, starting transfers between devices: 1.05 us -> 2.56 us  [on_device(): raw1 = lax.ppermute(line, ('row', 'col'), others)]
    ppermute x1, waiting for transfers between devices: 1.19 us -> 2.26 us  [on_device(): message1 = lax.ppermute(longer, ('row', 'col'), others)]
    ppermute x1, waiting for transfers between devices: 0.01 us -> 0.91 us  [on_device(): message0 = lax.ppermute(message, ('row', 'col'), pairs)]
    ppermute x1, starting transfers between devices: 0.78 us -> 0.15 us  [on_device(): message1 = lax.ppermute(longer, ('row', 'col'), others)]
    ppermute x1, starting transfers between devices: 0.59 us -> 0.01 us  [on_device(): raw0 = lax.ppermute(line, ('row', 'col'), pairs)]
    pallas_call x1, Pallas kernels: 4.42 us -> 3.95 us  [on_device(): pl.pallas_call(functools.partial(denoise_kernel, tile, reach), out_shape=...]
    pallas_call x0 -> x1, Pallas kernels: none -> 0.4 us  [on_device(): pl.pallas_call(functools.partial(neighbour_kernel, reach), out_shape=jax....]
  transfers between devices with their start and end apart: 7 -> 7, of which waited for: 2 -> 2; matrix products, arithmetic and copies ran while one was open for 0% -> 0% of each run, Pallas kernels for 11% -> 13%
where the time goes in v12:
time: 21.4 us; the launch traced here: 21.2 us
  starting transfers between devices  9.88 us (46%)
  Pallas kernels  8.05 us (38%)
  waiting for transfers between devices  3.19 us (15%)
    ppermute x3, starting transfers between devices, around(): lax.ppermute(x, 'band', [(i, (i + shift) % count) for i in range(count)])  6.11 us
    pallas_call x1, Pallas kernels, on_device(): pl.pallas_call(functools.partial(denoise_kernel, tile, reach), out_shape=...  3.95 us
    ppermute x1, starting transfers between devices, on_device(): raw1 = lax.ppermute(line, ('row', 'col'), others)  2.56 us
    ppermute x1, waiting for transfers between devices, on_device(): message1 = lax.ppermute(longer, ('row', 'col'), others)  2.26 us
    pallas_call x1, Pallas kernels, on_device(): pl.pallas_call(weights_kernel, out_shape=(jax.ShapeDtypeStruct((16 * ch,...  1.79 us
    pallas_call x1, Pallas kernels, on_device(): pl.pallas_call(functools.partial(project_kernel, reach), out_shape=(jax.S...  1.41 us
    ppermute x1, starting transfers between devices, on_device(): message0 = lax.ppermute(message, ('row', 'col'), pairs)  1.05 us
    ppermute x1, waiting for transfers between devices, on_device(): message0 = lax.ppermute(message, ('row', 'col'), pairs)  0.91 us
  transfers between devices with their start and end apart: 7, of which 2 were waited for; matrix products, arithmetic and copies ran while one was open for 0% of the time, Pallas kernels for 13%

profile of v12, /device:TPU:0, one launch (start us, length us, event | category | flops | bytes accessed | tf_op | source)
XLA Modules:
  0.0 21.2 jit_solution(130269764246450360)
XLA Ops:
  0.0 1.4 %project.1 = (bf16[80,128]{1,0:T(8,128)(2,1)S(1)}, bf16[224,128]{1,0:T(8,128)(2,1)S(1)}, bf16[224,128]{1,0:T(8,128)(2,1)S(1)}, bf16[24,4096]{1,0:T(8,128)(2,1)S(...) custom-call(bf16[22,4096]{1,0:T(8,128)(2,1)} %bitcast.7, ...), custom_call_target="tpu_custom_call" | custom-call | tf_op jit(solution)/shard_map/project/pallas_call | solution.py:539
  1.4 3.1 %collective-permute-start = (bf16[224,128]{1,0:T(8,128)(2,1)S(1)}, bf16[224,128]{1,0:T(8,128)(2,1)S(1)}, u32[]{:S(2)}, u32[]{:S(2)}) collective-permute-start(bf16[224,128]{1,0:T(8,128)(2,1)S(1)} %get-tuple-element.28), channel_id=1, source_target_pairs={{0,8},{8,16},{16,24},{24,0},{1,9},{9,17},{17,25},{25,1},{2,10},{10... | collective-permute-start | bytes 172040 | tf_op jit(solution)/shard_map/ppermute | solution.py:560
  4.5 2.1 %collective-permute-start.1 = (bf16[224,128]{1,0:T(8,128)(2,1)S(1)}, bf16[224,128]{1,0:T(8,128)(2,1)S(1)}, u32[]{:S(2)}, u32[]{:S(2)}) collective-permute-start(bf16[224,128]{1,0:T(8,128)(2,1)S(1)} %get-tuple-element.29), channel_id=1, source_target_pairs={{0,24},{8,0},{16,8},{24,16},{1,25},{9,1},{17,9},{25,17},{2,26},{10... | collective-permute-start | bytes 172040 | tf_op jit(solution)/shard_map/ppermute | solution.py:560
  6.6 0.9 %collective-permute-start.2 = (bf16[80,128]{1,0:T(8,128)(2,1)S(1)}, bf16[80,128]{1,0:T(8,128)(2,1)S(1)}, u32[]{:S(2)}, u32[]{:S(2)}) collective-permute-start(bf16[80,128]{1,0:T(8,128)(2,1)S(1)} %get-tuple-element.21._.own_ref), channel_id=1, source_target_pairs={{0,16},{8,24},{16,0},{24,8},{1,17},{9,25},{17,1},{25,9},{2,18},{10... | collective-permute-start | bytes 61448 | tf_op jit(solution)/shard_map/ppermute | solution.py:560
  7.5 0.0 collective-permute-start.3
  7.5 2.6 %collective-permute-start.5 = (bf16[24,4096]{1,0:T(8,128)(2,1)S(1)}, bf16[24,4096]{1,0:T(8,128)(2,1)S(1)}, u32[]{:S(2)}, u32[]{:S(2)}) collective-permute-start(bf16[24,4096]{1,0:T(8,128)(2,1)S(1)} %gate.1._.line_ref), channel_id=1, source_target_pairs={{0,7},{1,2},{2,1},{3,4},{4,3},{5,6},{6,5},{7,0},{8,15},{9,10},{10,... | collective-permute-start | bytes 589832 | tf_op jit(solution)/shard_map/ppermute | solution.py:581
  10.1 1.8 %weights.1 = (bf16[256,160]{1,0:T(8,128)(2,1)S(1)}, bf16[192,160]{1,0:T(8,128)(2,1)S(1)}, bf16[128,240]{1,0:T(8,128)(2,1)S(1)}, bf16[128,208]{1,0:T(8,128)(2,1)S(1)}, f32[128,128]{1,0:T(8,128)S(1)}) custom-call(bf16[24,4096]{1,0:T(8,128)(2,1)S(1)} %gate.1._.line_ref, bf16[16,9]{1,0:T(8,128)(2,1)} %sw_in.1, f32[1,16]{1,0:T(1,128)} %bitcast.10, ...), custom_call_target="tpu_custom_call" | custom-call | tf_op jit(solution)/shard_map/weights/pallas_call | solution.py:592
  11.9 0.0 collective-permute-done.2.rest_refs_0_
  11.9 0.0 collective-permute-done.below_ref
  11.9 0.0 collective-permute-done.1.above_ref
  11.9 0.5 %update.1 = (bf16[32,4096]{1,0:T(8,128)(2,1)S(1)}, bf16[288,128]{1,0:T(8,128)(2,1)S(1)}, bf16[304,128]{1,0:T(8,128)(2,1)S(1)}) custom-call(bf16[24,4096]{1,0:T(8,128)(2,1)S(1)} %gate.1._.line_ref, s32[1,4096]{1,0:T(1,128)S(1)} %get-tuple-element.24.ap_ref, f32[1,4444]{1,0:T(1,128)S(1)} %get-tuple-element.25.meas_ref, ...), custom_call_target="tpu_custom_call" | custom-call | flops 10000000000 | bytes 40000000 | tf_op jit(solution)/shard_map/update/pallas_call | solution.py:610
  12.4 0.1 collective-permute-start.6
  12.6 1.1 %collective-permute-start.4 = (bf16[288,128]{1,0:T(8,128)(2,1)S(1)}, bf16[288,128]{1,0:T(8,128)(2,1)S(1)}, u32[]{:S(2)}, u32[]{:S(2)}) collective-permute-start(bf16[288,128]{1,0:T(8,128)(2,1)S(1)} %get-tuple-element.31._), channel_id=1, source_target_pairs={{0,1},{1,0},{2,3},{3,2},{4,5},{5,4},{6,7},{7,6},{8,9},{9,8},{10,11... | collective-permute-start | bytes 221192 | tf_op jit(solution)/shard_map/ppermute | solution.py:631
  13.6 0.9 %collective-permute-done.4.msg_ref = bf16[288,128]{1,0:T(8,128)(2,1)S(1)} collective-permute-done((bf16[288,128]{1,0:T(8,128)(2,1)S(1)}, bf16[288,128]{1,0:T(8,128)(2,1)S(1)}, u32[]{:S(2)}, u32[]{:S(2)}) %collective-permute-start.4) | collective-permute-done | bytes 73760 | tf_op jit(solution)/shard_map/ppermute | solution.py:631
  14.6 0.0 collective-permute-done.3.raw_ref
  14.6 0.4 %partner.1.near0 = bf16[32,4096]{1,0:T(8,128)(2,1)S(1)} custom-call(s32[1,22]{1,0:T(1,128)S(1)} %get-tuple-element.26.shear_ref, f32[1,22]{1,0:T(1,128)S(1)} %get-tuple-element.27.step_ref, bf16[24,4096]{1,0:T(8,128)(2,1)S(1)} %collective-permute-done.3.raw_ref, bf16[288,128]{1,0:T(8,128)(2,1)S(1)} %collective-permute-done.4.msg_ref, ...), custom_call_target="tpu_custom_call" | custom-call | flops 1 | bytes 1 | tf_op jit(solution)/shard_map/partner/pallas_call | solution.py:634
  15.0 2.3 %collective-permute-done.6.msg_ref = bf16[304,128]{1,0:T(8,128)(2,1)S(1)} collective-permute-done((bf16[304,128]{1,0:T(8,128)(2,1)S(1)}, bf16[304,128]{1,0:T(8,128)(2,1)S(1)}, u32[]{:S(2)}, u32[]{:S(2)}) %collective-permute-start.6) | collective-permute-done | bytes 77856 | tf_op jit(solution)/shard_map/ppermute | solution.py:632
  17.2 0.0 collective-permute-done.5.raw_ref
  17.2 3.9 %denoise.1 = bf16[22,4096]{1,0:T(8,128)(2,1)} custom-call(f32[128,128]{1,0:T(8,128)S(1)} %get-tuple-element.23._.ow_ref, bf16[32,4096]{1,0:T(8,128)(2,1)S(1)} %get-tuple-element.30.mid_ref, s32[1,22]{1,0:T(1,128)S(1)} %get-tuple-element.26.shear_ref, f32[1,22]{1,0:T(1,128)S(1)} %get-tuple-element.27.step_ref, bf16[32,4096]{1,0:T(8,128)(2,1)S(1)} %partner.1.near0, ...), custom_call_target="tpu_custom_call" | custom-call | tf_op jit(solution)/shard_map/denoise/pallas_call | solution.py:646
  (1 shorter events, 0.0 us)
Async XLA Ops:
  1.4 10.5 %collective-permute-start = (bf16[224,128]{1,0:T(8,128)(2,1)S(1)}, bf16[224,128]{1,0:T(8,128)(2,1)S(1)}, u32[]{:S(2)}, u32[]{:S(2)}) collective-permute-start(bf16[224,128]{1,0:T(8,128)(2,1)S(1)} %get-tuple-element.28), channel_id=1, source_target_pairs={{0,8},{8,16},{16,24},{24,0},{1,9},{9,17},{17,25},{25,1},{2,10},{10... | collective-permute-start | bytes 172040 | tf_op jit(solution)/shard_map/ppermute | solution.py:560
  4.5 7.4 %collective-permute-start.1 = (bf16[224,128]{1,0:T(8,128)(2,1)S(1)}, bf16[224,128]{1,0:T(8,128)(2,1)S(1)}, u32[]{:S(2)}, u32[]{:S(2)}) collective-permute-start(bf16[224,128]{1,0:T(8,128)(2,1)S(1)} %get-tuple-element.29), channel_id=1, source_target_pairs={{0,24},{8,0},{16,8},{24,16},{1,25},{9,1},{17,9},{25,17},{2,26},{10... | collective-permute-start | bytes 172040 | tf_op jit(solution)/shard_map/ppermute | solution.py:560
  6.6 5.3 %collective-permute-start.2 = (bf16[80,128]{1,0:T(8,128)(2,1)S(1)}, bf16[80,128]{1,0:T(8,128)(2,1)S(1)}, u32[]{:S(2)}, u32[]{:S(2)}) collective-permute-start(bf16[80,128]{1,0:T(8,128)(2,1)S(1)} %get-tuple-element.21._.own_ref), channel_id=1, source_target_pairs={{0,16},{8,24},{16,0},{24,8},{1,17},{9,25},{17,1},{25,9},{2,18},{10... | collective-permute-start | bytes 61448 | tf_op jit(solution)/shard_map/ppermute | solution.py:560
  7.5 7.0 %collective-permute-start.3 = (bf16[24,4096]{1,0:T(8,128)(2,1)S(1)}, bf16[24,4096]{1,0:T(8,128)(2,1)S(1)}, u32[]{:S(2)}, u32[]{:S(2)}) collective-permute-start(bf16[24,4096]{1,0:T(8,128)(2,1)S(1)} %gate.1._.line_ref), channel_id=1, source_target_pairs={{0,1},{1,0},{2,3},{3,2},{4,5},{5,4},{6,7},{7,6},{8,9},{9,8},{10,11... | collective-permute-start | bytes 589832 | tf_op jit(solution)/shard_map/ppermute | solution.py:580
  7.5 9.7 %collective-permute-start.5 = (bf16[24,4096]{1,0:T(8,128)(2,1)S(1)}, bf16[24,4096]{1,0:T(8,128)(2,1)S(1)}, u32[]{:S(2)}, u32[]{:S(2)}) collective-permute-start(bf16[24,4096]{1,0:T(8,128)(2,1)S(1)} %gate.1._.line_ref), channel_id=1, source_target_pairs={{0,7},{1,2},{2,1},{3,4},{4,3},{5,6},{6,5},{7,0},{8,15},{9,10},{10,... | collective-permute-start | bytes 589832 | tf_op jit(solution)/shard_map/ppermute | solution.py:581
  12.4 4.8 %collective-permute-start.6 = (bf16[304,128]{1,0:T(8,128)(2,1)S(1)}, bf16[304,128]{1,0:T(8,128)(2,1)S(1)}, u32[]{:S(2)}, u32[]{:S(2)}) collective-permute-start(bf16[304,128]{1,0:T(8,128)(2,1)S(1)} %get-tuple-element.32), channel_id=1, source_target_pairs={{0,7},{1,2},{2,1},{3,4},{4,3},{5,6},{6,5},{7,0},{8,15},{9,10},{10,... | collective-permute-start | bytes 233480 | tf_op jit(solution)/shard_map/ppermute | solution.py:632
  12.6 2.0 %collective-permute-start.4 = (bf16[288,128]{1,0:T(8,128)(2,1)S(1)}, bf16[288,128]{1,0:T(8,128)(2,1)S(1)}, u32[]{:S(2)}, u32[]{:S(2)}) collective-permute-start(bf16[288,128]{1,0:T(8,128)(2,1)S(1)} %get-tuple-element.31._), channel_id=1, source_target_pairs={{0,1},{1,0},{2,3},{3,2},{4,5},{5,4},{6,7},{7,6},{8,9},{9,8},{10,11... | collective-permute-start | bytes 221192 | tf_op jit(solution)/shard_map/ppermute | solution.py:631

commit v13 on v12

--- a/solution.py
+++ b/solution.py
@@ -572,13 +572,12 @@
         compiler_params=pltpu.CompilerParams(vmem_limit_bytes=2**20),
         name="gate",
     )(part, kept[0])
-    kept[0] = line
 
     lines = lax.axis_size(("row", "col"))
     pairs = [(i, i ^ 1) for i in range(lines)]
     others = [(i, (i - 1 + i % 2 * 2) % lines) for i in range(lines)]
+    raw1 = lax.ppermute(kept[0], ("row", "col"), others)
     raw0 = lax.ppermute(line, ("row", "col"), pairs)
-    raw1 = lax.ppermute(line, ("row", "col"), others)
 
     small = (
         spatial_weight,

time: 21.4 us -> 20.8 us (0.972)
  waiting for transfers between devices: 3.19 us -> 2.85 us
    ppermute x1, starting transfers between devices: 2.56 us -> 1.05 us  [on_device(): raw1 = lax.ppermute(kept[0], ('row', 'col'), others)]
    ppermute x1, starting transfers between devices: 0.15 us -> 0.91 us  [on_device(): message1 = lax.ppermute(longer, ('row', 'col'), others)]
    ppermute x1, starting transfers between devices: 0.01 us -> 0.65 us  [on_device(): raw0 = lax.ppermute(line, ('row', 'col'), pairs)]
    ppermute x1, waiting for transfers between devices: 2.26 us -> 1.72 us  [on_device(): message1 = lax.ppermute(longer, ('row', 'col'), others)]
  transfers between devices with their start and end apart: 7 -> 7, of which waited for: 2 -> 3; matrix products, arithmetic and copies ran while one was open for 0% -> 0% of each run, Pallas kernels for 13% -> 13%
where the time goes in v13:
time: 20.8 us; the launch traced here: 20.6 us
  starting transfers between devices  9.67 us (46%)
  Pallas kernels  8.05 us (39%)
  waiting for transfers between devices  2.85 us (14%)
    ppermute x3, starting transfers between devices, around(): lax.ppermute(x, 'band', [(i, (i + shift) % count) for i in range(count)])  6.11 us
    pallas_call x1, Pallas kernels, on_device(): pl.pallas_call(functools.partial(denoise_kernel, tile, reach), out_shape=...  3.95 us
    pallas_call x1, Pallas kernels, on_device(): pl.pallas_call(weights_kernel, out_shape=(jax.ShapeDtypeStruct((16 * ch,...  1.79 us
    ppermute x1, waiting for transfers between devices, on_device(): message1 = lax.ppermute(longer, ('row', 'col'), others)  1.72 us
    pallas_call x1, Pallas kernels, on_device(): pl.pallas_call(functools.partial(project_kernel, reach), out_shape=(jax.S...  1.4 us
    ppermute x1, starting transfers between devices, on_device(): raw1 = lax.ppermute(kept[0], ('row', 'col'), others)  1.05 us
    ppermute x1, starting transfers between devices, on_device(): message0 = lax.ppermute(message, ('row', 'col'), pairs)  0.95 us
    ppermute x1, waiting for transfers between devices, on_device(): message0 = lax.ppermute(message, ('row', 'col'), pairs)  0.91 us
  transfers between devices with their start and end apart: 7, of which 3 were waited for; matrix products, arithmetic and copies ran while one was open for 0% of the time, Pallas kernels for 13%

profile of v13, /device:TPU:0, one launch (start us, length us, event | category | flops | bytes accessed | tf_op | source)
XLA Modules:
  0.0 20.6 jit_solution(16695172565865835115)
XLA Ops:
  0.0 1.4 %project.1 = (bf16[80,128]{1,0:T(8,128)(2,1)S(1)}, bf16[224,128]{1,0:T(8,128)(2,1)S(1)}, bf16[224,128]{1,0:T(8,128)(2,1)S(1)}, bf16[24,4096]{1,0:T(8,128)(2,1)S(...) custom-call(bf16[22,4096]{1,0:T(8,128)(2,1)} %bitcast.7, ...), custom_call_target="tpu_custom_call" | custom-call | tf_op jit(solution)/shard_map/project/pallas_call | solution.py:539
  1.4 3.1 %collective-permute-start = (bf16[224,128]{1,0:T(8,128)(2,1)S(1)}, bf16[224,128]{1,0:T(8,128)(2,1)S(1)}, u32[]{:S(2)}, u32[]{:S(2)}) collective-permute-start(bf16[224,128]{1,0:T(8,128)(2,1)S(1)} %get-tuple-element.28), channel_id=1, source_target_pairs={{0,8},{8,16},{16,24},{24,0},{1,9},{9,17},{17,25},{25,1},{2,10},{10... | collective-permute-start | bytes 172040 | tf_op jit(solution)/shard_map/ppermute | solution.py:560
  4.5 2.1 %collective-permute-start.1 = (bf16[224,128]{1,0:T(8,128)(2,1)S(1)}, bf16[224,128]{1,0:T(8,128)(2,1)S(1)}, u32[]{:S(2)}, u32[]{:S(2)}) collective-permute-start(bf16[224,128]{1,0:T(8,128)(2,1)S(1)} %get-tuple-element.29), channel_id=1, source_target_pairs={{0,24},{8,0},{16,8},{24,16},{1,25},{9,1},{17,9},{25,17},{2,26},{10... | collective-permute-start | bytes 172040 | tf_op jit(solution)/shard_map/ppermute | solution.py:560
  6.6 0.9 %collective-permute-start.2 = (bf16[80,128]{1,0:T(8,128)(2,1)S(1)}, bf16[80,128]{1,0:T(8,128)(2,1)S(1)}, u32[]{:S(2)}, u32[]{:S(2)}) collective-permute-start(bf16[80,128]{1,0:T(8,128)(2,1)S(1)} %get-tuple-element.21._.own_ref), channel_id=1, source_target_pairs={{0,16},{8,24},{16,0},{24,8},{1,17},{9,25},{17,1},{25,9},{2,18},{10... | collective-permute-start | bytes 61448 | tf_op jit(solution)/shard_map/ppermute | solution.py:560
  7.5 1.0 %collective-permute-start.5 = (bf16[24,4096]{1,0:T(8,128)(2,1)S(1)}, bf16[24,4096]{1,0:T(8,128)(2,1)S(1)}, u32[]{:S(2)}, u32[]{:S(2)}) collective-permute-start(bf16[24,4096]{1,0:T(8,128)(2,1)S(1)} %get-tuple-element.22.line_ref), channel_id=1, source_target_pairs={{0,7},{1,2},{2,1},{3,4},{4,3},{5,6},{6,5},{7,0},{8,15},{9,10},{10,... | collective-permute-start | bytes 589832 | tf_op jit(solution)/shard_map/ppermute | solution.py:579
  8.6 0.7 %collective-permute-start.3 = (bf16[24,4096]{1,0:T(8,128)(2,1)S(1)}, bf16[24,4096]{1,0:T(8,128)(2,1)S(1)}, u32[]{:S(2)}, u32[]{:S(2)}) collective-permute-start(bf16[24,4096]{1,0:T(8,128)(2,1)S(1)} %gate.1._), channel_id=1, source_target_pairs={{0,1},{1,0},{2,3},{3,2},{4,5},{5,4},{6,7},{7,6},{8,9},{9,8},{10,11... | collective-permute-start | bytes 589832 | tf_op jit(solution)/shard_map/ppermute | solution.py:580
  9.3 1.8 %weights.1 = (bf16[256,160]{1,0:T(8,128)(2,1)S(1)}, bf16[192,160]{1,0:T(8,128)(2,1)S(1)}, bf16[128,240]{1,0:T(8,128)(2,1)S(1)}, bf16[128,208]{1,0:T(8,128)(2,1)S(1)}, f32[128,128]{1,0:T(8,128)S(1)}) custom-call(bf16[24,4096]{1,0:T(8,128)(2,1)S(1)} %gate.1._, bf16[16,9]{1,0:T(8,128)(2,1)} %sw_in.1, f32[1,16]{1,0:T(1,128)} %bitcast.10, ...), custom_call_target="tpu_custom_call" | custom-call | tf_op jit(solution)/shard_map/weights/pallas_call | solution.py:591
  11.1 0.2 %collective-permute-done.2.rest_refs_0_ = bf16[80,128]{1,0:T(8,128)(2,1)S(1)} collective-permute-done((bf16[80,128]{1,0:T(8,128)(2,1)S(1)}, bf16[80,128]{1,0:T(8,128)(2,1)S(1)}, u32[]{:S(2)}, u32[]{:S(2)}) %collective-permute-start.2) | collective-permute-done | bytes 20512 | tf_op jit(solution)/shard_map/ppermute | solution.py:560
  11.3 0.0 collective-permute-done.below_ref
  11.3 0.0 collective-permute-done.1.above_ref
  11.3 0.5 %update.1 = (bf16[32,4096]{1,0:T(8,128)(2,1)S(1)}, bf16[288,128]{1,0:T(8,128)(2,1)S(1)}, bf16[304,128]{1,0:T(8,128)(2,1)S(1)}) custom-call(bf16[24,4096]{1,0:T(8,128)(2,1)S(1)} %get-tuple-element.22.line_ref, s32[1,4096]{1,0:T(1,128)S(1)} %get-tuple-element.24.ap_ref, f32[1,4444]{1,0:T(1,128)S(1)} %get-tuple-element.25.meas_ref, ...), custom_call_target="tpu_custom_call" | custom-call | flops 10000000000 | bytes 40000000 | tf_op jit(solution)/shard_map/update/pallas_call | solution.py:609
  11.8 0.9 %collective-permute-start.6 = (bf16[304,128]{1,0:T(8,128)(2,1)S(1)}, bf16[304,128]{1,0:T(8,128)(2,1)S(1)}, u32[]{:S(2)}, u32[]{:S(2)}) collective-permute-start(bf16[304,128]{1,0:T(8,128)(2,1)S(1)} %get-tuple-element.32), channel_id=1, source_target_pairs={{0,7},{1,2},{2,1},{3,4},{4,3},{5,6},{6,5},{7,0},{8,15},{9,10},{10,... | collective-permute-start | bytes 233480 | tf_op jit(solution)/shard_map/ppermute | solution.py:631
  12.7 0.9 %collective-permute-start.4 = (bf16[288,128]{1,0:T(8,128)(2,1)S(1)}, bf16[288,128]{1,0:T(8,128)(2,1)S(1)}, u32[]{:S(2)}, u32[]{:S(2)}) collective-permute-start(bf16[288,128]{1,0:T(8,128)(2,1)S(1)} %get-tuple-element.31._), channel_id=1, source_target_pairs={{0,1},{1,0},{2,3},{3,2},{4,5},{5,4},{6,7},{7,6},{8,9},{9,8},{10,11... | collective-permute-start | bytes 221192 | tf_op jit(solution)/shard_map/ppermute | solution.py:630
  13.6 0.9 %collective-permute-done.4.msg_ref = bf16[288,128]{1,0:T(8,128)(2,1)S(1)} collective-permute-done((bf16[288,128]{1,0:T(8,128)(2,1)S(1)}, bf16[288,128]{1,0:T(8,128)(2,1)S(1)}, u32[]{:S(2)}, u32[]{:S(2)}) %collective-permute-start.4) | collective-permute-done | bytes 73760 | tf_op jit(solution)/shard_map/ppermute | solution.py:630
  14.6 0.0 collective-permute-done.3.raw_ref
  14.6 0.4 %partner.1.near0 = bf16[32,4096]{1,0:T(8,128)(2,1)S(1)} custom-call(s32[1,22]{1,0:T(1,128)S(1)} %get-tuple-element.26.shear_ref, f32[1,22]{1,0:T(1,128)S(1)} %get-tuple-element.27.step_ref, bf16[24,4096]{1,0:T(8,128)(2,1)S(1)} %collective-permute-done.3.raw_ref, bf16[288,128]{1,0:T(8,128)(2,1)S(1)} %collective-permute-done.4.msg_ref, ...), custom_call_target="tpu_custom_call" | custom-call | flops 1 | bytes 1 | tf_op jit(solution)/shard_map/partner/pallas_call | solution.py:633
  15.0 1.7 %collective-permute-done.6.msg_ref = bf16[304,128]{1,0:T(8,128)(2,1)S(1)} collective-permute-done((bf16[304,128]{1,0:T(8,128)(2,1)S(1)}, bf16[304,128]{1,0:T(8,128)(2,1)S(1)}, u32[]{:S(2)}, u32[]{:S(2)}) %collective-permute-start.6) | collective-permute-done | bytes 77856 | tf_op jit(solution)/shard_map/ppermute | solution.py:631
  16.7 0.0 collective-permute-done.5.raw_ref
  16.7 3.9 %denoise.1 = bf16[22,4096]{1,0:T(8,128)(2,1)} custom-call(f32[128,128]{1,0:T(8,128)S(1)} %get-tuple-element.23._.ow_ref, bf16[32,4096]{1,0:T(8,128)(2,1)S(1)} %get-tuple-element.30.mid_ref, s32[1,22]{1,0:T(1,128)S(1)} %get-tuple-element.26.shear_ref, f32[1,22]{1,0:T(1,128)S(1)} %get-tuple-element.27.step_ref, bf16[32,4096]{1,0:T(8,128)(2,1)S(1)} %partner.1.near0, ...), custom_call_target="tpu_custom_call" | custom-call | tf_op jit(solution)/shard_map/denoise/pallas_call | solution.py:645
  (2 shorter events, 0.0 us)
Async XLA Ops:
  1.4 9.9 %collective-permute-start = (bf16[224,128]{1,0:T(8,128)(2,1)S(1)}, bf16[224,128]{1,0:T(8,128)(2,1)S(1)}, u32[]{:S(2)}, u32[]{:S(2)}) collective-permute-start(bf16[224,128]{1,0:T(8,128)(2,1)S(1)} %get-tuple-element.28), channel_id=1, source_target_pairs={{0,8},{8,16},{16,24},{24,0},{1,9},{9,17},{17,25},{25,1},{2,10},{10... | collective-permute-start | bytes 172040 | tf_op jit(solution)/shard_map/ppermute | solution.py:560
  4.5 6.8 %collective-permute-start.1 = (bf16[224,128]{1,0:T(8,128)(2,1)S(1)}, bf16[224,128]{1,0:T(8,128)(2,1)S(1)}, u32[]{:S(2)}, u32[]{:S(2)}) collective-permute-start(bf16[224,128]{1,0:T(8,128)(2,1)S(1)} %get-tuple-element.29), channel_id=1, source_target_pairs={{0,24},{8,0},{16,8},{24,16},{1,25},{9,1},{17,9},{25,17},{2,26},{10... | collective-permute-start | bytes 172040 | tf_op jit(solution)/shard_map/ppermute | solution.py:560
  6.6 4.7 %collective-permute-start.2 = (bf16[80,128]{1,0:T(8,128)(2,1)S(1)}, bf16[80,128]{1,0:T(8,128)(2,1)S(1)}, u32[]{:S(2)}, u32[]{:S(2)}) collective-permute-start(bf16[80,128]{1,0:T(8,128)(2,1)S(1)} %get-tuple-element.21._.own_ref), channel_id=1, source_target_pairs={{0,16},{8,24},{16,0},{24,8},{1,17},{9,25},{17,1},{25,9},{2,18},{10... | collective-permute-start | bytes 61448 | tf_op jit(solution)/shard_map/ppermute | solution.py:560
  7.5 9.1 %collective-permute-start.5 = (bf16[24,4096]{1,0:T(8,128)(2,1)S(1)}, bf16[24,4096]{1,0:T(8,128)(2,1)S(1)}, u32[]{:S(2)}, u32[]{:S(2)}) collective-permute-start(bf16[24,4096]{1,0:T(8,128)(2,1)S(1)} %get-tuple-element.22.line_ref), channel_id=1, source_target_pairs={{0,7},{1,2},{2,1},{3,4},{4,3},{5,6},{6,5},{7,0},{8,15},{9,10},{10,... | collective-permute-start | bytes 589832 | tf_op jit(solution)/shard_map/ppermute | solution.py:579
  8.6 6.0 %collective-permute-start.3 = (bf16[24,4096]{1,0:T(8,128)(2,1)S(1)}, bf16[24,4096]{1,0:T(8,128)(2,1)S(1)}, u32[]{:S(2)}, u32[]{:S(2)}) collective-permute-start(bf16[24,4096]{1,0:T(8,128)(2,1)S(1)} %gate.1._), channel_id=1, source_target_pairs={{0,1},{1,0},{2,3},{3,2},{4,5},{5,4},{6,7},{7,6},{8,9},{9,8},{10,11... | collective-permute-start | bytes 589832 | tf_op jit(solution)/shard_map/ppermute | solution.py:580
  11.8 4.9 %collective-permute-start.6 = (bf16[304,128]{1,0:T(8,128)(2,1)S(1)}, bf16[304,128]{1,0:T(8,128)(2,1)S(1)}, u32[]{:S(2)}, u32[]{:S(2)}) collective-permute-start(bf16[304,128]{1,0:T(8,128)(2,1)S(1)} %get-tuple-element.32), channel_id=1, source_target_pairs={{0,7},{1,2},{2,1},{3,4},{4,3},{5,6},{6,5},{7,0},{8,15},{9,10},{10,... | collective-permute-start | bytes 233480 | tf_op jit(solution)/shard_map/ppermute | solution.py:631
  12.7 1.9 %collective-permute-start.4 = (bf16[288,128]{1,0:T(8,128)(2,1)S(1)}, bf16[288,128]{1,0:T(8,128)(2,1)S(1)}, u32[]{:S(2)}, u32[]{:S(2)}) collective-permute-start(bf16[288,128]{1,0:T(8,128)(2,1)S(1)} %get-tuple-element.31._), channel_id=1, source_target_pairs={{0,1},{1,0},{2,3},{3,2},{4,5},{5,4},{6,7},{7,6},{8,9},{9,8},{10,11... | collective-permute-start | bytes 221192 | tf_op jit(solution)/shard_map/ppermute | solution.py:630

commit v14 on v13

--- a/solution.py
+++ b/solution.py
@@ -138,32 +138,17 @@
 
 
 def update_kernel(
-    reach,
-    fars,
-    line_ref,
-    ap_ref,
-    meas_ref,
-    shear_ref,
-    step_ref,
-    own_ref,
-    below_ref,
-    above_ref,
-    _,
-    *rest_refs,
+    reach, fars, ap_ref, meas_ref, own_ref, below_ref, above_ref, _, *rest_refs
 ):
     far_refs = rest_refs[:fars]
-    out_ref, msg_ref, long_ref, raw, meas, rest_row = rest_refs[fars:]
-    groups = line_ref.shape[0] // SUB
-    cols = line_ref.shape[1]
+    msg_ref, long_ref, meas, rest_row = rest_refs[fars:]
+    cols = ap_ref.shape[1]
     inner = cols // LANES
     half = inner // 2
     tall = own_ref.shape[0] // 2
     outer = -(-meas_ref.shape[1] // LANES)
-    raw[...] = line_ref[...].astype(F32)
     meas[:, (outer - 1) * LANES :] = jnp.zeros((1, LANES), F32)
     meas[:, 0 : meas_ref.shape[1]] = meas_ref[...]
-    shear_f = column(shear_ref[...].astype(F32), groups * SUB)
-    step_f = column(step_ref[...], groups * SUB)
     lane, sub = lanes_of(), rows_of()
     below = below_ref[...].astype(F32)
     above = above_ref[...].astype(F32)
@@ -189,41 +174,32 @@
 
     side = 2 * tall + half * SUB
     side = jnp.where(sub < 3, above[side : side + SUB], below[side : side + SUB])
-    shear_cols = [shear_f[g * SUB : (g + 1) * SUB] for g in range(groups)]
-    step_cols = [step_f[g * SUB : (g + 1) * SUB] for g in range(groups)]
     inside = rows_of((SUB, 1)) < 6
-    shear_cols.append(jnp.where(inside, 2.0 * side[:, 0:1] + side[:, 1:2], 0.0))
-    step_cols.append(jnp.where(inside, side[:, 2:3] + side[:, 3:4] + side[:, 4:5], 0.0))
-    index, delay, steps = [], [], []
-    for g in range(groups + 1):
-        s = jnp.broadcast_to(shear_cols[g].astype(I32), (SUB, LANES))
-        rest = s & (LANES - 1)
-        index.append((lane + rest) & (LANES - 1))
-        delay.append((s >> 7) + jnp.where(lane + rest >= LANES, 1, 0))
-        steps.append(jnp.broadcast_to(step_cols[g], (SUB, LANES)))
+    shear = jnp.where(inside, 2.0 * side[:, 0:1] + side[:, 1:2], 0.0)
+    step = jnp.where(inside, side[:, 2:3] + side[:, 3:4] + side[:, 4:5], 0.0)
+    shear = jnp.broadcast_to(shear.astype(I32), (SUB, LANES))
+    step = jnp.broadcast_to(step, (SUB, LANES))
+    rest = shear & (LANES - 1)
+    index = (lane + rest) & (LANES - 1)
+    delay = (shear >> 7) + jnp.where(lane + rest >= LANES, 1, 0)
     tiles = []
-    turned = [[] for _ in range(groups + 1)]
+    turned = []
     for p in range(outer + 1):
         if p < outer:
             residual = jnp.broadcast_to(rest_row[p : p + 1, :], (SUB, LANES))
+            turned.append(turn(residual, index))
         else:
             residual = jnp.zeros((SUB, LANES), F32)
+            turned.append(residual)
         lost = residual - residual.astype(BF16).astype(F32)
         tiles.append(jnp.where(sub < 7, residual, lost))
-        for g in range(groups + 1):
-            turned[g].append(turn(residual, index[g]) if p < outer else residual)
         q = p - (reach - 1)
         if q < 0 or q >= inner:
             continue
         here = slice(q * LANES, (q + 1) * LANES)
         open_q = jnp.broadcast_to(ap_ref[:, here].astype(F32), (SUB, LANES))
-        pieces = []
-        for g in range(groups + 1):
-            pulled = choose(delay[g], turned[g][q : q + reach])
-            base = raw[g * SUB : (g + 1) * SUB, here] if g < groups else halo(q)
-            pieces.append(base + pulled * open_q * steps[g])
-        out_ref[:, here] = jnp.concatenate(pieces, axis=0).astype(BF16)
-        tiles[q] = jnp.where(sub < 6, pieces[-1], tiles[q])
+        value = halo(q) + choose(delay, turned[q : q + reach]) * open_q * step
+        tiles[q] = jnp.where(sub < 6, value, tiles[q])
     words = jnp.concatenate(tiles, axis=0).astype(BF16)
     msg_ref[...] = words
     long_ref[0 : words.shape[0], :] = words
@@ -606,17 +582,15 @@
     )(line, *in_hbm(small))
 
     words = (outer + 1) * SUB
-    updated, message, longer = pl.pallas_call(
+    message, longer = pl.pallas_call(
         functools.partial(update_kernel, reach, len(far)),
         out_shape=(
-            jax.ShapeDtypeStruct((slots, cols), BF16),
             jax.ShapeDtypeStruct((words, LANES), BF16),
             jax.ShapeDtypeStruct((words + EXTRA, LANES), BF16),
         ),
-        in_specs=vmem(8) + [ANY] + vmem(len(far)),
-        out_specs=tuple(vmem(3)),
+        in_specs=vmem(5) + [ANY] + vmem(len(far)),
+        out_specs=tuple(vmem(2)),
         scratch_shapes=[
-            pltpu.VMEM((groups * SUB, cols), F32),
             pltpu.VMEM((1, outer * LANES), F32),
             pltpu.VMEM((tall, LANES), F32),
         ],
@@ -625,21 +599,25 @@
             flops=10**10, bytes_accessed=4 * 10**7, transcendentals=0
         ),
         name="update",
-    )(*kept, part, below, above, out_w, *far)
+    )(*kept[1:3], part, below, above, out_w, *far)
 
     message0 = lax.ppermute(message, ("row", "col"), pairs)
     message1 = lax.ppermute(longer, ("row", "col"), others)
 
-    near0 = pl.pallas_call(
-        functools.partial(neighbour_kernel, reach),
-        out_shape=jax.ShapeDtypeStruct((slots, cols), BF16),
-        in_specs=vmem(4) + [ANY],
-        out_specs=vmem(1)[0],
-        scratch_shapes=[pltpu.VMEM((words, LANES), F32)],
-        compiler_params=params,
-        cost_estimate=pl.CostEstimate(flops=1, bytes_accessed=1, transcendentals=0),
-        name="partner",
-    )(kept[3], kept[4], raw0, message0, message)
+    def renewed(raw, words_of, after, name):
+        return pl.pallas_call(
+            functools.partial(neighbour_kernel, reach),
+            out_shape=jax.ShapeDtypeStruct((slots, cols), BF16),
+            in_specs=vmem(4) + [ANY],
+            out_specs=vmem(1)[0],
+            scratch_shapes=[pltpu.VMEM((words, LANES), F32)],
+            compiler_params=params,
+            cost_estimate=pl.CostEstimate(flops=1, bytes_accessed=1, transcendentals=0),
+            name=name,
+        )(kept[3], kept[4], raw, words_of, after)
+
+    updated = renewed(kept[0], message, message, "own")
+    near0 = renewed(raw0, message0, updated, "partner")
 
     tile = 512
     result = pl.pallas_call(

time: 20.8 us -> 20.7 us (level)
  waiting for transfers between devices: 2.85 us -> 2.45 us
  Pallas kernels: 8.05 us -> 8.27 us
    ppermute x1, waiting for transfers between devices: 0.91 us -> 0.51 us  [on_device(): message0 = lax.ppermute(message, ('row', 'col'), pairs)]
    pallas_call x1 -> x2, Pallas kernels: 0.4 us -> 0.79 us  [renewed(): pl.pallas_call(functools.partial(neighbour_kernel, reach), out_shape=jax....]
    pallas_call x1, Pallas kernels: 0.51 us -> 0.26 us  [on_device(): pl.pallas_call(functools.partial(update_kernel, reach, len(far)), out_sha...]
  transfers between devices with their start and end apart: 7 -> 7, of which waited for: 3 -> 3; matrix products, arithmetic and copies ran while one was open for 0% -> 0% of each run, Pallas kernels for 13% -> 14%
where the time goes in v14:
time: 20.7 us; the launch traced here: 20.5 us
  starting transfers between devices  9.67 us (47%)
  Pallas kernels  8.27 us (40%)
  waiting for transfers between devices  2.45 us (12%)
    ppermute x3, starting transfers between devices, around(): lax.ppermute(x, 'band', [(i, (i + shift) % count) for i in range(count)])  6.11 us
    pallas_call x1, Pallas kernels, on_device(): pl.pallas_call(functools.partial(denoise_kernel, tile, reach), out_shape=...  4.02 us
    pallas_call x1, Pallas kernels, on_device(): pl.pallas_call(weights_kernel, out_shape=(jax.ShapeDtypeStruct((16 * ch,...  1.79 us
    ppermute x1, waiting for transfers between devices, on_device(): message1 = lax.ppermute(longer, ('row', 'col'), others)  1.72 us
    pallas_call x1, Pallas kernels, on_device(): pl.pallas_call(functools.partial(project_kernel, reach), out_shape=(jax.S...  1.41 us
    ppermute x1, starting transfers between devices, on_device(): raw1 = lax.ppermute(kept[0], ('row', 'col'), others)  1.05 us
    ppermute x1, starting transfers between devices, on_device(): message0 = lax.ppermute(message, ('row', 'col'), pairs)  0.95 us
    ppermute x1, starting transfers between devices, on_device(): message1 = lax.ppermute(longer, ('row', 'col'), others)  0.91 us
  transfers between devices with their start and end apart: 7, of which 3 were waited for; matrix products, arithmetic and copies ran while one was open for 0% of the time, Pallas kernels for 14%

profile of v14, /device:TPU:0, one launch (start us, length us, event | category | flops | bytes accessed | tf_op | source)
XLA Modules:
  0.0 20.5 jit_solution(18390057892597725865)
XLA Ops:
  0.0 1.4 %project.1 = (bf16[80,128]{1,0:T(8,128)(2,1)S(1)}, bf16[224,128]{1,0:T(8,128)(2,1)S(1)}, bf16[224,128]{1,0:T(8,128)(2,1)S(1)}, bf16[24,4096]{1,0:T(8,128)(2,1)S(...) custom-call(bf16[22,4096]{1,0:T(8,128)(2,1)} %bitcast.7, ...), custom_call_target="tpu_custom_call" | custom-call | tf_op jit(solution)/shard_map/project/pallas_call | solution.py:515
  1.4 3.1 %collective-permute-start = (bf16[224,128]{1,0:T(8,128)(2,1)S(1)}, bf16[224,128]{1,0:T(8,128)(2,1)S(1)}, u32[]{:S(2)}, u32[]{:S(2)}) collective-permute-start(bf16[224,128]{1,0:T(8,128)(2,1)S(1)} %get-tuple-element.27), channel_id=1, source_target_pairs={{0,8},{8,16},{16,24},{24,0},{1,9},{9,17},{17,25},{25,1},{2,10},{10... | collective-permute-start | bytes 172040 | tf_op jit(solution)/shard_map/ppermute | solution.py:536
  4.5 2.1 %collective-permute-start.1 = (bf16[224,128]{1,0:T(8,128)(2,1)S(1)}, bf16[224,128]{1,0:T(8,128)(2,1)S(1)}, u32[]{:S(2)}, u32[]{:S(2)}) collective-permute-start(bf16[224,128]{1,0:T(8,128)(2,1)S(1)} %get-tuple-element.28), channel_id=1, source_target_pairs={{0,24},{8,0},{16,8},{24,16},{1,25},{9,1},{17,9},{25,17},{2,26},{10... | collective-permute-start | bytes 172040 | tf_op jit(solution)/shard_map/ppermute | solution.py:536
  6.6 0.9 %collective-permute-start.2 = (bf16[80,128]{1,0:T(8,128)(2,1)S(1)}, bf16[80,128]{1,0:T(8,128)(2,1)S(1)}, u32[]{:S(2)}, u32[]{:S(2)}) collective-permute-start(bf16[80,128]{1,0:T(8,128)(2,1)S(1)} %get-tuple-element.20._.own_ref), channel_id=1, source_target_pairs={{0,16},{8,24},{16,0},{24,8},{1,17},{9,25},{17,1},{25,9},{2,18},{10... | collective-permute-start | bytes 61448 | tf_op jit(solution)/shard_map/ppermute | solution.py:536
  7.5 1.0 %collective-permute-start.5 = (bf16[24,4096]{1,0:T(8,128)(2,1)S(1)}, bf16[24,4096]{1,0:T(8,128)(2,1)S(1)}, u32[]{:S(2)}, u32[]{:S(2)}) collective-permute-start(bf16[24,4096]{1,0:T(8,128)(2,1)S(1)} %get-tuple-element.21.raw_ref), channel_id=1, source_target_pairs={{0,7},{1,2},{2,1},{3,4},{4,3},{5,6},{6,5},{7,0},{8,15},{9,10},{10,... | collective-permute-start | bytes 589832 | tf_op jit(solution)/shard_map/ppermute | solution.py:555
  8.6 0.7 %collective-permute-start.3 = (bf16[24,4096]{1,0:T(8,128)(2,1)S(1)}, bf16[24,4096]{1,0:T(8,128)(2,1)S(1)}, u32[]{:S(2)}, u32[]{:S(2)}) collective-permute-start(bf16[24,4096]{1,0:T(8,128)(2,1)S(1)} %gate.1._), channel_id=1, source_target_pairs={{0,1},{1,0},{2,3},{3,2},{4,5},{5,4},{6,7},{7,6},{8,9},{9,8},{10,11... | collective-permute-start | bytes 589832 | tf_op jit(solution)/shard_map/ppermute | solution.py:556
  9.3 1.8 %weights.1 = (bf16[256,160]{1,0:T(8,128)(2,1)S(1)}, bf16[192,160]{1,0:T(8,128)(2,1)S(1)}, bf16[128,240]{1,0:T(8,128)(2,1)S(1)}, bf16[128,208]{1,0:T(8,128)(2,1)S(1)}, f32[128,128]{1,0:T(8,128)S(1)}) custom-call(bf16[24,4096]{1,0:T(8,128)(2,1)S(1)} %gate.1._, bf16[16,9]{1,0:T(8,128)(2,1)} %sw_in.1, f32[1,16]{1,0:T(1,128)} %bitcast.10, ...), custom_call_target="tpu_custom_call" | custom-call | tf_op jit(solution)/shard_map/weights/pallas_call | solution.py:567
  11.1 0.2 %collective-permute-done.2.rest_refs_0_ = bf16[80,128]{1,0:T(8,128)(2,1)S(1)} collective-permute-done((bf16[80,128]{1,0:T(8,128)(2,1)S(1)}, bf16[80,128]{1,0:T(8,128)(2,1)S(1)}, u32[]{:S(2)}, u32[]{:S(2)}) %collective-permute-start.2) | collective-permute-done | bytes 20512 | tf_op jit(solution)/shard_map/ppermute | solution.py:536
  11.3 0.0 collective-permute-done.below_ref
  11.3 0.0 collective-permute-done.1.above_ref
  11.3 0.3 %update.1 = (bf16[288,128]{1,0:T(8,128)(2,1)S(1)}, bf16[304,128]{1,0:T(8,128)(2,1)S(1)}) custom-call(s32[1,4096]{1,0:T(1,128)S(1)} %get-tuple-element.25.ap_ref, f32[1,4444]{1,0:T(1,128)S(1)} %get-tuple-element.26.meas_ref, bf16[80,128]{1,0:T(8,128)(2,1)S(1)} %get-tuple-element.20._.own_ref, bf16[224,128]{1,0:T(8,128)(2,1)S(1)} %collective-permute-done.below_ref, ...), custom_call_target="tpu_custom_call" | custom-call | flops 10000000000 | bytes 40000000 | tf_op jit(solution)/shard_map/update/pallas_call | solution.py:585
  11.5 0.9 %collective-permute-start.6 = (bf16[304,128]{1,0:T(8,128)(2,1)S(1)}, bf16[304,128]{1,0:T(8,128)(2,1)S(1)}, u32[]{:S(2)}, u32[]{:S(2)}) collective-permute-start(bf16[304,128]{1,0:T(8,128)(2,1)S(1)} %get-tuple-element.30), channel_id=1, source_target_pairs={{0,7},{1,2},{2,1},{3,4},{4,3},{5,6},{6,5},{7,0},{8,15},{9,10},{10,... | collective-permute-start | bytes 233480 | tf_op jit(solution)/shard_map/ppermute | solution.py:605
  12.5 0.9 %collective-permute-start.4 = (bf16[288,128]{1,0:T(8,128)(2,1)S(1)}, bf16[288,128]{1,0:T(8,128)(2,1)S(1)}, u32[]{:S(2)}, u32[]{:S(2)}) collective-permute-start(bf16[288,128]{1,0:T(8,128)(2,1)S(1)} %get-tuple-element.29.msg_ref._), channel_id=1, source_target_pairs={{0,1},{1,0},{2,3},{3,2},{4,5},{5,4},{6,7},{7,6},{8,9},{9,8},{10,11... | collective-permute-start | bytes 221192 | tf_op jit(solution)/shard_map/ppermute | solution.py:604
  13.4 0.4 %own.1._.mid_ref = bf16[32,4096]{1,0:T(8,128)(2,1)S(1)} custom-call(s32[1,22]{1,0:T(1,128)S(1)} %get-tuple-element.23.shear_ref, f32[1,22]{1,0:T(1,128)S(1)} %get-tuple-element.24.step_ref, bf16[24,4096]{1,0:T(8,128)(2,1)S(1)} %get-tuple-element.21.raw_ref, bf16[288,128]{1,0:T(8,128)(2,1)S(1)} %get-tuple-element.29.msg_ref._, ...), custom_call_target="tpu_custom_call" | custom-call | flops 1 | bytes 1 | tf_op jit(solution)/shard_map/own/pallas_call | solution.py:608
  13.8 0.5 %collective-permute-done.4.msg_ref = bf16[288,128]{1,0:T(8,128)(2,1)S(1)} collective-permute-done((bf16[288,128]{1,0:T(8,128)(2,1)S(1)}, bf16[288,128]{1,0:T(8,128)(2,1)S(1)}, u32[]{:S(2)}, u32[]{:S(2)}) %collective-permute-start.4) | collective-permute-done | bytes 73760 | tf_op jit(solution)/shard_map/ppermute | solution.py:604
  14.3 0.0 collective-permute-done.3.raw_ref
  14.3 0.4 %partner.1.near0 = bf16[32,4096]{1,0:T(8,128)(2,1)S(1)} custom-call(s32[1,22]{1,0:T(1,128)S(1)} %get-tuple-element.23.shear_ref, f32[1,22]{1,0:T(1,128)S(1)} %get-tuple-element.24.step_ref, bf16[24,4096]{1,0:T(8,128)(2,1)S(1)} %collective-permute-done.3.raw_ref, bf16[288,128]{1,0:T(8,128)(2,1)S(1)} %collective-permute-done.4.msg_ref, ...), custom_call_target="tpu_custom_call" | custom-call | flops 1 | bytes 1 | tf_op jit(solution)/shard_map/partner/pallas_call | solution.py:608
  14.7 1.7 %collective-permute-done.6.msg_ref = bf16[304,128]{1,0:T(8,128)(2,1)S(1)} collective-permute-done((bf16[304,128]{1,0:T(8,128)(2,1)S(1)}, bf16[304,128]{1,0:T(8,128)(2,1)S(1)}, u32[]{:S(2)}, u32[]{:S(2)}) %collective-permute-start.6) | collective-permute-done | bytes 77856 | tf_op jit(solution)/shard_map/ppermute | solution.py:605
  16.4 0.0 collective-permute-done.5.raw_ref
  16.4 4.0 %denoise.1 = bf16[22,4096]{1,0:T(8,128)(2,1)} custom-call(f32[128,128]{1,0:T(8,128)S(1)} %get-tuple-element.22._.ow_ref, bf16[32,4096]{1,0:T(8,128)(2,1)S(1)} %own.1._.mid_ref, s32[1,22]{1,0:T(1,128)S(1)} %get-tuple-element.23.shear_ref, f32[1,22]{1,0:T(1,128)S(1)} %get-tuple-element.24.step_ref, bf16[32,4096]{1,0:T(8,128)(2,1)S(1)} %partner.1.near0, ...), custom_call_target="tpu_custom_call" | custom-call | tf_op jit(solution)/shard_map/denoise/pallas_call | solution.py:623
  (2 shorter events, 0.0 us)
Async XLA Ops:
  1.4 9.9 %collective-permute-start = (bf16[224,128]{1,0:T(8,128)(2,1)S(1)}, bf16[224,128]{1,0:T(8,128)(2,1)S(1)}, u32[]{:S(2)}, u32[]{:S(2)}) collective-permute-start(bf16[224,128]{1,0:T(8,128)(2,1)S(1)} %get-tuple-element.27), channel_id=1, source_target_pairs={{0,8},{8,16},{16,24},{24,0},{1,9},{9,17},{17,25},{25,1},{2,10},{10... | collective-permute-start | bytes 172040 | tf_op jit(solution)/shard_map/ppermute | solution.py:536
  4.5 6.8 %collective-permute-start.1 = (bf16[224,128]{1,0:T(8,128)(2,1)S(1)}, bf16[224,128]{1,0:T(8,128)(2,1)S(1)}, u32[]{:S(2)}, u32[]{:S(2)}) collective-permute-start(bf16[224,128]{1,0:T(8,128)(2,1)S(1)} %get-tuple-element.28), channel_id=1, source_target_pairs={{0,24},{8,0},{16,8},{24,16},{1,25},{9,1},{17,9},{25,17},{2,26},{10... | collective-permute-start | bytes 172040 | tf_op jit(solution)/shard_map/ppermute | solution.py:536
  6.6 4.7 %collective-permute-start.2 = (bf16[80,128]{1,0:T(8,128)(2,1)S(1)}, bf16[80,128]{1,0:T(8,128)(2,1)S(1)}, u32[]{:S(2)}, u32[]{:S(2)}) collective-permute-start(bf16[80,128]{1,0:T(8,128)(2,1)S(1)} %get-tuple-element.20._.own_ref), channel_id=1, source_target_pairs={{0,16},{8,24},{16,0},{24,8},{1,17},{9,25},{17,1},{25,9},{2,18},{10... | collective-permute-start | bytes 61448 | tf_op jit(solution)/shard_map/ppermute | solution.py:536
  7.5 8.9 %collective-permute-start.5 = (bf16[24,4096]{1,0:T(8,128)(2,1)S(1)}, bf16[24,4096]{1,0:T(8,128)(2,1)S(1)}, u32[]{:S(2)}, u32[]{:S(2)}) collective-permute-start(bf16[24,4096]{1,0:T(8,128)(2,1)S(1)} %get-tuple-element.21.raw_ref), channel_id=1, source_target_pairs={{0,7},{1,2},{2,1},{3,4},{4,3},{5,6},{6,5},{7,0},{8,15},{9,10},{10,... | collective-permute-start | bytes 589832 | tf_op jit(solution)/shard_map/ppermute | solution.py:555
  8.6 5.7 %collective-permute-start.3 = (bf16[24,4096]{1,0:T(8,128)(2,1)S(1)}, bf16[24,4096]{1,0:T(8,128)(2,1)S(1)}, u32[]{:S(2)}, u32[]{:S(2)}) collective-permute-start(bf16[24,4096]{1,0:T(8,128)(2,1)S(1)} %gate.1._), channel_id=1, source_target_pairs={{0,1},{1,0},{2,3},{3,2},{4,5},{5,4},{6,7},{7,6},{8,9},{9,8},{10,11... | collective-permute-start | bytes 589832 | tf_op jit(solution)/shard_map/ppermute | solution.py:556
  11.5 4.9 %collective-permute-start.6 = (bf16[304,128]{1,0:T(8,128)(2,1)S(1)}, bf16[304,128]{1,0:T(8,128)(2,1)S(1)}, u32[]{:S(2)}, u32[]{:S(2)}) collective-permute-start(bf16[304,128]{1,0:T(8,128)(2,1)S(1)} %get-tuple-element.30), channel_id=1, source_target_pairs={{0,7},{1,2},{2,1},{3,4},{4,3},{5,6},{6,5},{7,0},{8,15},{9,10},{10,... | collective-permute-start | bytes 233480 | tf_op jit(solution)/shard_map/ppermute | solution.py:605
  12.5 1.9 %collective-permute-start.4 = (bf16[288,128]{1,0:T(8,128)(2,1)S(1)}, bf16[288,128]{1,0:T(8,128)(2,1)S(1)}, u32[]{:S(2)}, u32[]{:S(2)}) collective-permute-start(bf16[288,128]{1,0:T(8,128)(2,1)S(1)} %get-tuple-element.29.msg_ref._), channel_id=1, source_target_pairs={{0,1},{1,0},{2,3},{3,2},{4,5},{5,4},{6,7},{7,6},{8,9},{9,8},{10,11... | collective-permute-start | bytes 221192 | tf_op jit(solution)/shard_map/ppermute | solution.py:604

commit v15 on v14

--- a/solution.py
+++ b/solution.py
@@ -334,11 +334,35 @@
     return make
 
 
-def neighbour_kernel(reach, shear_ref, step_ref, raw_ref, msg_ref, _, near, words):
+def shifted(ref, start, end):
+    rows, cols = ref.shape
+    blank = jnp.zeros((rows, LANES), BF16)
+    left = ref[:, start - LANES : start] if start else blank
+    here = ref[:, start:end]
+    right = ref[:, end : end + LANES] if end < cols else blank
+    row = jnp.concatenate([left, here, right], axis=1)
+    width = end - start
+    back = pltpu.roll(row, 1, 1)[:, LANES : LANES + width]
+    ahead = pltpu.roll(row, row.shape[1] - 1, 1)[:, LANES : LANES + width]
+    return back, here, ahead
+
+
+def neighbour_kernel(tile, reach, shear_ref, step_ref, raw_ref, msg_ref, _, out_ref, near, words):
     bands = shear_ref.shape[1]
     make = neighbour_chunks(reach, bands, shear_ref, step_ref, raw_ref, msg_ref, near, words)
-    for q in range(near.shape[1] // LANES):
-        make(q)
+    cols = near.shape[1]
+    slots = near.shape[0] // 2
+    made = 0
+    for start in range(0, cols, tile):
+        while made < min((start + tile) // LANES + 1, cols // LANES):
+            make(made)
+            made += 1
+        three = shifted(near, start, start + tile)
+        for part in range(2):
+            rows = [x[part * slots : (part + 1) * slots] for x in three]
+            out_ref[part * 3 * slots : (part + 1) * 3 * slots, start : start + tile] = (
+                jnp.concatenate(rows, axis=0)
+            )
 
 
 def denoise_kernel(
@@ -365,10 +389,8 @@
     ch = main_ref.shape[0] // slots
     tiles = cols // tile
     inner = cols // LANES
-    wide = tile + 2 * LANES
     groups = -(-bands // SUB)
     ones = jnp.where(rows_of((slots, tile)) < 3, 1.0, 0.0).astype(BF16)
-    blank = jnp.zeros((2 * slots, LANES), BF16)
     neighbours = neighbour_chunks(
         reach, bands, shear_ref, step_ref, raw_ref, msg_ref, near1, words
     )
@@ -388,19 +410,12 @@
     def patches(t):
         start = t * tile
         end = start + tile
-        parts = []
-        for ref in (near0, mid_ref, near1):
-            left = ref[:, start - LANES : start] if t else blank
-            here = ref[:, start:end]
-            right = ref[:, end : end + LANES] if t < tiles - 1 else blank
-            row = jnp.concatenate([left, here, right], axis=1)
-            back = pltpu.roll(row, 1, 1)[:, LANES : LANES + tile]
-            ahead = pltpu.roll(row, wide - 1, 1)[:, LANES : LANES + tile]
-            parts += [back, here, ahead]
+        three = shifted(near1, start, end)
         for part in range(2):
-            inputs[t, part] = jnp.concatenate(
-                [p[part * slots : (part + 1) * slots] for p in parts] + [ones], axis=0
-            )
+            rows = slice(part * 3 * slots, (part + 1) * 3 * slots)
+            x = [near0[rows, start:end], mid_ref[rows, start:end]]
+            x += [p[part * slots : (part + 1) * slots] for p in three]
+            inputs[t, part] = jnp.concatenate(x + [ones], axis=0)
 
     def spatial(t, part):
         w_ref = halo_ref if part else main_ref
@@ -436,7 +451,11 @@
         if i == groups - 1:
             start = t * tile
             update = jnp.concatenate([sums.pop((t, n)) for n in range(groups)], axis=0)[0:bands]
-            center = mid_ref[:, start : start + tile].astype(F32)[0:bands]
+            center = [
+                mid_ref[at : at + slots, start : start + tile].astype(F32)
+                for at in (slots, 4 * slots)
+            ]
+            center = jnp.concatenate(center, axis=0)[0:bands]
             out_ref[:, start : start + tile] = (center + update).astype(BF16)
 
     update_up_to(0)
@@ -604,13 +623,15 @@
     message0 = lax.ppermute(message, ("row", "col"), pairs)
     message1 = lax.ppermute(longer, ("row", "col"), others)
 
+    tile = 512
+
     def renewed(raw, words_of, after, name):
         return pl.pallas_call(
-            functools.partial(neighbour_kernel, reach),
-            out_shape=jax.ShapeDtypeStruct((slots, cols), BF16),
+            functools.partial(neighbour_kernel, tile, reach),
+            out_shape=jax.ShapeDtypeStruct((3 * slots, cols), BF16),
             in_specs=vmem(4) + [ANY],
             out_specs=vmem(1)[0],
-            scratch_shapes=[pltpu.VMEM((words, LANES), F32)],
+            scratch_shapes=[pltpu.VMEM((slots, cols), BF16), pltpu.VMEM((words, LANES), F32)],
             compiler_params=params,
             cost_estimate=pl.CostEstimate(flops=1, bytes_accessed=1, transcendentals=0),
             name=name,
@@ -619,7 +640,6 @@
     updated = renewed(kept[0], message, message, "own")
     near0 = renewed(raw0, message0, updated, "partner")
 
-    tile = 512
     result = pl.pallas_call(
         functools.partial(denoise_kernel, tile, reach),
         out_shape=jax.ShapeDtypeStruct((bands, cols), BF16),

time: 20.7 us -> 20.6 us (level)
  waiting for transfers between devices: 2.45 us -> 1.63 us
  Pallas kernels: 8.27 us -> 9.08 us
    pallas_call x2, Pallas kernels: 0.79 us -> 1.61 us  [renewed(): pl.pallas_call(functools.partial(neighbour_kernel, tile, reach), out_shap...]
    ppermute x1, waiting for transfers between devices: 0.51 us -> 0.1 us  [on_device(): message0 = lax.ppermute(message, ('row', 'col'), pairs)]
    ppermute x1, waiting for transfers between devices: 1.72 us -> 1.31 us  [on_device(): message1 = lax.ppermute(longer, ('row', 'col'), others)]
  transfers between devices with their start and end apart: 7 -> 7, of which waited for: 3 -> 3; matrix products, arithmetic and copies ran while one was open for 0% -> 0% of each run, Pallas kernels for 14% -> 18%
where the time goes in v15:
time: 20.6 us; the launch traced here: 20.4 us
  starting transfers between devices  9.67 us (47%)
  Pallas kernels  9.08 us (44%)
  waiting for transfers between devices  1.63 us (8%)
    ppermute x3, starting transfers between devices, around(): lax.ppermute(x, 'band', [(i, (i + shift) % count) for i in range(count)])  6.11 us
    pallas_call x1, Pallas kernels, on_device(): pl.pallas_call(functools.partial(denoise_kernel, tile, reach), out_shape=...  4.01 us
    pallas_call x1, Pallas kernels, on_device(): pl.pallas_call(weights_kernel, out_shape=(jax.ShapeDtypeStruct((16 * ch,...  1.79 us
    pallas_call x2, Pallas kernels, renewed(): pl.pallas_call(functools.partial(neighbour_kernel, tile, reach), out_shap...  1.61 us
    pallas_call x1, Pallas kernels, on_device(): pl.pallas_call(functools.partial(project_kernel, reach), out_shape=(jax.S...  1.41 us
    ppermute x1, waiting for transfers between devices, on_device(): message1 = lax.ppermute(longer, ('row', 'col'), others)  1.31 us
    ppermute x1, starting transfers between devices, on_device(): raw1 = lax.ppermute(kept[0], ('row', 'col'), others)  1.05 us
    ppermute x1, starting transfers between devices, on_device(): message0 = lax.ppermute(message, ('row', 'col'), pairs)  0.95 us
  transfers between devices with their start and end apart: 7, of which 3 were waited for; matrix products, arithmetic and copies ran while one was open for 0% of the time, Pallas kernels for 18%

profile of v15, /device:TPU:0, one launch (start us, length us, event | category | flops | bytes accessed | tf_op | source)
XLA Modules:
  0.0 20.4 jit_solution(48149606674320718)
XLA Ops:
  0.0 1.4 %project.1 = (bf16[80,128]{1,0:T(8,128)(2,1)S(1)}, bf16[224,128]{1,0:T(8,128)(2,1)S(1)}, bf16[224,128]{1,0:T(8,128)(2,1)S(1)}, bf16[24,4096]{1,0:T(8,128)(2,1)S(...) custom-call(bf16[22,4096]{1,0:T(8,128)(2,1)} %bitcast.7, ...), custom_call_target="tpu_custom_call" | custom-call | tf_op jit(solution)/shard_map/project/pallas_call | solution.py:534
  1.4 3.1 %collective-permute-start = (bf16[224,128]{1,0:T(8,128)(2,1)S(1)}, bf16[224,128]{1,0:T(8,128)(2,1)S(1)}, u32[]{:S(2)}, u32[]{:S(2)}) collective-permute-start(bf16[224,128]{1,0:T(8,128)(2,1)S(1)} %get-tuple-element.27), channel_id=1, source_target_pairs={{0,8},{8,16},{16,24},{24,0},{1,9},{9,17},{17,25},{25,1},{2,10},{10... | collective-permute-start | bytes 172040 | tf_op jit(solution)/shard_map/ppermute | solution.py:555
  4.5 2.1 %collective-permute-start.1 = (bf16[224,128]{1,0:T(8,128)(2,1)S(1)}, bf16[224,128]{1,0:T(8,128)(2,1)S(1)}, u32[]{:S(2)}, u32[]{:S(2)}) collective-permute-start(bf16[224,128]{1,0:T(8,128)(2,1)S(1)} %get-tuple-element.28), channel_id=1, source_target_pairs={{0,24},{8,0},{16,8},{24,16},{1,25},{9,1},{17,9},{25,17},{2,26},{10... | collective-permute-start | bytes 172040 | tf_op jit(solution)/shard_map/ppermute | solution.py:555
  6.6 0.9 %collective-permute-start.2 = (bf16[80,128]{1,0:T(8,128)(2,1)S(1)}, bf16[80,128]{1,0:T(8,128)(2,1)S(1)}, u32[]{:S(2)}, u32[]{:S(2)}) collective-permute-start(bf16[80,128]{1,0:T(8,128)(2,1)S(1)} %get-tuple-element.20._.own_ref), channel_id=1, source_target_pairs={{0,16},{8,24},{16,0},{24,8},{1,17},{9,25},{17,1},{25,9},{2,18},{10... | collective-permute-start | bytes 61448 | tf_op jit(solution)/shard_map/ppermute | solution.py:555
  7.5 1.0 %collective-permute-start.5 = (bf16[24,4096]{1,0:T(8,128)(2,1)S(1)}, bf16[24,4096]{1,0:T(8,128)(2,1)S(1)}, u32[]{:S(2)}, u32[]{:S(2)}) collective-permute-start(bf16[24,4096]{1,0:T(8,128)(2,1)S(1)} %get-tuple-element.21.raw_ref), channel_id=1, source_target_pairs={{0,7},{1,2},{2,1},{3,4},{4,3},{5,6},{6,5},{7,0},{8,15},{9,10},{10,... | collective-permute-start | bytes 589832 | tf_op jit(solution)/shard_map/ppermute | solution.py:574
  8.6 0.7 %collective-permute-start.3 = (bf16[24,4096]{1,0:T(8,128)(2,1)S(1)}, bf16[24,4096]{1,0:T(8,128)(2,1)S(1)}, u32[]{:S(2)}, u32[]{:S(2)}) collective-permute-start(bf16[24,4096]{1,0:T(8,128)(2,1)S(1)} %gate.1._), channel_id=1, source_target_pairs={{0,1},{1,0},{2,3},{3,2},{4,5},{5,4},{6,7},{7,6},{8,9},{9,8},{10,11... | collective-permute-start | bytes 589832 | tf_op jit(solution)/shard_map/ppermute | solution.py:575
  9.3 1.8 %weights.1 = (bf16[256,160]{1,0:T(8,128)(2,1)S(1)}, bf16[192,160]{1,0:T(8,128)(2,1)S(1)}, bf16[128,240]{1,0:T(8,128)(2,1)S(1)}, bf16[128,208]{1,0:T(8,128)(2,1)S(1)}, f32[128,128]{1,0:T(8,128)S(1)}) custom-call(bf16[24,4096]{1,0:T(8,128)(2,1)S(1)} %gate.1._, bf16[16,9]{1,0:T(8,128)(2,1)} %sw_in.1, f32[1,16]{1,0:T(1,128)} %bitcast.10, ...), custom_call_target="tpu_custom_call" | custom-call | tf_op jit(solution)/shard_map/weights/pallas_call | solution.py:586
  11.1 0.2 %collective-permute-done.2.rest_refs_0_ = bf16[80,128]{1,0:T(8,128)(2,1)S(1)} collective-permute-done((bf16[80,128]{1,0:T(8,128)(2,1)S(1)}, bf16[80,128]{1,0:T(8,128)(2,1)S(1)}, u32[]{:S(2)}, u32[]{:S(2)}) %collective-permute-start.2) | collective-permute-done | bytes 20512 | tf_op jit(solution)/shard_map/ppermute | solution.py:555
  11.3 0.0 collective-permute-done.below_ref
  11.3 0.0 collective-permute-done.1.above_ref
  11.3 0.3 %update.1 = (bf16[288,128]{1,0:T(8,128)(2,1)S(1)}, bf16[304,128]{1,0:T(8,128)(2,1)S(1)}) custom-call(s32[1,4096]{1,0:T(1,128)S(1)} %get-tuple-element.25.ap_ref, f32[1,4444]{1,0:T(1,128)S(1)} %get-tuple-element.26.meas_ref, bf16[80,128]{1,0:T(8,128)(2,1)S(1)} %get-tuple-element.20._.own_ref, bf16[224,128]{1,0:T(8,128)(2,1)S(1)} %collective-permute-done.below_ref, ...), custom_call_target="tpu_custom_call" | custom-call | flops 10000000000 | bytes 40000000 | tf_op jit(solution)/shard_map/update/pallas_call | solution.py:604
  11.5 0.9 %collective-permute-start.6 = (bf16[304,128]{1,0:T(8,128)(2,1)S(1)}, bf16[304,128]{1,0:T(8,128)(2,1)S(1)}, u32[]{:S(2)}, u32[]{:S(2)}) collective-permute-start(bf16[304,128]{1,0:T(8,128)(2,1)S(1)} %get-tuple-element.30), channel_id=1, source_target_pairs={{0,7},{1,2},{2,1},{3,4},{4,3},{5,6},{6,5},{7,0},{8,15},{9,10},{10,... | collective-permute-start | bytes 233480 | tf_op jit(solution)/shard_map/ppermute | solution.py:624
  12.5 0.9 %collective-permute-start.4 = (bf16[288,128]{1,0:T(8,128)(2,1)S(1)}, bf16[288,128]{1,0:T(8,128)(2,1)S(1)}, u32[]{:S(2)}, u32[]{:S(2)}) collective-permute-start(bf16[288,128]{1,0:T(8,128)(2,1)S(1)} %get-tuple-element.29.msg_ref._), channel_id=1, source_target_pairs={{0,1},{1,0},{2,3},{3,2},{4,5},{5,4},{6,7},{7,6},{8,9},{9,8},{10,11... | collective-permute-start | bytes 221192 | tf_op jit(solution)/shard_map/ppermute | solution.py:623
  13.4 0.8 %own.1._.mid_ref = bf16[96,4096]{1,0:T(8,128)(2,1)S(1)} custom-call(s32[1,22]{1,0:T(1,128)S(1)} %get-tuple-element.23.shear_ref, f32[1,22]{1,0:T(1,128)S(1)} %get-tuple-element.24.step_ref, bf16[24,4096]{1,0:T(8,128)(2,1)S(1)} %get-tuple-element.21.raw_ref, bf16[288,128]{1,0:T(8,128)(2,1)S(1)} %get-tuple-element.29.msg_ref._, ...), custom_call_target="tpu_custom_call" | custom-call | flops 1 | bytes 1 | tf_op jit(solution)/shard_map/own/pallas_call | solution.py:629
  14.2 0.1 collective-permute-done.4.msg_ref
  14.3 0.0 collective-permute-done.3.raw_ref
  14.3 0.8 %partner.1.near0 = bf16[96,4096]{1,0:T(8,128)(2,1)S(1)} custom-call(s32[1,22]{1,0:T(1,128)S(1)} %get-tuple-element.23.shear_ref, f32[1,22]{1,0:T(1,128)S(1)} %get-tuple-element.24.step_ref, bf16[24,4096]{1,0:T(8,128)(2,1)S(1)} %collective-permute-done.3.raw_ref, bf16[288,128]{1,0:T(8,128)(2,1)S(1)} %collective-permute-done.4.msg_ref, ...), custom_call_target="tpu_custom_call" | custom-call | flops 1 | bytes 1 | tf_op jit(solution)/shard_map/partner/pallas_call | solution.py:629
  15.1 1.3 %collective-permute-done.6.msg_ref = bf16[304,128]{1,0:T(8,128)(2,1)S(1)} collective-permute-done((bf16[304,128]{1,0:T(8,128)(2,1)S(1)}, bf16[304,128]{1,0:T(8,128)(2,1)S(1)}, u32[]{:S(2)}, u32[]{:S(2)}) %collective-permute-start.6) | collective-permute-done | bytes 77856 | tf_op jit(solution)/shard_map/ppermute | solution.py:624
  16.4 0.0 collective-permute-done.5.raw_ref
  16.4 4.0 %denoise.1 = bf16[22,4096]{1,0:T(8,128)(2,1)} custom-call(f32[128,128]{1,0:T(8,128)S(1)} %get-tuple-element.22._.ow_ref, bf16[96,4096]{1,0:T(8,128)(2,1)S(1)} %own.1._.mid_ref, s32[1,22]{1,0:T(1,128)S(1)} %get-tuple-element.23.shear_ref, f32[1,22]{1,0:T(1,128)S(1)} %get-tuple-element.24.step_ref, bf16[96,4096]{1,0:T(8,128)(2,1)S(1)} %partner.1.near0, ...), custom_call_target="tpu_custom_call" | custom-call | tf_op jit(solution)/shard_map/denoise/pallas_call | solution.py:643
  (2 shorter events, 0.0 us)
Async XLA Ops:
  1.4 9.9 %collective-permute-start = (bf16[224,128]{1,0:T(8,128)(2,1)S(1)}, bf16[224,128]{1,0:T(8,128)(2,1)S(1)}, u32[]{:S(2)}, u32[]{:S(2)}) collective-permute-start(bf16[224,128]{1,0:T(8,128)(2,1)S(1)} %get-tuple-element.27), channel_id=1, source_target_pairs={{0,8},{8,16},{16,24},{24,0},{1,9},{9,17},{17,25},{25,1},{2,10},{10... | collective-permute-start | bytes 172040 | tf_op jit(solution)/shard_map/ppermute | solution.py:555
  4.5 6.8 %collective-permute-start.1 = (bf16[224,128]{1,0:T(8,128)(2,1)S(1)}, bf16[224,128]{1,0:T(8,128)(2,1)S(1)}, u32[]{:S(2)}, u32[]{:S(2)}) collective-permute-start(bf16[224,128]{1,0:T(8,128)(2,1)S(1)} %get-tuple-element.28), channel_id=1, source_target_pairs={{0,24},{8,0},{16,8},{24,16},{1,25},{9,1},{17,9},{25,17},{2,26},{10... | collective-permute-start | bytes 172040 | tf_op jit(solution)/shard_map/ppermute | solution.py:555
  6.6 4.7 %collective-permute-start.2 = (bf16[80,128]{1,0:T(8,128)(2,1)S(1)}, bf16[80,128]{1,0:T(8,128)(2,1)S(1)}, u32[]{:S(2)}, u32[]{:S(2)}) collective-permute-start(bf16[80,128]{1,0:T(8,128)(2,1)S(1)} %get-tuple-element.20._.own_ref), channel_id=1, source_target_pairs={{0,16},{8,24},{16,0},{24,8},{1,17},{9,25},{17,1},{25,9},{2,18},{10... | collective-permute-start | bytes 61448 | tf_op jit(solution)/shard_map/ppermute | solution.py:555
  7.5 8.9 %collective-permute-start.5 = (bf16[24,4096]{1,0:T(8,128)(2,1)S(1)}, bf16[24,4096]{1,0:T(8,128)(2,1)S(1)}, u32[]{:S(2)}, u32[]{:S(2)}) collective-permute-start(bf16[24,4096]{1,0:T(8,128)(2,1)S(1)} %get-tuple-element.21.raw_ref), channel_id=1, source_target_pairs={{0,7},{1,2},{2,1},{3,4},{4,3},{5,6},{6,5},{7,0},{8,15},{9,10},{10,... | collective-permute-start | bytes 589832 | tf_op jit(solution)/shard_map/ppermute | solution.py:574
  8.6 5.7 %collective-permute-start.3 = (bf16[24,4096]{1,0:T(8,128)(2,1)S(1)}, bf16[24,4096]{1,0:T(8,128)(2,1)S(1)}, u32[]{:S(2)}, u32[]{:S(2)}) collective-permute-start(bf16[24,4096]{1,0:T(8,128)(2,1)S(1)} %gate.1._), channel_id=1, source_target_pairs={{0,1},{1,0},{2,3},{3,2},{4,5},{5,4},{6,7},{7,6},{8,9},{9,8},{10,11... | collective-permute-start | bytes 589832 | tf_op jit(solution)/shard_map/ppermute | solution.py:575
  11.5 4.9 %collective-permute-start.6 = (bf16[304,128]{1,0:T(8,128)(2,1)S(1)}, bf16[304,128]{1,0:T(8,128)(2,1)S(1)}, u32[]{:S(2)}, u32[]{:S(2)}) collective-permute-start(bf16[304,128]{1,0:T(8,128)(2,1)S(1)} %get-tuple-element.30), channel_id=1, source_target_pairs={{0,7},{1,2},{2,1},{3,4},{4,3},{5,6},{6,5},{7,0},{8,15},{9,10},{10,... | collective-permute-start | bytes 233480 | tf_op jit(solution)/shard_map/ppermute | solution.py:624
  12.5 1.9 %collective-permute-start.4 = (bf16[288,128]{1,0:T(8,128)(2,1)S(1)}, bf16[288,128]{1,0:T(8,128)(2,1)S(1)}, u32[]{:S(2)}, u32[]{:S(2)}) collective-permute-start(bf16[288,128]{1,0:T(8,128)(2,1)S(1)} %get-tuple-element.29.msg_ref._), channel_id=1, source_target_pairs={{0,1},{1,0},{2,3},{3,2},{4,5},{5,4},{6,7},{7,6},{8,9},{9,8},{10,11... | collective-permute-start | bytes 221192 | tf_op jit(solution)/shard_map/ppermute | solution.py:623

commit v16 on v15

--- a/solution.py
+++ b/solution.py
@@ -623,7 +623,7 @@
     message0 = lax.ppermute(message, ("row", "col"), pairs)
     message1 = lax.ppermute(longer, ("row", "col"), others)
 
-    tile = 512
+    tile = 1024
 
     def renewed(raw, words_of, after, name):
         return pl.pallas_call(

time: 20.6 us -> 21 us (1.019)
  Pallas kernels: 9.08 us -> 9.33 us
    pallas_call x1, Pallas kernels: 4.01 us -> 4.4 us  [on_device(): pl.pallas_call(functools.partial(denoise_kernel, tile, reach), out_shape=...]
  transfers between devices with their start and end apart: 7 -> 7, of which waited for: 3 -> 3; matrix products, arithmetic and copies ran while one was open for 0% -> 0% of each run, Pallas kernels for 18% -> 17%
where the time goes in v16:
time: 21 us; the launch traced here: 20.8 us
  starting transfers between devices  9.67 us (46%)
  Pallas kernels  9.33 us (44%)
  waiting for transfers between devices  1.76 us (8%)
    ppermute x3, starting transfers between devices, around(): lax.ppermute(x, 'band', [(i, (i + shift) % count) for i in range(count)])  6.11 us
    pallas_call x1, Pallas kernels, on_device(): pl.pallas_call(functools.partial(denoise_kernel, tile, reach), out_shape=...  4.4 us
    pallas_call x1, Pallas kernels, on_device(): pl.pallas_call(weights_kernel, out_shape=(jax.ShapeDtypeStruct((16 * ch,...  1.79 us
    pallas_call x2, Pallas kernels, renewed(): pl.pallas_call(functools.partial(neighbour_kernel, tile, reach), out_shap...  1.47 us
    pallas_call x1, Pallas kernels, on_device(): pl.pallas_call(functools.partial(project_kernel, reach), out_shape=(jax.S...  1.41 us
    ppermute x1, waiting for transfers between devices, on_device(): message1 = lax.ppermute(longer, ('row', 'col'), others)  1.37 us
    ppermute x1, starting transfers between devices, on_device(): raw1 = lax.ppermute(kept[0], ('row', 'col'), others)  1.05 us
    ppermute x1, starting transfers between devices, on_device(): message0 = lax.ppermute(message, ('row', 'col'), pairs)  0.95 us
  transfers between devices with their start and end apart: 7, of which 3 were waited for; matrix products, arithmetic and copies ran while one was open for 0% of the time, Pallas kernels for 17%

profile of v16, /device:TPU:0, one launch (start us, length us, event | category | flops | bytes accessed | tf_op | source)
XLA Modules:
  0.0 20.8 jit_solution(2403859745082461210)
XLA Ops:
  0.0 1.4 %project.1 = (bf16[80,128]{1,0:T(8,128)(2,1)S(1)}, bf16[224,128]{1,0:T(8,128)(2,1)S(1)}, bf16[224,128]{1,0:T(8,128)(2,1)S(1)}, bf16[24,4096]{1,0:T(8,128)(2,1)S(...) custom-call(bf16[22,4096]{1,0:T(8,128)(2,1)} %bitcast.7, ...), custom_call_target="tpu_custom_call" | custom-call | tf_op jit(solution)/shard_map/project/pallas_call | solution.py:534
  1.4 3.1 %collective-permute-start = (bf16[224,128]{1,0:T(8,128)(2,1)S(1)}, bf16[224,128]{1,0:T(8,128)(2,1)S(1)}, u32[]{:S(2)}, u32[]{:S(2)}) collective-permute-start(bf16[224,128]{1,0:T(8,128)(2,1)S(1)} %get-tuple-element.27), channel_id=1, source_target_pairs={{0,8},{8,16},{16,24},{24,0},{1,9},{9,17},{17,25},{25,1},{2,10},{10... | collective-permute-start | bytes 172040 | tf_op jit(solution)/shard_map/ppermute | solution.py:555
  4.5 2.1 %collective-permute-start.1 = (bf16[224,128]{1,0:T(8,128)(2,1)S(1)}, bf16[224,128]{1,0:T(8,128)(2,1)S(1)}, u32[]{:S(2)}, u32[]{:S(2)}) collective-permute-start(bf16[224,128]{1,0:T(8,128)(2,1)S(1)} %get-tuple-element.28), channel_id=1, source_target_pairs={{0,24},{8,0},{16,8},{24,16},{1,25},{9,1},{17,9},{25,17},{2,26},{10... | collective-permute-start | bytes 172040 | tf_op jit(solution)/shard_map/ppermute | solution.py:555
  6.6 0.9 %collective-permute-start.2 = (bf16[80,128]{1,0:T(8,128)(2,1)S(1)}, bf16[80,128]{1,0:T(8,128)(2,1)S(1)}, u32[]{:S(2)}, u32[]{:S(2)}) collective-permute-start(bf16[80,128]{1,0:T(8,128)(2,1)S(1)} %get-tuple-element.20._.own_ref), channel_id=1, source_target_pairs={{0,16},{8,24},{16,0},{24,8},{1,17},{9,25},{17,1},{25,9},{2,18},{10... | collective-permute-start | bytes 61448 | tf_op jit(solution)/shard_map/ppermute | solution.py:555
  7.5 1.0 %collective-permute-start.5 = (bf16[24,4096]{1,0:T(8,128)(2,1)S(1)}, bf16[24,4096]{1,0:T(8,128)(2,1)S(1)}, u32[]{:S(2)}, u32[]{:S(2)}) collective-permute-start(bf16[24,4096]{1,0:T(8,128)(2,1)S(1)} %get-tuple-element.21.raw_ref), channel_id=1, source_target_pairs={{0,7},{1,2},{2,1},{3,4},{4,3},{5,6},{6,5},{7,0},{8,15},{9,10},{10,... | collective-permute-start | bytes 589832 | tf_op jit(solution)/shard_map/ppermute | solution.py:574
  8.6 0.7 %collective-permute-start.3 = (bf16[24,4096]{1,0:T(8,128)(2,1)S(1)}, bf16[24,4096]{1,0:T(8,128)(2,1)S(1)}, u32[]{:S(2)}, u32[]{:S(2)}) collective-permute-start(bf16[24,4096]{1,0:T(8,128)(2,1)S(1)} %gate.1._), channel_id=1, source_target_pairs={{0,1},{1,0},{2,3},{3,2},{4,5},{5,4},{6,7},{7,6},{8,9},{9,8},{10,11... | collective-permute-start | bytes 589832 | tf_op jit(solution)/shard_map/ppermute | solution.py:575
  9.3 1.8 %weights.1 = (bf16[256,160]{1,0:T(8,128)(2,1)S(1)}, bf16[192,160]{1,0:T(8,128)(2,1)S(1)}, bf16[128,240]{1,0:T(8,128)(2,1)S(1)}, bf16[128,208]{1,0:T(8,128)(2,1)S(1)}, f32[128,128]{1,0:T(8,128)S(1)}) custom-call(bf16[24,4096]{1,0:T(8,128)(2,1)S(1)} %gate.1._, bf16[16,9]{1,0:T(8,128)(2,1)} %sw_in.1, f32[1,16]{1,0:T(1,128)} %bitcast.10, ...), custom_call_target="tpu_custom_call" | custom-call | tf_op jit(solution)/shard_map/weights/pallas_call | solution.py:586
  11.1 0.2 %collective-permute-done.2.rest_refs_0_ = bf16[80,128]{1,0:T(8,128)(2,1)S(1)} collective-permute-done((bf16[80,128]{1,0:T(8,128)(2,1)S(1)}, bf16[80,128]{1,0:T(8,128)(2,1)S(1)}, u32[]{:S(2)}, u32[]{:S(2)}) %collective-permute-start.2) | collective-permute-done | bytes 20512 | tf_op jit(solution)/shard_map/ppermute | solution.py:555
  11.3 0.0 collective-permute-done.below_ref
  11.3 0.0 collective-permute-done.1.above_ref
  11.3 0.3 %update.1 = (bf16[288,128]{1,0:T(8,128)(2,1)S(1)}, bf16[304,128]{1,0:T(8,128)(2,1)S(1)}) custom-call(s32[1,4096]{1,0:T(1,128)S(1)} %get-tuple-element.25.ap_ref, f32[1,4444]{1,0:T(1,128)S(1)} %get-tuple-element.26.meas_ref, bf16[80,128]{1,0:T(8,128)(2,1)S(1)} %get-tuple-element.20._.own_ref, bf16[224,128]{1,0:T(8,128)(2,1)S(1)} %collective-permute-done.below_ref, ...), custom_call_target="tpu_custom_call" | custom-call | flops 10000000000 | bytes 40000000 | tf_op jit(solution)/shard_map/update/pallas_call | solution.py:604
  11.5 0.9 %collective-permute-start.6 = (bf16[304,128]{1,0:T(8,128)(2,1)S(1)}, bf16[304,128]{1,0:T(8,128)(2,1)S(1)}, u32[]{:S(2)}, u32[]{:S(2)}) collective-permute-start(bf16[304,128]{1,0:T(8,128)(2,1)S(1)} %get-tuple-element.30), channel_id=1, source_target_pairs={{0,7},{1,2},{2,1},{3,4},{4,3},{5,6},{6,5},{7,0},{8,15},{9,10},{10,... | collective-permute-start | bytes 233480 | tf_op jit(solution)/shard_map/ppermute | solution.py:624
  12.5 0.9 %collective-permute-start.4 = (bf16[288,128]{1,0:T(8,128)(2,1)S(1)}, bf16[288,128]{1,0:T(8,128)(2,1)S(1)}, u32[]{:S(2)}, u32[]{:S(2)}) collective-permute-start(bf16[288,128]{1,0:T(8,128)(2,1)S(1)} %get-tuple-element.29.msg_ref._), channel_id=1, source_target_pairs={{0,1},{1,0},{2,3},{3,2},{4,5},{5,4},{6,7},{7,6},{8,9},{9,8},{10,11... | collective-permute-start | bytes 221192 | tf_op jit(solution)/shard_map/ppermute | solution.py:623
  13.4 0.7 %own.1._.mid_ref = bf16[96,4096]{1,0:T(8,128)(2,1)S(1)} custom-call(s32[1,22]{1,0:T(1,128)S(1)} %get-tuple-element.23.shear_ref, f32[1,22]{1,0:T(1,128)S(1)} %get-tuple-element.24.step_ref, bf16[24,4096]{1,0:T(8,128)(2,1)S(1)} %get-tuple-element.21.raw_ref, bf16[288,128]{1,0:T(8,128)(2,1)S(1)} %get-tuple-element.29.msg_ref._, ...), custom_call_target="tpu_custom_call" | custom-call | flops 1 | bytes 1 | tf_op jit(solution)/shard_map/own/pallas_call | solution.py:629
  14.1 0.2 collective-permute-done.4.msg_ref
  14.3 0.0 collective-permute-done.3.raw_ref
  14.3 0.7 %partner.1.near0 = bf16[96,4096]{1,0:T(8,128)(2,1)S(1)} custom-call(s32[1,22]{1,0:T(1,128)S(1)} %get-tuple-element.23.shear_ref, f32[1,22]{1,0:T(1,128)S(1)} %get-tuple-element.24.step_ref, bf16[24,4096]{1,0:T(8,128)(2,1)S(1)} %collective-permute-done.3.raw_ref, bf16[288,128]{1,0:T(8,128)(2,1)S(1)} %collective-permute-done.4.msg_ref, ...), custom_call_target="tpu_custom_call" | custom-call | flops 1 | bytes 1 | tf_op jit(solution)/shard_map/partner/pallas_call | solution.py:629
  15.1 1.4 %collective-permute-done.6.msg_ref = bf16[304,128]{1,0:T(8,128)(2,1)S(1)} collective-permute-done((bf16[304,128]{1,0:T(8,128)(2,1)S(1)}, bf16[304,128]{1,0:T(8,128)(2,1)S(1)}, u32[]{:S(2)}, u32[]{:S(2)}) %collective-permute-start.6) | collective-permute-done | bytes 77856 | tf_op jit(solution)/shard_map/ppermute | solution.py:624
  16.4 0.0 collective-permute-done.5.raw_ref
  16.4 4.4 %denoise.1 = bf16[22,4096]{1,0:T(8,128)(2,1)} custom-call(f32[128,128]{1,0:T(8,128)S(1)} %get-tuple-element.22._.ow_ref, bf16[96,4096]{1,0:T(8,128)(2,1)S(1)} %own.1._.mid_ref, s32[1,22]{1,0:T(1,128)S(1)} %get-tuple-element.23.shear_ref, f32[1,22]{1,0:T(1,128)S(1)} %get-tuple-element.24.step_ref, bf16[96,4096]{1,0:T(8,128)(2,1)S(1)} %partner.1.near0, ...), custom_call_target="tpu_custom_call" | custom-call | tf_op jit(solution)/shard_map/denoise/pallas_call | solution.py:643
  (2 shorter events, 0.0 us)
Async XLA Ops:
  1.4 9.9 %collective-permute-start = (bf16[224,128]{1,0:T(8,128)(2,1)S(1)}, bf16[224,128]{1,0:T(8,128)(2,1)S(1)}, u32[]{:S(2)}, u32[]{:S(2)}) collective-permute-start(bf16[224,128]{1,0:T(8,128)(2,1)S(1)} %get-tuple-element.27), channel_id=1, source_target_pairs={{0,8},{8,16},{16,24},{24,0},{1,9},{9,17},{17,25},{25,1},{2,10},{10... | collective-permute-start | bytes 172040 | tf_op jit(solution)/shard_map/ppermute | solution.py:555
  4.5 6.8 %collective-permute-start.1 = (bf16[224,128]{1,0:T(8,128)(2,1)S(1)}, bf16[224,128]{1,0:T(8,128)(2,1)S(1)}, u32[]{:S(2)}, u32[]{:S(2)}) collective-permute-start(bf16[224,128]{1,0:T(8,128)(2,1)S(1)} %get-tuple-element.28), channel_id=1, source_target_pairs={{0,24},{8,0},{16,8},{24,16},{1,25},{9,1},{17,9},{25,17},{2,26},{10... | collective-permute-start | bytes 172040 | tf_op jit(solution)/shard_map/ppermute | solution.py:555
  6.6 4.7 %collective-permute-start.2 = (bf16[80,128]{1,0:T(8,128)(2,1)S(1)}, bf16[80,128]{1,0:T(8,128)(2,1)S(1)}, u32[]{:S(2)}, u32[]{:S(2)}) collective-permute-start(bf16[80,128]{1,0:T(8,128)(2,1)S(1)} %get-tuple-element.20._.own_ref), channel_id=1, source_target_pairs={{0,16},{8,24},{16,0},{24,8},{1,17},{9,25},{17,1},{25,9},{2,18},{10... | collective-permute-start | bytes 61448 | tf_op jit(solution)/shard_map/ppermute | solution.py:555
  7.5 8.9 %collective-permute-start.5 = (bf16[24,4096]{1,0:T(8,128)(2,1)S(1)}, bf16[24,4096]{1,0:T(8,128)(2,1)S(1)}, u32[]{:S(2)}, u32[]{:S(2)}) collective-permute-start(bf16[24,4096]{1,0:T(8,128)(2,1)S(1)} %get-tuple-element.21.raw_ref), channel_id=1, source_target_pairs={{0,7},{1,2},{2,1},{3,4},{4,3},{5,6},{6,5},{7,0},{8,15},{9,10},{10,... | collective-permute-start | bytes 589832 | tf_op jit(solution)/shard_map/ppermute | solution.py:574
  8.6 5.7 %collective-permute-start.3 = (bf16[24,4096]{1,0:T(8,128)(2,1)S(1)}, bf16[24,4096]{1,0:T(8,128)(2,1)S(1)}, u32[]{:S(2)}, u32[]{:S(2)}) collective-permute-start(bf16[24,4096]{1,0:T(8,128)(2,1)S(1)} %gate.1._), channel_id=1, source_target_pairs={{0,1},{1,0},{2,3},{3,2},{4,5},{5,4},{6,7},{7,6},{8,9},{9,8},{10,11... | collective-permute-start | bytes 589832 | tf_op jit(solution)/shard_map/ppermute | solution.py:575
  11.5 4.9 %collective-permute-start.6 = (bf16[304,128]{1,0:T(8,128)(2,1)S(1)}, bf16[304,128]{1,0:T(8,128)(2,1)S(1)}, u32[]{:S(2)}, u32[]{:S(2)}) collective-permute-start(bf16[304,128]{1,0:T(8,128)(2,1)S(1)} %get-tuple-element.30), channel_id=1, source_target_pairs={{0,7},{1,2},{2,1},{3,4},{4,3},{5,6},{6,5},{7,0},{8,15},{9,10},{10,... | collective-permute-start | bytes 233480 | tf_op jit(solution)/shard_map/ppermute | solution.py:624
  12.5 1.9 %collective-permute-start.4 = (bf16[288,128]{1,0:T(8,128)(2,1)S(1)}, bf16[288,128]{1,0:T(8,128)(2,1)S(1)}, u32[]{:S(2)}, u32[]{:S(2)}) collective-permute-start(bf16[288,128]{1,0:T(8,128)(2,1)S(1)} %get-tuple-element.29.msg_ref._), channel_id=1, source_target_pairs={{0,1},{1,0},{2,3},{3,2},{4,5},{5,4},{6,7},{7,6},{8,9},{9,8},{10,11... | collective-permute-start | bytes 221192 | tf_op jit(solution)/shard_map/ppermute | solution.py:623
